TPU v7x, 32 devices: a whole 2x2x4 slice. The times are simulated.
32 devices in a mesh: group: 1, expert: 32 (over z, y, x, core).
Axes of the slice: x: 2, y: 2, z: 4, core: 2. Of those that a mesh axis runs over, the one named last changes fastest.
Arguments:
- hidden_in: bfloat16 [256, 7168], P(('group', 'expert')), may hold values from -1.75 to 1.75
- q_latent: bfloat16 [256, 128, 512], P(('group', 'expert')), may hold values from -4 to 4
- q_rope: bfloat16 [256, 8192], P(('group', 'expert')), may hold values from -125 to 125
- cache_latent: bfloat16 [256, 256, 512], P(('group', 'expert')), may hold values from -6 to 6
- cache_rope: bfloat16 [256, 64, 256], P(('group', 'expert')), may hold values from -4 to 4
- lengths: int32 [256], P(('group', 'expert')), may hold values from 2 to 256, as said below
- value_up_weight: bfloat16 [128, 512, 128], P('expert'), may hold values from -0.25 to 0.25
- out_weight: bfloat16 [16384, 7168], P('expert'), may hold values from -0.046875 to 0.046875
- norm_gain: bfloat16 [7168], replicated, may hold values from 0.099609375 to 1.8984375
- route_ids: int32 [256, 4], P(('group', 'expert')), may hold values from 0 to 3, all different within a row; in each aligned block of 8 rows (0 to 7, 8 to 15, ...) at most 8 rows name the same one
- route_logits: float32 [256, 4], P(('group', 'expert')), may hold values from -12 to 12
- gate_weight: bfloat16 [32, 7168, 128], P('expert'), may hold values from -0.0625 to 0.0625
- up_weight: bfloat16 [32, 7168, 128], P('expert'), may hold values from -0.0625 to 0.0625
- down_projection_weight: bfloat16 [32, 128, 7168], P('expert'), may hold values from -0.1875 to 0.1875
Outputs:
- layer_out: bfloat16 [256, 7168], P(('group', 'expert'))
Inputs may be any that keep to these rules, and one draw needn't show every extreme that they name: `route_ids`: each row names 4 different experts; among the 8 tokens of one device no expert is named more than 8 times, a bound that some block reaches. `lengths`: some token has exactly 256 valid rows.
All inputs are finite; a program needn't handle non-finite values.
Results may differ from a plain program's by a relative error of at most 0.014.
Values may be sent and summed in bfloat16 or wider, within the bound.
No kernel may reach another device: no remote copies, remote signals or barrier semaphores. Data moves between devices by JAX's collectives and lax.ppermute only.
A program may use at most 256 MiB of HBM per device.

v0:
```python
import jax
import jax.numpy as jnp
from jax import lax
from jax.sharding import PartitionSpec as P

SHARDS = 8


score_scale = 192.0 ** (-0.5)
epsilon = 1e-06
route_scale = 2.5


def slot_table(routes, experts, capacity):
    flattened = routes.reshape(-1)
    onehot = (flattened[:, None] == jnp.arange(experts, dtype=jnp.int32)[None, :]).astype(jnp.int32)
    before = jnp.cumsum(onehot, axis=0) - onehot
    ranking = jnp.sum(before * onehot, axis=1)
    return (flattened * capacity + ranking).reshape(routes.shape)


def shards(
    hidden_in,
    q_latent,
    q_rope,
    cache_latent,
    cache_rope,
    lengths,
    value_up_weight,
    out_weight,
    norm_gain,
    route_ids,
    route_logits,
    gate_weight,
    up_weight,
    down_projection_weight,
):
    devices = lax.axis_size("expert")
    tokens_here = hidden_in.shape[0]
    model_width = hidden_in.shape[1]
    heads_all = q_latent.shape[1]
    rope_width = cache_rope.shape[1]
    cache_rows = cache_latent.shape[1]
    top_count = route_ids.shape[1]
    experts = devices // SHARDS
    capacity = min(tokens_here, max(2, (tokens_here * top_count + experts - 1) // experts + 1))
    slot_count = experts * capacity
    scores = jnp.einsum("thk,tlk->thl", q_latent, cache_latent, preferred_element_type=jnp.float32)
    scores = scores + jnp.einsum(
        "thr,trl->thl",
        q_rope.reshape(tokens_here, heads_all, rope_width),
        cache_rope,
        preferred_element_type=jnp.float32,
    )
    scores = scores * score_scale
    usable = jnp.arange(cache_rows, dtype=jnp.int32)[None, :] < lengths[:, None]
    scores = jnp.where(usable[:, None, :], scores, -jnp.inf)
    highest = jnp.max(scores, axis=2, keepdims=True)
    expd = jnp.exp(scores - highest)
    attention_probabilities = (expd / jnp.sum(expd, axis=2, keepdims=True)).astype(jnp.bfloat16)
    latent_context_output = jnp.einsum(
        "thl,tlk->thk", attention_probabilities, cache_latent, preferred_element_type=jnp.float32
    ).astype(jnp.bfloat16)
    head_first_layout = lax.all_to_all(
        latent_context_output, "expert", split_axis=1, concat_axis=0, tiled=True
    )
    slot_ids = slot_table(route_ids, experts, capacity)
    slot_range = jnp.arange(slot_count, dtype=jnp.int32)
    per_head_value_rows = jnp.einsum(
        "aqg,qge->aqe", head_first_layout, value_up_weight, preferred_element_type=jnp.float32
    ).astype(jnp.bfloat16)
    attn = lax.psum_scatter(
        jnp.dot(
            per_head_value_rows.reshape(lax.axis_size("expert") * tokens_here, -1),
            out_weight,
            preferred_element_type=jnp.float32,
        ),
        "expert",
        scatter_dimension=0,
        tiled=True,
    )
    residual = (hidden_in.astype(jnp.float32) + attn).astype(jnp.bfloat16)
    res32 = residual.astype(jnp.float32)
    normed = (
        res32
        * lax.rsqrt(jnp.mean(res32 * res32, axis=1, keepdims=True) + epsilon)
        * norm_gain.astype(jnp.float32)
    ).astype(jnp.bfloat16)
    placement = jnp.sum(
        (slot_ids[:, :, None] == slot_range[None, None, :]).astype(jnp.int32), axis=1
    ).astype(jnp.bfloat16)
    outgoing = jnp.einsum(
        "tq,tw->qw", placement, normed, preferred_element_type=jnp.float32
    ).astype(jnp.bfloat16)
    outgoing = jnp.broadcast_to(
        outgoing.reshape(experts, 1, capacity, model_width),
        (experts, SHARDS, capacity, model_width),
    )
    outgoing = outgoing.reshape(devices, capacity, model_width)
    received = lax.all_to_all(outgoing, "expert", split_axis=0, concat_axis=0, tiled=True)
    sources, item_count, feature_count = received.shape
    flattened = received.reshape(sources * item_count, feature_count)
    gate_act = jnp.dot(flattened, gate_weight[0], preferred_element_type=jnp.float32)
    up_act = jnp.dot(flattened, up_weight[0], preferred_element_type=jnp.float32)
    hidden = (jax.nn.silu(gate_act) * up_act).astype(jnp.bfloat16)
    piece_out = jnp.dot(
        hidden, down_projection_weight[0], preferred_element_type=jnp.float32
    ).astype(jnp.bfloat16)
    returned_rows = lax.all_to_all(
        piece_out.reshape(sources, item_count, feature_count),
        "expert",
        split_axis=0,
        concat_axis=0,
        tiled=True,
    )
    sigm = jax.nn.sigmoid(route_logits)
    route_weights = route_scale * sigm / jnp.sum(sigm, axis=1, keepdims=True)
    combiner = jnp.sum(
        route_weights[:, :, None]
        * (slot_ids[:, :, None] == slot_range[None, None, :]).astype(jnp.float32),
        axis=1,
    )
    summed = jnp.sum(
        returned_rows.reshape(experts, SHARDS, capacity, model_width).astype(jnp.float32), axis=1
    ).reshape(slot_count, model_width)
    expert_sum = jnp.dot(combiner, summed, precision=lax.Precision.HIGHEST)
    return (residual.astype(jnp.float32) + expert_sum).astype(jnp.bfloat16)


def solution(mesh):
    placed = (
        P(("group", "expert"), None),
        P(("group", "expert"), None, None),
        P(("group", "expert"), None),
        P(("group", "expert"), None, None),
        P(("group", "expert"), None, None),
        P(("group", "expert")),
        P("expert", None, None),
        P("expert", None),
        P(),
        P(("group", "expert"), None),
        P(("group", "expert"), None),
        P("expert", None, None),
        P("expert", None, None),
        P("expert", None, None),
    )
    return jax.shard_map(
        shards, mesh=mesh, in_specs=placed, out_specs=P(("group", "expert"), None), check_vma=False
    )
```

profile of v0, /device:TPU:0, one launch (start us, length us, event | category | flops | bytes accessed | tf_op | source)
XLA Modules:
  0.0 399.1 jit_solution(4686713320334175104)
XLA Ops:
  6.5 1.3 reshape.61
  7.9 0.7 iota_compare_fusion.2
  8.6 1.2 fusion.51
  9.8 2.1 fusion.14
  11.9 0.4 fusion.50
  12.3 2.9 convolution_convert_fusion.2
  15.2 1.9 copy.35
  17.0 33.3 %all_to_all.28 = bf16[8,128,512]{2,0,1:T(8,128)(2,1)S(1)} all-to-all(bf16[8,128,512]{2,0,1:T(8,128)(2,1)S(1)} %copy.35), channel_id=1, replica_groups=mesh['group'=1,'expert'=32] {'expert'}, dimensions={1} | all-to-all | bytes 2097152 | tf_op jit(solution)/shard_map/all_to_all | solution.py:64
  50.4 0.5 convolution_convert_fusion.3
  50.9 8.2 %fusion.52 = f32[256,7168]{1,0:T(8,128)} fusion(bf16[256,512]{0,1:T(8,128)(2,1)S(1)} %bitcast.59, bf16[512,7168]{1,0:T(8,128)(2,1)} %param.21), kind=kOutput, calls=%fused_computation.60 | convolution fusion | flops 1879048192 | bytes 14942208 | tf_op jit(solution)/shard_map/dot_general | solution.py:73
  59.1 0.7 copy-done.6
  59.7 0.1 copy.38
  59.8 0.1 eq.14
  59.9 0.1 fusion.45
  60.0 0.1 reduce_window_sum.11
  60.0 0.2 select_reduce_fusion.1
  60.2 0.1 reduce_sum.67
  60.3 0.1 copy.40
  60.4 0.1 convert_reduce_fusion.1
  60.5 144.7 %reduce-scatter.2.cloned.1.call-done = f32[8,7168]{1,0:T(8,128)} async-done(((f32[256,7168]{1,0:T(8,128)}), f32[8,7168]{1,0:T(8,128)}) %reduce-scatter.2.cloned.1.call-update) | async-done | bytes 229392 | tf_op jit(solution)/shard_map/reduce_scatter | solution.py:72
  205.2 1.1 fusion.33
  206.3 0.3 fusion.2
  206.7 0.4 broadcast_in_dim.19
  207.1 84.8 %all_to_all.29 = bf16[32,8,7168]{2,1,0:T(8,128)(2,1)S(1)} all-to-all(bf16[32,8,7168]{2,1,0:T(8,128)(2,1)S(1)} %bitcast.57), channel_id=1, replica_groups=mesh['group'=1,'expert'=32] {'expert'}, dimensions={0} | all-to-all | bytes 7340032 | tf_op jit(solution)/shard_map/all_to_all | solution.py:100
  291.9 1.8 copy-done.1
  293.7 1.2 fusion.6
  294.9 7.1 %fusion.1 = bf16[32,8,7168]{2,1,0:T(8,128)(2,1)} fusion(bf16[1,128,7168]{2,1,0:T(8,128)(2,1)} %param.27, bf16[1,7168,128]{2,1,0:T(8,128)(2,1)} %param.26, bf16[32,8,7168]{2,1,0:T(8,128)(2,1)} %copy-done.1, f32[256,128]{1,0:T(8,128)S(1)} %fusion.6), kind=kOutput, calls=%fused_computation.2 | convolution fusion | flops 941555712 | bytes 11141120 | tf_op jit(solution)/shard_map/dot_general | solution.py:106
  302.0 3.7 all-to-all-start.2
  305.7 0.1 select_reduce_fusion
  305.8 82.6 %all-to-all-done.2 = bf16[32,8,7168]{2,1,0:T(8,128)(2,1)} async-done(((bf16[32,8,7168]{2,1,0:T(8,128)(2,1)}), bf16[32,8,7168]{2,1,0:T(8,128)(2,1)}, u32[]{:S(2)}, u32[]{:S(2)}) %all-to-all-start.2) | async-done | bytes 3670048 | tf_op jit(solution)/shard_map/all_to_all | solution.py:109
  388.4 2.7 convert_reduce_fusion
  391.1 1.2 fusion.3
  (21 shorter events, 0.1 us)
Async XLA Ops:
  6.5 3.3 copy-start
  6.5 198.6 %reduce-scatter.2.cloned.1.call-start = ((), (), s32[]{:S(2)}) async-start(), calls=%async_computation.4 | async-start | bytes 7569408 | tf_op jit(solution)/shard_map/reduce_scatter | solution.py:72
  15.2 35.2 %copy-start.7 = (bf16[4,512,128]{2,1,0:T(8,128)(2,1)S(1)}, bf16[4,512,128]{2,1,0:T(8,128)(2,1)}, u32[]{:S(2)}) copy-start(bf16[4,512,128]{2,1,0:T(8,128)(2,1)} %param.20) | copy-start | bytes 1572868
  59.0 0.7 copy-start.6
  59.0 1.3 copy-start.4
  59.0 146.1 %copy-start.3 = (bf16[8,7168]{1,0:T(8,128)(2,1)S(1)}, bf16[8,7168]{1,0:T(8,128)(2,1)}, u32[]{:S(2)}) copy-start(bf16[8,7168]{1,0:T(8,128)(2,1)} %param.14) | copy-start | bytes 344068
  207.1 86.7 %copy-start.2 = (bf16[1,7168,128]{2,1,0:T(8,128)(2,1)S(1)}, bf16[1,7168,128]{2,1,0:T(8,128)(2,1)}, u32[]{:S(2)}) copy-start(bf16[1,7168,128]{2,1,0:T(8,128)(2,1)} %param.25) | copy-start | bytes 5505028
  291.9 1.8 copy-start.1
  302.0 3.7 copy-start.5
  302.0 86.4 %all-to-all-start.2 = ((bf16[32,8,7168]{2,1,0:T(8,128)(2,1)}), bf16[32,8,7168]{2,1,0:T(8,128)(2,1)}, u32[]{:S(2)}, u32[]{:S(2)}) async-start(bf16[32,8,7168]{2,1,0:T(8,128)(2,1)} %fusion.1), calls=%async_computation.3 | async-start | bytes 7340032 | tf_op jit(solution)/shard_map/all_to_all | solution.py:109
Sparse Core Ops, SparseCore 0:
  59.2 145.9 reduce-scatter.1
where the time goes:
time: 400 us; the launch traced here: 399 us
  waiting for transfers between devices  227 us (57%)
  blocking collectives  118 us (30%)
  matrix products  24.6 us (6%)
  between operations  13.5 us (3%)
  local copies, waits for them, and re-layouts  6.43 us (2%)
  other arithmetic  5.41 us (1%)
    reduce_scatter x1, waiting for transfers between devices, shards(): lax.psum_scatter(jnp.dot(per_head_value_rows.reshape(lax.axis_size('exper...  145 us
    all_to_all x1, blocking collectives, shards(): lax.all_to_all(outgoing, 'expert', split_axis=0, concat_axis=0, tiled=True)  84.8 us
    all_to_all x1, waiting for transfers between devices, shards(): lax.all_to_all(piece_out.reshape(sources, item_count, feature_count), 'ex...  82.6 us
    all_to_all x1, blocking collectives, shards(): lax.all_to_all(latent_context_output, 'expert', split_axis=1, concat_axis...  33.3 us
    dot_general x1, matrix products, shards(): jnp.dot(per_head_value_rows.reshape(lax.axis_size('expert') * tokens_here...  8.16 us
  transfers between devices with their start and end apart: 2, of which 2 were waited for; matrix products, arithmetic and copies ran while one was open for 0% of the time, Pallas kernels for 0%

commit v1 on v0

v1 whole, which is shorter than its diff:
```python
import jax
import jax.numpy as jnp
from jax import lax
from jax.sharding import PartitionSpec as P

SHARDS = 8
LANES = 128


score_scale = 192.0 ** (-0.5)
epsilon = 1e-06
route_scale = 2.5
f32 = jnp.float32
bf16 = jnp.bfloat16


def slot_table(routes, experts, capacity):
    flattened = routes.reshape(-1)
    onehot = (flattened[:, None] == jnp.arange(experts, dtype=jnp.int32)[None, :]).astype(jnp.int32)
    before = jnp.cumsum(onehot, axis=0) - onehot
    ranking = jnp.sum(before * onehot, axis=1)
    return (flattened * capacity + ranking).reshape(routes.shape)


def swap(x, bit, devices):
    return lax.ppermute(x, "expert", [(i, i ^ (1 << bit)) for i in range(devices)])


def pick(x, bits, bit, value):
    return lax.index_in_dim(x, value, bits.index(bit), keepdims=False)


def scatter_sum(partial, order, devices):
    bits = list(range(len(order)))[::-1]
    send = pick(partial, bits, order[0], 1).astype(bf16)
    keep = pick(partial, bits, order[0], 0)
    bits.remove(order[0])
    for step, bit in enumerate(order):
        came = swap(send, bit, devices)
        if step + 1 == len(order):
            return keep.astype(f32) + came.astype(f32)
        after = order[step + 1]
        halves = [
            pick(keep, bits, after, v).astype(f32) + pick(came, bits, after, v).astype(f32)
            for v in (0, 1)
        ]
        bits.remove(after)
        keep, send = halves[0].astype(bf16), halves[1].astype(bf16)


def gather(block, order, devices):
    bits = []
    for bit in order:
        came = swap(block, bit, devices)
        place = len([b for b in bits if b > bit])
        block = jnp.stack([block, came], axis=place)
        bits.insert(place, bit)
    return block


def chain_orders(nbits):
    rest = list(range(1, nbits))
    orders = []
    for first in (0, 1, 2):
        lead = [rest[first], *[b for b in rest[:3] if b != rest[first]]]
        orders.append([0, *lead, *rest[3:]])
    return orders


def cuts(width, chunks):
    tiles = width // LANES
    sizes = [(tiles // chunks + (1 if i < tiles % chunks else 0)) * LANES for i in range(chunks)]
    starts = [sum(sizes[:i]) for i in range(chunks)]
    return list(zip(starts, sizes, strict=True))


def three_parts(x):
    parts = []
    for _ in range(3):
        part = lax.reduce_precision(x, 8, 7)
        parts.append(part.astype(bf16))
        x = x - part
    return parts


def attend(q_latent, q_rope, cache_latent, cache_rope, lengths):
    tokens_here, heads_all, _ = q_latent.shape
    rope_width = cache_rope.shape[1]
    cache_rows = cache_latent.shape[1]
    scores = jnp.einsum("thk,tlk->thl", q_latent, cache_latent, preferred_element_type=f32)
    scores = scores + jnp.einsum(
        "thr,trl->thl",
        q_rope.reshape(tokens_here, heads_all, rope_width),
        cache_rope,
        preferred_element_type=f32,
    )
    scores = scores * score_scale
    usable = jnp.arange(cache_rows, dtype=jnp.int32)[None, :] < lengths[:, None]
    scores = jnp.where(usable[:, None, :], scores, -jnp.inf)
    highest = jnp.max(scores, axis=2, keepdims=True)
    expd = jnp.exp(scores - highest)
    weights = (expd / jnp.sum(expd, axis=2, keepdims=True)).astype(bf16)
    return jnp.einsum("thl,tlk->thk", weights, cache_latent, preferred_element_type=f32).astype(bf16)


def shards(
    hidden_in,
    q_latent,
    q_rope,
    cache_latent,
    cache_rope,
    lengths,
    value_up_weight,
    out_weight,
    norm_gain,
    route_ids,
    route_logits,
    gate_weight,
    up_weight,
    down_projection_weight,
):
    devices = lax.axis_size("expert")
    me = lax.axis_index("expert")
    nbits = devices.bit_length() - 1
    tokens_here = hidden_in.shape[0]
    model_width = hidden_in.shape[1]
    top_count = route_ids.shape[1]
    experts = devices // SHARDS
    orders = chain_orders(nbits)
    chunks = cuts(model_width, len(orders))
    sigm = jax.nn.sigmoid(route_logits)
    route_weights = route_scale * sigm / jnp.sum(sigm, axis=1, keepdims=True)

    latent_out = attend(q_latent, q_rope, cache_latent, cache_rope, lengths)
    by_head = lax.all_to_all(latent_out, "expert", split_axis=1, concat_axis=0, tiled=True)
    head_values = jnp.einsum(
        "aqg,qge->aqe", by_head, value_up_weight, preferred_element_type=f32
    ).astype(bf16)
    rows = devices * tokens_here
    head_values = head_values.reshape(rows, -1)
    at = jnp.arange(rows, dtype=jnp.int32)
    source = (((at // tokens_here) ^ me) * tokens_here) + at % tokens_here
    shuffle = (source[:, None] == at[None, :]).astype(bf16)
    head_values = jnp.dot(shuffle, head_values, preferred_element_type=f32).astype(bf16)
    blocks = (2,) * nbits + (tokens_here,)

    residual = []
    for (start, size), order in zip(chunks, orders, strict=True):
        partial = jnp.dot(
            head_values, out_weight[:, start : start + size], preferred_element_type=f32
        ).reshape(*blocks, size)
        attn = scatter_sum(partial, order, devices)
        residual.append((hidden_in[:, start : start + size].astype(f32) + attn).astype(bf16))

    if experts > top_count:
        return routed(
            jnp.concatenate(residual, axis=1),
            norm_gain,
            route_ids,
            route_weights,
            gate_weight,
            up_weight,
            down_projection_weight,
        )

    chosen = route_ids[:, :, None] == jnp.arange(experts, dtype=jnp.int32)[None, None, :]
    shares = jnp.sum(jnp.where(chosen, route_weights[:, :, None], 0.0), axis=1)
    extra = jnp.concatenate(three_parts(shares), axis=1)
    extra = jnp.pad(extra, ((0, 0), (0, LANES - extra.shape[1])))
    gate_act = jnp.zeros((rows, gate_weight.shape[2]), f32)
    up_act = jnp.zeros((rows, up_weight.shape[2]), f32)
    squares = jnp.zeros((rows, 1), f32)
    for i, ((start, size), order) in enumerate(zip(chunks, orders, strict=True)):
        last = i + 1 == len(chunks)
        block = jnp.concatenate([residual[i], extra], axis=1) if last else residual[i]
        taken = gather(block, order[::-1], devices).reshape(rows, -1)
        if last:
            got = taken[:, size:].astype(f32)
            taken = taken[:, :size]
        wide = taken.astype(f32)
        squares = squares + jnp.sum(wide * wide, axis=1, keepdims=True)
        scaled = (wide * norm_gain[start : start + size].astype(f32)).astype(bf16)
        gate_act = gate_act + jnp.dot(
            scaled, gate_weight[0, start : start + size], preferred_element_type=f32
        )
        up_act = up_act + jnp.dot(
            scaled, up_weight[0, start : start + size], preferred_element_type=f32
        )
    factor = lax.rsqrt(squares / model_width + epsilon)
    own = (jnp.arange(LANES, dtype=jnp.int32) % experts == me // SHARDS) & (
        jnp.arange(LANES, dtype=jnp.int32) < 3 * experts
    )
    share = jnp.sum(jnp.where(own[None, :], got, 0.0), axis=1, keepdims=True)
    hidden = (jax.nn.silu(gate_act * factor) * (up_act * factor) * share).astype(bf16)
    out = []
    for (start, size), order, base in zip(chunks, orders, residual, strict=True):
        piece = jnp.dot(
            hidden, down_projection_weight[0, :, start : start + size], preferred_element_type=f32
        ).reshape(*blocks, size)
        out.append((base.astype(f32) + scatter_sum(piece, order, devices)).astype(bf16))
    return jnp.concatenate(out, axis=1)


def routed(
    residual, norm_gain, route_ids, route_weights, gate_weight, up_weight, down_projection_weight
):
    devices = lax.axis_size("expert")
    tokens_here, model_width = residual.shape
    top_count = route_ids.shape[1]
    experts = devices // SHARDS
    capacity = min(tokens_here, max(2, (tokens_here * top_count + experts - 1) // experts + 1))
    slot_count = experts * capacity
    slot_ids = slot_table(route_ids, experts, capacity)
    slot_range = jnp.arange(slot_count, dtype=jnp.int32)
    res32 = residual.astype(f32)
    normed = (
        res32
        * lax.rsqrt(jnp.mean(res32 * res32, axis=1, keepdims=True) + epsilon)
        * norm_gain.astype(f32)
    ).astype(bf16)
    placement = jnp.sum(
        (slot_ids[:, :, None] == slot_range[None, None, :]).astype(jnp.int32), axis=1
    ).astype(bf16)
    outgoing = jnp.einsum("tq,tw->qw", placement, normed, preferred_element_type=f32).astype(bf16)
    outgoing = jnp.broadcast_to(
        outgoing.reshape(experts, 1, capacity, model_width),
        (experts, SHARDS, capacity, model_width),
    )
    outgoing = outgoing.reshape(devices, capacity, model_width)
    received = lax.all_to_all(outgoing, "expert", split_axis=0, concat_axis=0, tiled=True)
    sources, item_count, feature_count = received.shape
    flattened = received.reshape(sources * item_count, feature_count)
    gate_act = jnp.dot(flattened, gate_weight[0], preferred_element_type=f32)
    up_act = jnp.dot(flattened, up_weight[0], preferred_element_type=f32)
    hidden = (jax.nn.silu(gate_act) * up_act).astype(bf16)
    piece_out = jnp.dot(hidden, down_projection_weight[0], preferred_element_type=f32).astype(bf16)
    returned_rows = lax.all_to_all(
        piece_out.reshape(sources, item_count, feature_count),
        "expert",
        split_axis=0,
        concat_axis=0,
        tiled=True,
    )
    combiner = jnp.sum(
        route_weights[:, :, None]
        * (slot_ids[:, :, None] == slot_range[None, None, :]).astype(f32),
        axis=1,
    )
    summed = jnp.sum(
        returned_rows.reshape(experts, SHARDS, capacity, model_width).astype(f32), axis=1
    ).reshape(slot_count, model_width)
    expert_sum = jnp.dot(combiner, summed, precision=lax.Precision.HIGHEST)
    return (res32 + expert_sum).astype(bf16)


def solution(mesh):
    placed = (
        P(("group", "expert"), None),
        P(("group", "expert"), None, None),
        P(("group", "expert"), None),
        P(("group", "expert"), None, None),
        P(("group", "expert"), None, None),
        P(("group", "expert")),
        P("expert", None, None),
        P("expert", None),
        P(),
        P(("group", "expert"), None),
        P(("group", "expert"), None),
        P("expert", None, None),
        P("expert", None, None),
        P("expert", None, None),
    )
    return jax.shard_map(
        shards, mesh=mesh, in_specs=placed, out_specs=P(("group", "expert"), None), check_vma=False
    )
```

time: 400 us -> 162 us (0.41)
  waiting for transfers between devices: 227 us -> 75.7 us
  blocking collectives: 118 us -> 0 us
  starting transfers between devices: 3.67 us -> 51.6 us
  between operations: 13.5 us -> 0.63 us
  matrix products: 24.6 us -> 17.6 us
    reduce_scatter x1 -> x0, waiting for transfers between devices: 145 us -> none  [shards(): lax.psum_scatter(jnp.dot(per_head_value_rows.reshape(lax.axis_size('exper...]
    all_to_all x2 -> x0, blocking collectives: 118 us -> none  [the longest x1 84.8 us: shards(): lax.all_to_all(outgoing, 'expert', split_axis=0, concat_axis=0, tiled=True)]
    all_to_all x1, waiting for transfers between devices: 82.6 us -> 25.8 us  [shards(): lax.all_to_all(latent_out, 'expert', split_axis=1, concat_axis=0, tiled=T...]
    ppermute x0 -> x45, waiting for transfers between devices: none -> 49.9 us  [swap(): lax.ppermute(x, 'expert', [(i, i ^ 1 << bit) for i in range(devices)])]
    ppermute x0 -> x45, starting transfers between devices: none -> 44.1 us  [swap(): lax.ppermute(x, 'expert', [(i, i ^ 1 << bit) for i in range(devices)])]
    dot_general x9 -> x17, matrix products: 24.6 us -> 17.6 us  [the longest x3 7.54 us: shards(): jnp.dot(head_values, out_weight[:, start:start + size], preferred_element...]
  transfers between devices with their start and end apart: 2 -> 46, of which waited for: 2 -> 31; matrix products, arithmetic and copies ran while one was open for 0% -> 2% of each run, Pallas kernels for 0% -> 0%
where the time goes in v1:
time: 162 us
  waiting for transfers between devices  75.7 us (47%)
  starting transfers between devices  51.6 us (32%)
  matrix products  17.6 us (11%)
  local copies, waits for them, and re-layouts  9.39 us (6%)
  other arithmetic  6.72 us (4%)
    ppermute x45, waiting for transfers between devices, swap(): lax.ppermute(x, 'expert', [(i, i ^ 1 << bit) for i in range(devices)])  49.9 us
    ppermute x45, starting transfers between devices, swap(): lax.ppermute(x, 'expert', [(i, i ^ 1 << bit) for i in range(devices)])  44.1 us
    all_to_all x1, waiting for transfers between devices, shards(): lax.all_to_all(latent_out, 'expert', split_axis=1, concat_axis=0, tiled=T...  25.8 us
    dot_general x3, matrix products, shards(): jnp.dot(head_values, out_weight[:, start:start + size], preferred_element...  7.54 us
    all_to_all x1, starting transfers between devices, shards(): lax.all_to_all(latent_out, 'expert', split_axis=1, concat_axis=0, tiled=T...  7.47 us
  transfers between devices with their start and end apart: 46, of which 31 were waited for; matrix products, arithmetic and copies ran while one was open for 2% of the time, Pallas kernels for 0%

profile of v1, /device:TPU:0, one launch (start us, length us, event | category | flops | bytes accessed | tf_op | source)
XLA Modules:
  0.0 161.6 jit_solution(13411157549117953663)
XLA Ops:
  4.6 2.9 %convolution_convert_fusion = bf16[8,128,512]{2,1,0:T(8,128)(2,1)} fusion(bf16[8,256,512]{2,1,0:T(8,128)(2,1)S(1)} %copy-done, f32[8,128]{1,0:T(8,128)S(1)} %fusion.165, f32[8,128,256]{2,1,0:T(8,128)S(1)} %fusion.16), kind=kOutput, calls=%fused_computation.19 | convolution fusion | flops 269747456 | bytes 4198400 | tf_op jit(solution)/shard_map/thl,tlk->thk/dot_general | solution.py:103
  7.6 2.9 %copy.110 = bf16[8,128,512]{2,0,1:T(8,128)(2,1)} copy(bf16[8,128,512]{2,1,0:T(8,128)(2,1)} %convolution_convert_fusion) | data formatting | bytes 2097152 | tf_op jit(solution)/shard_map/convert_element_type | solution.py:103
  10.4 7.5 %all-to-all-start = ((bf16[8,128,512]{2,0,1:T(8,128)(2,1)}), bf16[8,128,512]{2,0,1:T(8,128)(2,1)S(1)}, u32[]{:S(2)}, u32[]{:S(2)}) async-start(bf16[8,128,512]{2,0,1:T(8,128)(2,1)} %copy.110), calls=%async_computation | async-start | bytes 2097152 | tf_op jit(solution)/shard_map/all_to_all | solution.py:135
  18.2 25.8 %all-to-all-done = bf16[8,128,512]{2,0,1:T(8,128)(2,1)S(1)} async-done(((bf16[8,128,512]{2,0,1:T(8,128)(2,1)}), bf16[8,128,512]{2,0,1:T(8,128)(2,1)S(1)}, u32[]{:S(2)}, u32[]{:S(2)}) %all-to-all-start) | async-done | bytes 1048608 | tf_op jit(solution)/shard_map/all_to_all | solution.py:135
  44.7 2.4 %fusion.11 = f32[256,2304]{1,0:T(8,128)S(1)} fusion(bf16[256,512]{1,0:T(8,128)(2,1)S(1)} %convolution_convert_fusion.1, bf16[512,7168]{1,0:T(8,128)(2,1)} %param.21), kind=kOutput, calls=%fused_computation.17 | convolution fusion | flops 603979776 | bytes 4980736 | tf_op jit(solution)/shard_map/dot_general | solution.py:149
  47.3 2.5 %fusion.5 = f32[256,2432]{1,0:T(8,128)S(1)} fusion(bf16[256,512]{1,0:T(8,128)(2,1)S(1)} %convolution_convert_fusion.1, bf16[512,7168]{1,0:T(8,128)(2,1)} %param.21), kind=kOutput, calls=%fused_computation.11 | convolution fusion | flops 637534208 | bytes 5242880 | tf_op jit(solution)/shard_map/dot_general | solution.py:149
  50.1 2.5 %fusion.7 = f32[256,2432]{1,0:T(8,128)S(1)} fusion(bf16[256,512]{1,0:T(8,128)(2,1)S(1)} %convolution_convert_fusion.1, bf16[512,7168]{1,0:T(8,128)(2,1)} %param.21), kind=kOutput, calls=%fused_computation.13 | convolution fusion | flops 637534208 | bytes 5242880 | tf_op jit(solution)/shard_map/dot_general | solution.py:149
  55.8 1.5 collective-permute-start.11
  57.4 1.5 collective-permute-start.1
  58.9 5.0 %collective-permute-done.21 = bf16[2,2,2,8,2304]{4,3,1,0,2:T(8,128)(2,1)S(1)} collective-permute-done((bf16[2,2,2,8,2304]{4,3,1,0,2:T(8,128)(2,1)S(1)}, bf16[2,2,2,8,2304]{4,3,1,0,2:T(8,128)(2,1)S(1)}, u32[]{:S(2)}, u32[]{:S(2)}) %collective-permute-start.21) | collective-permute-done | bytes 294944 | tf_op jit(solution)/shard_map/ppermute | solution.py:26
  64.0 1.5 collective-permute-start.22
  68.4 2.4 %collective-permute-done.22 = bf16[2,2,8,2304]{3,2,1,0:T(8,128)(2,1)S(1)} collective-permute-done((bf16[2,2,8,2304]{3,2,1,0:T(8,128)(2,1)S(1)}, bf16[2,2,8,2304]{3,2,1,0:T(8,128)(2,1)S(1)}, u32[]{:S(2)}, u32[]{:S(2)}) %collective-permute-start.22) | collective-permute-done | bytes 147488 | tf_op jit(solution)/shard_map/ppermute | solution.py:26
  70.9 1.5 collective-permute-start.23
  77.4 3.4 %collective-permute-done.24 = bf16[8,2304]{1,0:T(8,128)(2,1)S(1)} collective-permute-done((bf16[8,2304]{1,0:T(8,128)(2,1)S(1)}, bf16[8,2304]{1,0:T(8,128)(2,1)S(1)}, u32[]{:S(2)}, u32[]{:S(2)}) %collective-permute-start.24) | collective-permute-done | bytes 36896 | tf_op jit(solution)/shard_map/ppermute | solution.py:26
  81.8 2.1 %collective-permute-start.4 = (bf16[8,2432]{1,0:T(8,128)(2,1)S(1)}, bf16[8,2432]{1,0:T(8,128)(2,1)S(1)}, u32[]{:S(2)}, u32[]{:S(2)}) collective-permute-start(bf16[8,2432]{1,0:T(8,128)(2,1)S(1)} %fusion.127), channel_id=1, source_target_pairs={{0,16},{1,17},{2,18},{3,19},{4,20},{5,21},{6,22},{7,23},{8,24},{9,... | collective-permute-start | bytes 116744 | tf_op jit(solution)/shard_map/ppermute | solution.py:26
  86.0 1.9 %collective-permute-done.4 = bf16[8,2432]{1,0:T(8,128)(2,1)S(1)} collective-permute-done((bf16[8,2432]{1,0:T(8,128)(2,1)S(1)}, bf16[8,2432]{1,0:T(8,128)(2,1)S(1)}, u32[]{:S(2)}, u32[]{:S(2)}) %collective-permute-start.4) | collective-permute-done | bytes 38944 | tf_op jit(solution)/shard_map/ppermute | solution.py:26
  89.6 1.4 collective-permute-start.26
  93.8 2.1 %collective-permute-done.15 = bf16[8,2432]{1,0:T(8,128)(2,1)S(1)} collective-permute-done((bf16[8,2432]{1,0:T(8,128)(2,1)S(1)}, bf16[8,2432]{1,0:T(8,128)(2,1)S(1)}, u32[]{:S(2)}, u32[]{:S(2)}) %collective-permute-start.15) | collective-permute-done | bytes 38944 | tf_op jit(solution)/shard_map/ppermute | solution.py:26
  96.2 1.8 %collective-permute-start.27 = (bf16[2,2,8,2432]{3,2,0,1:T(8,128)(2,1)S(1)}, bf16[2,2,8,2432]{3,2,0,1:T(8,128)(2,1)S(1)}, u32[]{:S(2)}, u32[]{:S(2)}) collective-permute-start(bf16[2,2,8,2432]{3,2,0,1:T(8,128)(2,1)S(1)} %get-tuple-element.56), channel_id=1, source_target_pairs={{0,2},{1,3},{2,0},{3,1},{4,6},{5,7},{6,4},{7,5},{8,10},{9,11},{10,... | collective-permute-start | bytes 466952 | tf_op jit(solution)/shard_map/ppermute | solution.py:26
  99.3 2.0 %collective-permute-done.16 = bf16[2,8,2432]{2,1,0:T(8,128)(2,1)S(1)} collective-permute-done((bf16[2,8,2432]{2,1,0:T(8,128)(2,1)S(1)}, bf16[2,8,2432]{2,1,0:T(8,128)(2,1)S(1)}, u32[]{:S(2)}, u32[]{:S(2)}) %collective-permute-start.16) | collective-permute-done | bytes 77856 | tf_op jit(solution)/shard_map/ppermute | solution.py:26
  107.7 2.5 %collective-permute-done.28 = bf16[2,2,2,8,2432]{4,3,0,1,2:T(8,128)(2,1)S(1)} collective-permute-done((bf16[2,2,2,8,2432]{4,3,0,1,2:T(8,128)(2,1)S(1)}, bf16[2,2,2,8,2432]{4,3,0,1,2:T(8,128)(2,1)S(1)}, u32[]{:S(2)}, u32[]{:S(2)}) %collective-permute-start.28) | collective-permute-done | bytes 311328 | tf_op jit(solution)/shard_map/ppermute | solution.py:26
  110.3 1.7 %collective-permute-done.8 = bf16[2,2,2,8,2432]{4,3,0,1,2:T(8,128)(2,1)S(1)} collective-permute-done((bf16[2,2,2,8,2432]{4,3,0,1,2:T(8,128)(2,1)S(1)}, bf16[2,2,2,8,2432]{4,3,0,1,2:T(8,128)(2,1)S(1)}, u32[]{:S(2)}, u32[]{:S(2)}) %collective-permute-start.8) | collective-permute-done | bytes 311328 | tf_op jit(solution)/shard_map/ppermute | solution.py:26
  115.8 1.4 fusion.4
  130.5 1.4 collective-permute-start.31
  132.0 5.6 %collective-permute-done.41 = bf16[2,2,2,8,2304]{4,3,1,0,2:T(8,128)(2,1)S(1)} collective-permute-done((bf16[2,2,2,8,2304]{4,3,1,0,2:T(8,128)(2,1)S(1)}, bf16[2,2,2,8,2304]{4,3,1,0,2:T(8,128)(2,1)S(1)}, u32[]{:S(2)}, u32[]{:S(2)}) %collective-permute-start.41) | collective-permute-done | bytes 294944 | tf_op jit(solution)/shard_map/ppermute | solution.py:26
  141.2 3.3 %collective-permute-done.42 = bf16[2,2,8,2304]{3,2,1,0:T(8,128)(2,1)S(1)} collective-permute-done((bf16[2,2,8,2304]{3,2,1,0:T(8,128)(2,1)S(1)}, bf16[2,2,8,2304]{3,2,1,0:T(8,128)(2,1)S(1)}, u32[]{:S(2)}, u32[]{:S(2)}) %collective-permute-start.42) | collective-permute-done | bytes 147488 | tf_op jit(solution)/shard_map/ppermute | solution.py:26
  147.3 1.6 collective-permute-done.43
  149.0 1.5 collective-permute-start.44
  150.5 1.5 collective-permute-start.33
  152.0 3.2 %collective-permute-done.44 = bf16[8,2304]{1,0:T(8,128)(2,1)S(1)} collective-permute-done((bf16[8,2304]{1,0:T(8,128)(2,1)S(1)}, bf16[8,2304]{1,0:T(8,128)(2,1)S(1)}, u32[]{:S(2)}, u32[]{:S(2)}) %collective-permute-start.44) | collective-permute-done | bytes 36896 | tf_op jit(solution)/shard_map/ppermute | solution.py:26
  156.0 2.3 %collective-permute-start.34 = (bf16[8,2432]{1,0:T(8,128)(2,1)S(1)}, bf16[8,2432]{1,0:T(8,128)(2,1)S(1)}, u32[]{:S(2)}, u32[]{:S(2)}) collective-permute-start(bf16[8,2432]{1,0:T(8,128)(2,1)S(1)} %fusion.131), channel_id=1, source_target_pairs={{0,16},{1,17},{2,18},{3,19},{4,20},{5,21},{6,22},{7,23},{8,24},{9,... | collective-permute-start | bytes 116744 | tf_op jit(solution)/shard_map/ppermute | solution.py:26
  158.3 1.9 %collective-permute-done.39 = bf16[8,2432]{1,0:T(8,128)(2,1)S(1)} collective-permute-done((bf16[8,2432]{1,0:T(8,128)(2,1)S(1)}, bf16[8,2432]{1,0:T(8,128)(2,1)S(1)}, u32[]{:S(2)}, u32[]{:S(2)}) %collective-permute-start.39) | collective-permute-done | bytes 38944 | tf_op jit(solution)/shard_map/ppermute | solution.py:26
  (182 shorter events, 58.4 us)
Async XLA Ops:
  10.4 33.5 %all-to-all-start = ((bf16[8,128,512]{2,0,1:T(8,128)(2,1)}), bf16[8,128,512]{2,0,1:T(8,128)(2,1)S(1)}, u32[]{:S(2)}, u32[]{:S(2)}) async-start(bf16[8,128,512]{2,0,1:T(8,128)(2,1)} %copy.110), calls=%async_computation | async-start | bytes 2097152 | tf_op jit(solution)/shard_map/all_to_all | solution.py:135
  54.8 9.1 %collective-permute-start.21 = (bf16[2,2,2,8,2304]{4,3,1,0,2:T(8,128)(2,1)S(1)}, bf16[2,2,2,8,2304]{4,3,1,0,2:T(8,128)(2,1)S(1)}, u32[]{:S(2)}, u32[]{:S(2)}) collective-permute-start(bf16[2,2,2,8,2304]{4,3,1,0,2:T(8,128)(2,1)S(1)} %get-tuple-element.14), channel_id=1, source_target_pairs={{0,8},{1,9},{2,10},{3,11},{4,12},{5,13},{6,14},{7,15},{8,0},{9,1},... | collective-permute-start | bytes 884744 | tf_op jit(solution)/shard_map/ppermute | solution.py:26
  55.8 9.8 %collective-permute-start.11 = (bf16[2,2,2,8,2432]{4,3,1,0,2:T(8,128)(2,1)S(1)}, bf16[2,2,2,8,2432]{4,3,1,0,2:T(8,128)(2,1)S(1)}, u32[]{:S(2)}, u32[]{:S(2)}) collective-permute-start(bf16[2,2,2,8,2432]{4,3,1,0,2:T(8,128)(2,1)S(1)} %get-tuple-element.8), channel_id=1, source_target_pairs={{0,4},{1,5},{2,6},{3,7},{4,0},{5,1},{6,2},{7,3},{8,12},{9,13},{10,... | collective-permute-start | bytes 933896 | tf_op jit(solution)/shard_map/ppermute | solution.py:26
  57.4 9.7 %collective-permute-start.1 = (bf16[2,2,2,8,2432]{4,3,1,0,2:T(8,128)(2,1)S(1)}, bf16[2,2,2,8,2432]{4,3,1,0,2:T(8,128)(2,1)S(1)}, u32[]{:S(2)}, u32[]{:S(2)}) collective-permute-start(bf16[2,2,2,8,2432]{4,3,1,0,2:T(8,128)(2,1)S(1)} %get-tuple-element.10), channel_id=1, source_target_pairs={{0,2},{1,3},{2,0},{3,1},{4,6},{5,7},{6,4},{7,5},{8,10},{9,11},{10,... | collective-permute-start | bytes 933896 | tf_op jit(solution)/shard_map/ppermute | solution.py:26
  64.0 6.9 %collective-permute-start.22 = (bf16[2,2,8,2304]{3,2,1,0:T(8,128)(2,1)S(1)}, bf16[2,2,8,2304]{3,2,1,0:T(8,128)(2,1)S(1)}, u32[]{:S(2)}, u32[]{:S(2)}) collective-permute-start(bf16[2,2,8,2304]{3,2,1,0:T(8,128)(2,1)S(1)} %get-tuple-element.36), channel_id=1, source_target_pairs={{0,2},{1,3},{2,0},{3,1},{4,6},{5,7},{6,4},{7,5},{8,10},{9,11},{10,... | collective-permute-start | bytes 442376 | tf_op jit(solution)/shard_map/ppermute | solution.py:26
  65.6 7.4 %collective-permute-start.12 = (bf16[2,2,8,2432]{3,2,1,0:T(8,128)(2,1)S(1)}, bf16[2,2,8,2432]{3,2,1,0:T(8,128)(2,1)S(1)}, u32[]{:S(2)}, u32[]{:S(2)}) collective-permute-start(bf16[2,2,8,2432]{3,2,1,0:T(8,128)(2,1)S(1)} %get-tuple-element.28), channel_id=1, source_target_pairs={{0,2},{1,3},{2,0},{3,1},{4,6},{5,7},{6,4},{7,5},{8,10},{9,11},{10,... | collective-permute-start | bytes 466952 | tf_op jit(solution)/shard_map/ppermute | solution.py:26
  67.2 9.6 %collective-permute-start.2 = (bf16[2,2,8,2432]{3,2,1,0:T(8,128)(2,1)S(1)}, bf16[2,2,8,2432]{3,2,1,0:T(8,128)(2,1)S(1)}, u32[]{:S(2)}, u32[]{:S(2)}) collective-permute-start(bf16[2,2,8,2432]{3,2,1,0:T(8,128)(2,1)S(1)} %get-tuple-element.32), channel_id=1, source_target_pairs={{0,4},{1,5},{2,6},{3,7},{4,0},{5,1},{6,2},{7,3},{8,12},{9,13},{10,... | collective-permute-start | bytes 466952 | tf_op jit(solution)/shard_map/ppermute | solution.py:26
  73.1 7.7 %collective-permute-start.13 = (bf16[2,8,2432]{2,1,0:T(8,128)(2,1)S(1)}, bf16[2,8,2432]{2,1,0:T(8,128)(2,1)S(1)}, u32[]{:S(2)}, u32[]{:S(2)}) collective-permute-start(bf16[2,8,2432]{2,1,0:T(8,128)(2,1)S(1)} %get-tuple-element.46), channel_id=1, source_target_pairs={{0,8},{1,9},{2,10},{3,11},{4,12},{5,13},{6,14},{7,15},{8,0},{9,1},... | collective-permute-start | bytes 233480 | tf_op jit(solution)/shard_map/ppermute | solution.py:26
  75.3 5.4 %collective-permute-start.24 = (bf16[8,2304]{1,0:T(8,128)(2,1)S(1)}, bf16[8,2304]{1,0:T(8,128)(2,1)S(1)}, u32[]{:S(2)}, u32[]{:S(2)}) collective-permute-start(bf16[8,2304]{1,0:T(8,128)(2,1)S(1)} %fusion.135), channel_id=1, source_target_pairs={{0,16},{1,17},{2,18},{3,19},{4,20},{5,21},{6,22},{7,23},{8,24},{9,... | collective-permute-start | bytes 110600 | tf_op jit(solution)/shard_map/ppermute | solution.py:26
  76.8 5.0 %collective-permute-start.3 = (bf16[2,8,2432]{2,1,0:T(8,128)(2,1)S(1)}, bf16[2,8,2432]{2,1,0:T(8,128)(2,1)S(1)}, u32[]{:S(2)}, u32[]{:S(2)}) collective-permute-start(bf16[2,8,2432]{2,1,0:T(8,128)(2,1)S(1)} %get-tuple-element.50), channel_id=1, source_target_pairs={{0,8},{1,9},{2,10},{3,11},{4,12},{5,13},{6,14},{7,15},{8,0},{9,1},... | collective-permute-start | bytes 233480 | tf_op jit(solution)/shard_map/ppermute | solution.py:26
  80.8 5.2 %collective-permute-start.14 = (bf16[8,2432]{1,0:T(8,128)(2,1)S(1)}, bf16[8,2432]{1,0:T(8,128)(2,1)S(1)}, u32[]{:S(2)}, u32[]{:S(2)}) collective-permute-start(bf16[8,2432]{1,0:T(8,128)(2,1)S(1)} %fusion.129), channel_id=1, source_target_pairs={{0,16},{1,17},{2,18},{3,19},{4,20},{5,21},{6,22},{7,23},{8,24},{9,... | collective-permute-start | bytes 116744 | tf_op jit(solution)/shard_map/ppermute | solution.py:26
  81.8 6.1 %collective-permute-start.4 = (bf16[8,2432]{1,0:T(8,128)(2,1)S(1)}, bf16[8,2432]{1,0:T(8,128)(2,1)S(1)}, u32[]{:S(2)}, u32[]{:S(2)}) collective-permute-start(bf16[8,2432]{1,0:T(8,128)(2,1)S(1)} %fusion.127), channel_id=1, source_target_pairs={{0,16},{1,17},{2,18},{3,19},{4,20},{5,21},{6,22},{7,23},{8,24},{9,... | collective-permute-start | bytes 116744 | tf_op jit(solution)/shard_map/ppermute | solution.py:26
  83.9 5.7 %collective-permute-start.25 = (bf16[8,2432]{1,0:T(8,128)(2,1)S(1)}, bf16[8,2432]{1,0:T(8,128)(2,1)S(1)}, u32[]{:S(2)}, u32[]{:S(2)}) collective-permute-start(bf16[8,2432]{1,0:T(8,128)(2,1)S(1)} %get-tuple-element.70), channel_id=1, source_target_pairs={{0,16},{1,17},{2,18},{3,19},{4,20},{5,21},{6,22},{7,23},{8,24},{9,... | collective-permute-start | bytes 116744 | tf_op jit(solution)/shard_map/ppermute | solution.py:26
  87.9 4.9 %collective-permute-start.5 = (bf16[8,2432]{1,0:T(8,128)(2,1)S(1)}, bf16[8,2432]{1,0:T(8,128)(2,1)S(1)}, u32[]{:S(2)}, u32[]{:S(2)}) collective-permute-start(bf16[8,2432]{1,0:T(8,128)(2,1)S(1)} %get-tuple-element.62), channel_id=1, source_target_pairs={{0,16},{1,17},{2,18},{3,19},{4,20},{5,21},{6,22},{7,23},{8,24},{9,... | collective-permute-start | bytes 116744 | tf_op jit(solution)/shard_map/ppermute | solution.py:26
  89.6 6.5 %collective-permute-start.26 = (bf16[2,8,2432]{2,1,0:T(8,128)(2,1)S(1)}, bf16[2,8,2432]{2,1,0:T(8,128)(2,1)S(1)}, u32[]{:S(2)}, u32[]{:S(2)}) collective-permute-start(bf16[2,8,2432]{2,1,0:T(8,128)(2,1)S(1)} %get-tuple-element.64), channel_id=1, source_target_pairs={{0,4},{1,5},{2,6},{3,7},{4,0},{5,1},{6,2},{7,3},{8,12},{9,13},{10,... | collective-permute-start | bytes 233480 | tf_op jit(solution)/shard_map/ppermute | solution.py:26
  92.9 5.1 %collective-permute-start.6 = (bf16[2,8,2432]{2,1,0:T(8,128)(2,1)S(1)}, bf16[2,8,2432]{2,1,0:T(8,128)(2,1)S(1)}, u32[]{:S(2)}, u32[]{:S(2)}) collective-permute-start(bf16[2,8,2432]{2,1,0:T(8,128)(2,1)S(1)} %get-tuple-element.68), channel_id=1, source_target_pairs={{0,8},{1,9},{2,10},{3,11},{4,12},{5,13},{6,14},{7,15},{8,0},{9,1},... | collective-permute-start | bytes 233480 | tf_op jit(solution)/shard_map/ppermute | solution.py:26
  95.9 5.4 %collective-permute-start.16 = (bf16[2,8,2432]{2,1,0:T(8,128)(2,1)S(1)}, bf16[2,8,2432]{2,1,0:T(8,128)(2,1)S(1)}, u32[]{:S(2)}, u32[]{:S(2)}) collective-permute-start(bf16[2,8,2432]{2,1,0:T(8,128)(2,1)S(1)} %get-tuple-element.66), channel_id=1, source_target_pairs={{0,8},{1,9},{2,10},{3,11},{4,12},{5,13},{6,14},{7,15},{8,0},{9,1},... | collective-permute-start | bytes 233480 | tf_op jit(solution)/shard_map/ppermute | solution.py:26
  96.2 7.0 %collective-permute-start.27 = (bf16[2,2,8,2432]{3,2,0,1:T(8,128)(2,1)S(1)}, bf16[2,2,8,2432]{3,2,0,1:T(8,128)(2,1)S(1)}, u32[]{:S(2)}, u32[]{:S(2)}) collective-permute-start(bf16[2,2,8,2432]{3,2,0,1:T(8,128)(2,1)S(1)} %get-tuple-element.56), channel_id=1, source_target_pairs={{0,2},{1,3},{2,0},{3,1},{4,6},{5,7},{6,4},{7,5},{8,10},{9,11},{10,... | collective-permute-start | bytes 466952 | tf_op jit(solution)/shard_map/ppermute | solution.py:26
  98.0 7.0 %collective-permute-start.7 = (bf16[2,2,8,2432]{3,2,0,1:T(8,128)(2,1)S(1)}, bf16[2,2,8,2432]{3,2,0,1:T(8,128)(2,1)S(1)}, u32[]{:S(2)}, u32[]{:S(2)}) collective-permute-start(bf16[2,2,8,2432]{3,2,0,1:T(8,128)(2,1)S(1)} %get-tuple-element.60), channel_id=1, source_target_pairs={{0,4},{1,5},{2,6},{3,7},{4,0},{5,1},{6,2},{7,3},{8,12},{9,13},{10,... | collective-permute-start | bytes 466952 | tf_op jit(solution)/shard_map/ppermute | solution.py:26
  101.3 5.3 %collective-permute-start.17 = (bf16[2,2,8,2432]{3,2,0,1:T(8,128)(2,1)S(1)}, bf16[2,2,8,2432]{3,2,0,1:T(8,128)(2,1)S(1)}, u32[]{:S(2)}, u32[]{:S(2)}) collective-permute-start(bf16[2,2,8,2432]{3,2,0,1:T(8,128)(2,1)S(1)} %get-tuple-element.58), channel_id=1, source_target_pairs={{0,2},{1,3},{2,0},{3,1},{4,6},{5,7},{6,4},{7,5},{8,10},{9,11},{10,... | collective-permute-start | bytes 466952 | tf_op jit(solution)/shard_map/ppermute | solution.py:26
  103.2 7.0 %collective-permute-start.28 = (bf16[2,2,2,8,2432]{4,3,0,1,2:T(8,128)(2,1)S(1)}, bf16[2,2,2,8,2432]{4,3,0,1,2:T(8,128)(2,1)S(1)}, u32[]{:S(2)}, u32[]{:S(2)}) collective-permute-start(bf16[2,2,2,8,2432]{4,3,0,1,2:T(8,128)(2,1)S(1)} %get-tuple-element.42), channel_id=1, source_target_pairs={{0,8},{1,9},{2,10},{3,11},{4,12},{5,13},{6,14},{7,15},{8,0},{9,1},... | collective-permute-start | bytes 933896 | tf_op jit(solution)/shard_map/ppermute | solution.py:26
  105.1 7.0 %collective-permute-start.8 = (bf16[2,2,2,8,2432]{4,3,0,1,2:T(8,128)(2,1)S(1)}, bf16[2,2,2,8,2432]{4,3,0,1,2:T(8,128)(2,1)S(1)}, u32[]{:S(2)}, u32[]{:S(2)}) collective-permute-start(bf16[2,2,2,8,2432]{4,3,0,1,2:T(8,128)(2,1)S(1)} %get-tuple-element.48), channel_id=1, source_target_pairs={{0,2},{1,3},{2,0},{3,1},{4,6},{5,7},{6,4},{7,5},{8,10},{9,11},{10,... | collective-permute-start | bytes 933896 | tf_op jit(solution)/shard_map/ppermute | solution.py:26
  106.7 7.0 %collective-permute-start.18 = (bf16[2,2,2,8,2432]{4,3,0,1,2:T(8,128)(2,1)S(1)}, bf16[2,2,2,8,2432]{4,3,0,1,2:T(8,128)(2,1)S(1)}, u32[]{:S(2)}, u32[]{:S(2)}) collective-permute-start(bf16[2,2,2,8,2432]{4,3,0,1,2:T(8,128)(2,1)S(1)} %get-tuple-element.44), channel_id=1, source_target_pairs={{0,4},{1,5},{2,6},{3,7},{4,0},{5,1},{6,2},{7,3},{8,12},{9,13},{10,... | collective-permute-start | bytes 933896 | tf_op jit(solution)/shard_map/ppermute | solution.py:26
  128.4 9.1 %collective-permute-start.41 = (bf16[2,2,2,8,2304]{4,3,1,0,2:T(8,128)(2,1)S(1)}, bf16[2,2,2,8,2304]{4,3,1,0,2:T(8,128)(2,1)S(1)}, u32[]{:S(2)}, u32[]{:S(2)}) collective-permute-start(bf16[2,2,2,8,2304]{4,3,1,0,2:T(8,128)(2,1)S(1)} %get-tuple-element.12), channel_id=1, source_target_pairs={{0,8},{1,9},{2,10},{3,11},{4,12},{5,13},{6,14},{7,15},{8,0},{9,1},... | collective-permute-start | bytes 884744 | tf_op jit(solution)/shard_map/ppermute | solution.py:26
  129.3 9.7 %collective-permute-start.36 = (bf16[2,2,2,8,2432]{4,3,1,0,2:T(8,128)(2,1)S(1)}, bf16[2,2,2,8,2432]{4,3,1,0,2:T(8,128)(2,1)S(1)}, u32[]{:S(2)}, u32[]{:S(2)}) collective-permute-start(bf16[2,2,2,8,2432]{4,3,1,0,2:T(8,128)(2,1)S(1)} %get-tuple-element.6), channel_id=1, source_target_pairs={{0,4},{1,5},{2,6},{3,7},{4,0},{5,1},{6,2},{7,3},{8,12},{9,13},{10,... | collective-permute-start | bytes 933896 | tf_op jit(solution)/shard_map/ppermute | solution.py:26
  130.5 9.7 %collective-permute-start.31 = (bf16[2,2,2,8,2432]{4,3,2,1,0:T(8,128)(2,1)S(1)}, bf16[2,2,2,8,2432]{4,3,2,1,0:T(8,128)(2,1)S(1)}, u32[]{:S(2)}, u32[]{:S(2)}) collective-permute-start(bf16[2,2,2,8,2432]{4,3,2,1,0:T(8,128)(2,1)S(1)} %fusion.68), channel_id=1, source_target_pairs={{0,2},{1,3},{2,0},{3,1},{4,6},{5,7},{6,4},{7,5},{8,10},{9,11},{10,... | collective-permute-start | bytes 933896 | tf_op jit(solution)/shard_map/ppermute | solution.py:26
  137.6 6.9 %collective-permute-start.42 = (bf16[2,2,8,2304]{3,2,1,0:T(8,128)(2,1)S(1)}, bf16[2,2,8,2304]{3,2,1,0:T(8,128)(2,1)S(1)}, u32[]{:S(2)}, u32[]{:S(2)}) collective-permute-start(bf16[2,2,8,2304]{3,2,1,0:T(8,128)(2,1)S(1)} %get-tuple-element.34), channel_id=1, source_target_pairs={{0,2},{1,3},{2,0},{3,1},{4,6},{5,7},{6,4},{7,5},{8,10},{9,11},{10,... | collective-permute-start | bytes 442376 | tf_op jit(solution)/shard_map/ppermute | solution.py:26
  139.1 7.2 %collective-permute-start.37 = (bf16[2,2,8,2432]{3,2,1,0:T(8,128)(2,1)S(1)}, bf16[2,2,8,2432]{3,2,1,0:T(8,128)(2,1)S(1)}, u32[]{:S(2)}, u32[]{:S(2)}) collective-permute-start(bf16[2,2,8,2432]{3,2,1,0:T(8,128)(2,1)S(1)} %get-tuple-element.22), channel_id=1, source_target_pairs={{0,2},{1,3},{2,0},{3,1},{4,6},{5,7},{6,4},{7,5},{8,10},{9,11},{10,... | collective-permute-start | bytes 466952 | tf_op jit(solution)/shard_map/ppermute | solution.py:26
  140.3 10.2 %collective-permute-start.32 = (bf16[2,2,8,2432]{3,2,1,0:T(8,128)(2,1)S(1)}, bf16[2,2,8,2432]{3,2,1,0:T(8,128)(2,1)S(1)}, u32[]{:S(2)}, u32[]{:S(2)}) collective-permute-start(bf16[2,2,8,2432]{3,2,1,0:T(8,128)(2,1)S(1)} %fusion.88), channel_id=1, source_target_pairs={{0,4},{1,5},{2,6},{3,7},{4,0},{5,1},{6,2},{7,3},{8,12},{9,13},{10,... | collective-permute-start | bytes 466952 | tf_op jit(solution)/shard_map/ppermute | solution.py:26
  146.3 8.9 %collective-permute-start.38 = (bf16[2,8,2432]{2,1,0:T(8,128)(2,1)S(1)}, bf16[2,8,2432]{2,1,0:T(8,128)(2,1)S(1)}, u32[]{:S(2)}, u32[]{:S(2)}) collective-permute-start(bf16[2,8,2432]{2,1,0:T(8,128)(2,1)S(1)} %get-tuple-element.40), channel_id=1, source_target_pairs={{0,8},{1,9},{2,10},{3,11},{4,12},{5,13},{6,14},{7,15},{8,0},{9,1},... | collective-permute-start | bytes 233480 | tf_op jit(solution)/shard_map/ppermute | solution.py:26
  149.0 6.2 %collective-permute-start.44 = (bf16[8,2304]{1,0:T(8,128)(2,1)S(1)}, bf16[8,2304]{1,0:T(8,128)(2,1)S(1)}, u32[]{:S(2)}, u32[]{:S(2)}) collective-permute-start(bf16[8,2304]{1,0:T(8,128)(2,1)S(1)} %fusion.137), channel_id=1, source_target_pairs={{0,16},{1,17},{2,18},{3,19},{4,20},{5,21},{6,22},{7,23},{8,24},{9,... | collective-permute-start | bytes 110600 | tf_op jit(solution)/shard_map/ppermute | solution.py:26
  150.5 5.5 %collective-permute-start.33 = (bf16[2,8,2432]{2,1,0:T(8,128)(2,1)S(1)}, bf16[2,8,2432]{2,1,0:T(8,128)(2,1)S(1)}, u32[]{:S(2)}, u32[]{:S(2)}) collective-permute-start(bf16[2,8,2432]{2,1,0:T(8,128)(2,1)S(1)} %get-tuple-element.38), channel_id=1, source_target_pairs={{0,8},{1,9},{2,10},{3,11},{4,12},{5,13},{6,14},{7,15},{8,0},{9,1},... | collective-permute-start | bytes 233480 | tf_op jit(solution)/shard_map/ppermute | solution.py:26
  (25 other events, 165.9 us)

commit v2 on v1

--- a/solution.py
+++ b/solution.py
@@ -5,6 +5,7 @@
 
 SHARDS = 8
 LANES = 128
+TILE = 128
 
 
 score_scale = 192.0 ** (-0.5)
@@ -22,56 +23,67 @@
     return (flattened * capacity + ranking).reshape(routes.shape)
 
 
-def swap(x, bit, devices):
-    return lax.ppermute(x, "expert", [(i, i ^ (1 << bit)) for i in range(devices)])
-
-
-def pick(x, bits, bit, value):
-    return lax.index_in_dim(x, value, bits.index(bit), keepdims=False)
-
-
-def scatter_sum(partial, order, devices):
-    bits = list(range(len(order)))[::-1]
-    send = pick(partial, bits, order[0], 1).astype(bf16)
-    keep = pick(partial, bits, order[0], 0)
-    bits.remove(order[0])
-    for step, bit in enumerate(order):
-        came = swap(send, bit, devices)
-        if step + 1 == len(order):
-            return keep.astype(f32) + came.astype(f32)
-        after = order[step + 1]
-        halves = [
-            pick(keep, bits, after, v).astype(f32) + pick(came, bits, after, v).astype(f32)
-            for v in (0, 1)
-        ]
-        bits.remove(after)
-        keep, send = halves[0].astype(bf16), halves[1].astype(bf16)
-
-
-def gather(block, order, devices):
-    bits = []
-    for bit in order:
-        came = swap(block, bit, devices)
-        place = len([b for b in bits if b > bit])
-        block = jnp.stack([block, came], axis=place)
-        bits.insert(place, bit)
-    return block
-
-
-def chain_orders(nbits):
-    rest = list(range(1, nbits))
-    orders = []
-    for first in (0, 1, 2):
-        lead = [rest[first], *[b for b in rest[:3] if b != rest[first]]]
-        orders.append([0, *lead, *rest[3:]])
-    return orders
-
-
-def cuts(width, chunks):
-    tiles = width // LANES
-    sizes = [(tiles // chunks + (1 if i < tiles % chunks else 0)) * LANES for i in range(chunks)]
-    starts = [sum(sizes[:i]) for i in range(chunks)]
-    return list(zip(starts, sizes, strict=True))
+def stage_bits(nbits):
+    low = list(range(nbits))
+    high = [0, 2, 1, *low[3:]]
+    return list(zip(low, high, strict=True))
+
+
+def chain_plans(nbits, width):
+    stages = stage_bits(nbits)
+    tiles = width // TILE
+    plans, start = [], 0
+    for order, share in (((1, 2, 3), 19), ((1, 2, 3), 19), ((1, 2, 3), 18)):
+        order = [*order, *range(4, nbits - 1)]
+        size = tiles * share // 56 * TILE
+        plans.append((start, size, order, [stages[0], *[stages[k] for k in order], stages[-1]]))
+        start += size
+    return plans
+
+
+def reorder(rows, old, new):
+    shape = rows.shape
+    axes = [*[old.index(k) for k in new], len(old), len(old) + 1]
+    return rows.reshape(*(2,) * len(old), -1, shape[1]).transpose(axes).reshape(shape)
+
+
+def swap(x, stage, devices):
+    pairs = [(i, i ^ (1 << stage[i & 1])) for i in range(devices)]
+    return lax.ppermute(x, "expert", pairs)
+
+
+def row_sources(me, stages, devices, tokens_here):
+    at = jnp.arange(devices * tokens_here, dtype=jnp.int32)
+    place = at // tokens_here
+    top = len(stages) - 1
+    other = place >> top
+    core = (me & 1) ^ other
+    owner = me ^ other
+    for step in range(1, len(stages)):
+        bit = (place >> (top - step)) & 1
+        owner = owner ^ jnp.where(core == 0, bit << stages[step][0], bit << stages[step][1])
+    return owner * tokens_here + at % tokens_here
+
+
+def add32(a, b):
+    return a.astype(f32) + b.astype(f32)
+
+
+def halve(keep, send, stages, devices):
+    for step, stage in enumerate(stages[:-1]):
+        came = swap(send, stage, devices)
+        half = keep.shape[0] // 2
+        send = add32(keep[half:], came[half:]).astype(bf16)
+        keep = add32(keep[:half], came[:half])
+        if step + 2 < len(stages):
+            keep = keep.astype(bf16)
+    return keep, send
+
+
+def double(rows, stages, devices):
+    for stage in stages[:0:-1]:
+        rows = jnp.concatenate([rows, swap(rows, stage, devices)], axis=0)
+    return rows, swap(rows, stages[0], devices)
 
 
 def three_parts(x):
@@ -126,8 +138,8 @@
     model_width = hidden_in.shape[1]
     top_count = route_ids.shape[1]
     experts = devices // SHARDS
-    orders = chain_orders(nbits)
-    chunks = cuts(model_width, len(orders))
+    plans = chain_plans(nbits, model_width)
+    base_order = plans[0][2]
     sigm = jax.nn.sigmoid(route_logits)
     route_weights = route_scale * sigm / jnp.sum(sigm, axis=1, keepdims=True)
 
@@ -137,24 +149,35 @@
         "aqg,qge->aqe", by_head, value_up_weight, preferred_element_type=f32
     ).astype(bf16)
     rows = devices * tokens_here
+    half = rows // 2
     head_values = head_values.reshape(rows, -1)
-    at = jnp.arange(rows, dtype=jnp.int32)
-    source = (((at // tokens_here) ^ me) * tokens_here) + at % tokens_here
-    shuffle = (source[:, None] == at[None, :]).astype(bf16)
-    head_values = jnp.dot(shuffle, head_values, preferred_element_type=f32).astype(bf16)
-    blocks = (2,) * nbits + (tokens_here,)
+    chosen = route_ids[:, :, None] == jnp.arange(experts, dtype=jnp.int32)[None, None, :]
+    shares = jnp.sum(jnp.where(chosen, route_weights[:, :, None], 0.0), axis=1)
+    extra = jnp.concatenate(three_parts(shares), axis=1)
+    extra = jnp.pad(extra, ((0, 0), (0, LANES - extra.shape[1])))
+    dense = experts <= top_count
 
     residual = []
-    for (start, size), order in zip(chunks, orders, strict=True):
-        partial = jnp.dot(
-            head_values, out_weight[:, start : start + size], preferred_element_type=f32
-        ).reshape(*blocks, size)
-        attn = scatter_sum(partial, order, devices)
-        residual.append((hidden_in[:, start : start + size].astype(f32) + attn).astype(bf16))
-
-    if experts > top_count:
+    for i, (start, size, _, stages) in enumerate(plans):
+        source = row_sources(me, stages, devices, tokens_here)
+        shuffle = (source[:, None] == jnp.arange(rows, dtype=jnp.int32)[None, :]).astype(bf16)
+        values = jnp.dot(shuffle, head_values, preferred_element_type=f32).astype(bf16)
+        weight = out_weight[:, start : start + size]
+        send = jnp.dot(values[half:], weight, preferred_element_type=f32).astype(bf16)
+        keep = jnp.dot(values[:half], weight, preferred_element_type=f32)
+        own, partners = halve(keep, send, stages, devices)
+        own = (own + hidden_in[:, start : start + size].astype(f32)).astype(bf16)
+        both = jnp.concatenate([own, partners], axis=0)
+        if dense and i + 1 == len(plans):
+            beside = jnp.concatenate([extra, jnp.zeros_like(extra)], axis=0)
+            both = jnp.concatenate([both, beside], axis=1)
+        came = swap(both, stages[-1], devices)
+        came = jnp.concatenate([came[tokens_here:], came[:tokens_here]], axis=0)
+        residual.append(add32(both, came).astype(bf16))
+
+    if not dense:
         return routed(
-            jnp.concatenate(residual, axis=1),
+            jnp.concatenate(residual, axis=1)[:tokens_here],
             norm_gain,
             route_ids,
             route_weights,
@@ -163,41 +186,54 @@
             down_projection_weight,
         )
 
-    chosen = route_ids[:, :, None] == jnp.arange(experts, dtype=jnp.int32)[None, None, :]
-    shares = jnp.sum(jnp.where(chosen, route_weights[:, :, None], 0.0), axis=1)
-    extra = jnp.concatenate(three_parts(shares), axis=1)
-    extra = jnp.pad(extra, ((0, 0), (0, LANES - extra.shape[1])))
-    gate_act = jnp.zeros((rows, gate_weight.shape[2]), f32)
-    up_act = jnp.zeros((rows, up_weight.shape[2]), f32)
-    squares = jnp.zeros((rows, 1), f32)
-    for i, ((start, size), order) in enumerate(zip(chunks, orders, strict=True)):
-        last = i + 1 == len(chunks)
-        block = jnp.concatenate([residual[i], extra], axis=1) if last else residual[i]
-        taken = gather(block, order[::-1], devices).reshape(rows, -1)
-        if last:
-            got = taken[:, size:].astype(f32)
-            taken = taken[:, :size]
-        wide = taken.astype(f32)
-        squares = squares + jnp.sum(wide * wide, axis=1, keepdims=True)
-        scaled = (wide * norm_gain[start : start + size].astype(f32)).astype(bf16)
-        gate_act = gate_act + jnp.dot(
-            scaled, gate_weight[0, start : start + size], preferred_element_type=f32
+    gate_act, up_act, squares = [0.0, 0.0], [0.0, 0.0], [0.0, 0.0]
+    got = [None, None]
+    for i, (start, size, order, stages) in enumerate(plans):
+        gain = norm_gain[start : start + size].astype(f32)
+        for h, taken in enumerate(double(residual[i], stages[:-1], devices)):
+            if i + 1 == len(plans):
+                got[h] = reorder(taken[:, size:].astype(f32), order, base_order)
+                taken = taken[:, :size]
+            wide = taken.astype(f32)
+            parts = (
+                jnp.sum(wide * wide, axis=1, keepdims=True),
+                jnp.dot(
+                    (wide * gain).astype(bf16),
+                    gate_weight[0, start : start + size],
+                    preferred_element_type=f32,
+                ),
+                jnp.dot(
+                    (wide * gain).astype(bf16),
+                    up_weight[0, start : start + size],
+                    preferred_element_type=f32,
+                ),
+            )
+            if order != base_order:
+                parts = tuple(reorder(p, order, base_order) for p in parts)
+            squares[h], gate_act[h], up_act[h] = (
+                squares[h] + parts[0],
+                gate_act[h] + parts[1],
+                up_act[h] + parts[2],
+            )
+    lane = jnp.arange(LANES, dtype=jnp.int32)
+    own = (lane % experts == me // SHARDS) & (lane < 3 * experts)
+    hidden = []
+    for h in range(2):
+        factor = lax.rsqrt(squares[h] / model_width + epsilon)
+        share = jnp.sum(jnp.where(own[None, :], got[h], 0.0), axis=1, keepdims=True)
+        hidden.append(
+            (jax.nn.silu(gate_act[h] * factor) * (up_act[h] * factor) * share).astype(bf16)
         )
-        up_act = up_act + jnp.dot(
-            scaled, up_weight[0, start : start + size], preferred_element_type=f32
-        )
-    factor = lax.rsqrt(squares / model_width + epsilon)
-    own = (jnp.arange(LANES, dtype=jnp.int32) % experts == me // SHARDS) & (
-        jnp.arange(LANES, dtype=jnp.int32) < 3 * experts
-    )
-    share = jnp.sum(jnp.where(own[None, :], got, 0.0), axis=1, keepdims=True)
-    hidden = (jax.nn.silu(gate_act * factor) * (up_act * factor) * share).astype(bf16)
     out = []
-    for (start, size), order, base in zip(chunks, orders, residual, strict=True):
-        piece = jnp.dot(
-            hidden, down_projection_weight[0, :, start : start + size], preferred_element_type=f32
-        ).reshape(*blocks, size)
-        out.append((base.astype(f32) + scatter_sum(piece, order, devices)).astype(bf16))
+    for (start, size, order, stages), base in zip(plans, residual, strict=True):
+        weight = down_projection_weight[0, :, start : start + size]
+        acts = [reorder(x, base_order, order) for x in hidden] if order != base_order else hidden
+        send = jnp.dot(acts[1], weight, preferred_element_type=f32).astype(bf16)
+        keep = jnp.dot(acts[0], weight, preferred_element_type=f32)
+        own, partners = halve(keep, send, stages, devices)
+        came = swap(partners, stages[-1], devices)
+        total = base[:tokens_here, :size].astype(f32) + own + came.astype(f32)
+        out.append(total.astype(bf16))
     return jnp.concatenate(out, axis=1)
 
 

time: 162 us -> 157 us (0.969)
  matrix products: 17.6 us -> 23.1 us
  starting transfers between devices: 51.6 us -> 46.4 us
  local copies, waits for them, and re-layouts: 9.39 us -> 6.04 us
    ppermute x45 -> x42, starting transfers between devices: 44.1 us -> 38.9 us  [swap(): return lax.ppermute(x, 'expert', pairs)]
    dot_general x12 -> x24, matrix products: 11.8 us -> 16.2 us  [the longest x3 6.95 us: shards(): jnp.dot(values[half:], weight, preferred_element_type=f32).astype(bf16)]
    convert_element_type x8 -> x0, local copies, waits for them, and re-layouts: 1.86 us -> none  [the longest x2 1.47 us: shards(): scaled = (wide * norm_gain[start:start + size].astype(f32)).astype(bf16)]
    ppermute x45 -> x42, waiting for transfers between devices: 49.9 us -> 49.6 us  [swap(): return lax.ppermute(x, 'expert', pairs)]
  transfers between devices with their start and end apart: 46 -> 43, of which waited for: 31 -> 26; matrix products, arithmetic and copies ran while one was open for 2% -> 5% of each run, Pallas kernels for 0% -> 0%
where the time goes in v2:
time: 157 us
  waiting for transfers between devices  75.4 us (48%)
  starting transfers between devices  46.4 us (30%)
  matrix products  23.1 us (15%)
  local copies, waits for them, and re-layouts  6.04 us (4%)
  other arithmetic  5.32 us (3%)
    ppermute x42, waiting for transfers between devices, swap(): return lax.ppermute(x, 'expert', pairs)  49.6 us
    ppermute x42, starting transfers between devices, swap(): return lax.ppermute(x, 'expert', pairs)  38.9 us
    all_to_all x1, waiting for transfers between devices, shards(): lax.all_to_all(latent_out, 'expert', split_axis=1, concat_axis=0, tiled=T...  25.7 us
    all_to_all x1, starting transfers between devices, shards(): lax.all_to_all(latent_out, 'expert', split_axis=1, concat_axis=0, tiled=T...  7.47 us
    dot_general x3, matrix products, shards(): jnp.dot(values[half:], weight, preferred_element_type=f32).astype(bf16)  6.95 us
    dot_general x3, matrix products, shards(): keep = jnp.dot(values[:half], weight, preferred_element_type=f32)  3.24 us
  transfers between devices with their start and end apart: 43, of which 26 were waited for; matrix products, arithmetic and copies ran while one was open for 5% of the time, Pallas kernels for 0%

profile of v2, /device:TPU:0, one launch (start us, length us, event | category | flops | bytes accessed | tf_op | source)
XLA Modules:
  0.0 156.8 jit_solution(14670960587783075605)
XLA Ops:
  4.6 3.0 %convolution_convert_fusion.6 = bf16[8,128,512]{2,1,0:T(8,128)(2,1)} fusion(bf16[8,256,512]{2,1,0:T(8,128)(2,1)S(1)} %copy-done, f32[8,128]{1,0:T(8,128)S(1)} %fusion.140, f32[8,128,256]{2,1,0:T(8,128)S(1)} %fusion.13), kind=kOutput, calls=%fused_computation.24 | convolution fusion | flops 269747456 | bytes 4198400 | tf_op jit(solution)/shard_map/thl,tlk->thk/dot_general | solution.py:115
  7.6 2.8 %copy.32 = bf16[8,128,512]{2,0,1:T(8,128)(2,1)} copy(bf16[8,128,512]{2,1,0:T(8,128)(2,1)} %convolution_convert_fusion.6) | data formatting | bytes 2097152 | tf_op jit(solution)/shard_map/convert_element_type | solution.py:115
  10.4 7.5 %all-to-all-start = ((bf16[8,128,512]{2,0,1:T(8,128)(2,1)}), bf16[8,128,512]{2,0,1:T(8,128)(2,1)S(1)}, u32[]{:S(2)}, u32[]{:S(2)}) async-start(bf16[8,128,512]{2,0,1:T(8,128)(2,1)} %copy.32), calls=%async_computation | async-start | bytes 2097152 | tf_op jit(solution)/shard_map/all_to_all | solution.py:147
  18.1 25.7 %all-to-all-done = bf16[8,128,512]{2,0,1:T(8,128)(2,1)S(1)} async-done(((bf16[8,128,512]{2,0,1:T(8,128)(2,1)}), bf16[8,128,512]{2,0,1:T(8,128)(2,1)S(1)}, u32[]{:S(2)}, u32[]{:S(2)}) %all-to-all-start) | async-done | bytes 1048608 | tf_op jit(solution)/shard_map/all_to_all | solution.py:147
  43.9 1.5 convolution_convert_fusion.8
  45.7 2.3 %convolution_convert_fusion.3 = bf16[128,2304]{1,0:T(8,128)(2,1)S(1)} fusion(bf16[512,7168]{1,0:T(8,128)(2,1)} %param.21, bf16[256,512]{1,0:T(8,128)(2,1)S(1)} %convolution_convert_fusion.7), kind=kOutput, calls=%fused_computation.4 | convolution fusion | flops 302284800 | bytes 3080192 | tf_op jit(solution)/shard_map/dot_general | solution.py:166
  48.0 2.4 %convolution_convert_fusion.4 = bf16[128,2432]{1,0:T(8,128)(2,1)S(1)} fusion(bf16[512,7168]{1,0:T(8,128)(2,1)} %param.21, bf16[256,512]{1,0:T(8,128)(2,1)S(1)} %convolution_convert_fusion.7), kind=kOutput, calls=%fused_computation.5 | convolution fusion | flops 319078400 | bytes 3244032 | tf_op jit(solution)/shard_map/dot_general | solution.py:166
  50.4 2.2 %convolution_convert_fusion.5 = bf16[128,2432]{1,0:T(8,128)(2,1)S(1)} fusion(bf16[512,7168]{1,0:T(8,128)(2,1)} %param.21, bf16[256,512]{1,0:T(8,128)(2,1)S(1)} %convolution_convert_fusion.7), kind=kOutput, calls=%fused_computation.6 | convolution fusion | flops 319078400 | bytes 3244032 | tf_op jit(solution)/shard_map/dot_general | solution.py:166
  52.7 2.2 %fusion.2 = f32[128,2432]{1,0:T(8,128)S(1)} fusion(bf16[512,7168]{1,0:T(8,128)(2,1)} %param.21, bf16[256,512]{1,0:T(8,128)(2,1)S(1)} %convolution_convert_fusion.7), kind=kOutput, calls=%fused_computation.8 | convolution fusion | flops 318767104 | bytes 3866624 | tf_op jit(solution)/shard_map/dot_general | solution.py:167
  61.2 2.7 %collective-permute-done.17 = bf16[64,2304]{1,0:T(8,128)(2,1)S(1)} collective-permute-done((bf16[64,2304]{1,0:T(8,128)(2,1)S(1)}, bf16[64,2304]{1,0:T(8,128)(2,1)S(1)}, u32[]{:S(2)}, u32[]{:S(2)}) %collective-permute-start.17) | collective-permute-done | bytes 294944 | tf_op jit(solution)/shard_map/ppermute | solution.py:52
  64.0 1.5 collective-permute-start.18
  65.5 3.0 %collective-permute-done.9 = bf16[64,2432]{1,0:T(8,128)(2,1)S(1)} collective-permute-done((bf16[64,2432]{1,0:T(8,128)(2,1)S(1)}, bf16[64,2432]{1,0:T(8,128)(2,1)S(1)}, u32[]{:S(2)}, u32[]{:S(2)}) %collective-permute-start.9) | collective-permute-done | bytes 311328 | tf_op jit(solution)/shard_map/ppermute | solution.py:52
  68.6 1.5 collective-permute-start.10
  70.1 3.7 %collective-permute-done.1 = bf16[64,2432]{1,0:T(8,128)(2,1)S(1)} collective-permute-done((bf16[64,2432]{1,0:T(8,128)(2,1)S(1)}, bf16[64,2432]{1,0:T(8,128)(2,1)S(1)}, u32[]{:S(2)}, u32[]{:S(2)}) %collective-permute-start.1) | collective-permute-done | bytes 311328 | tf_op jit(solution)/shard_map/ppermute | solution.py:52
  73.9 1.5 collective-permute-start.2
  76.1 1.6 %collective-permute-start.11 = (bf16[16,2432]{1,0:T(8,128)(2,1)S(1)}, bf16[16,2432]{1,0:T(8,128)(2,1)S(1)}, u32[]{:S(2)}, u32[]{:S(2)}) collective-permute-start(bf16[16,2432]{1,0:T(8,128)(2,1)S(1)} %get-tuple-element.42), channel_id=1, source_target_pairs={{0,8},{1,9},{2,10},{3,11},{4,12},{5,13},{6,14},{7,15},{8,0},{9,1},... | collective-permute-start | bytes 233480 | tf_op jit(solution)/shard_map/ppermute | solution.py:52
  81.7 3.4 %collective-permute-done.3 = bf16[16,2432]{1,0:T(8,128)(2,1)S(1)} collective-permute-done((bf16[16,2432]{1,0:T(8,128)(2,1)S(1)}, bf16[16,2432]{1,0:T(8,128)(2,1)S(1)}, u32[]{:S(2)}, u32[]{:S(2)}) %collective-permute-start.3) | collective-permute-done | bytes 77856 | tf_op jit(solution)/shard_map/ppermute | solution.py:52
  85.6 2.6 %collective-permute-start.4 = (bf16[16,2432]{1,0:T(8,128)(2,1)S(1)}, bf16[16,2432]{1,0:T(8,128)(2,1)S(1)}, u32[]{:S(2)}, u32[]{:S(2)}) collective-permute-start(bf16[16,2432]{1,0:T(8,128)(2,1)S(1)} %pad_maximum_fusion.10), channel_id=1, source_target_pairs={{0,16},{1,17},{2,18},{3,19},{4,20},{5,21},{6,22},{7,23},{8,24},{9,... | collective-permute-start | bytes 233480 | tf_op jit(solution)/shard_map/ppermute | solution.py:52
  88.3 3.2 %collective-permute-done.12 = bf16[16,2432]{1,0:T(8,128)(2,1)S(1)} collective-permute-done((bf16[16,2432]{1,0:T(8,128)(2,1)S(1)}, bf16[16,2432]{1,0:T(8,128)(2,1)S(1)}, u32[]{:S(2)}, u32[]{:S(2)}) %collective-permute-start.12) | collective-permute-done | bytes 77856 | tf_op jit(solution)/shard_map/ppermute | solution.py:52
  98.2 1.7 %collective-permute-done.22 = bf16[32,2432]{1,0:T(8,128)(2,1)S(1)} collective-permute-done((bf16[32,2432]{1,0:T(8,128)(2,1)S(1)}, bf16[32,2432]{1,0:T(8,128)(2,1)S(1)}, u32[]{:S(2)}, u32[]{:S(2)}) %collective-permute-start.22) | collective-permute-done | bytes 155680 | tf_op jit(solution)/shard_map/ppermute | solution.py:52
  101.1 2.2 %collective-permute-done.14 = bf16[32,2432]{1,0:T(8,128)(2,1)S(1)} collective-permute-done((bf16[32,2432]{1,0:T(8,128)(2,1)S(1)}, bf16[32,2432]{1,0:T(8,128)(2,1)S(1)}, u32[]{:S(2)}, u32[]{:S(2)}) %collective-permute-start.14) | collective-permute-done | bytes 155680 | tf_op jit(solution)/shard_map/ppermute | solution.py:52
  104.4 2.2 %collective-permute-done.6 = bf16[32,2432]{1,0:T(8,128)(2,1)S(1)} collective-permute-done((bf16[32,2432]{1,0:T(8,128)(2,1)S(1)}, bf16[32,2432]{1,0:T(8,128)(2,1)S(1)}, u32[]{:S(2)}, u32[]{:S(2)}) %collective-permute-start.6) | collective-permute-done | bytes 155680 | tf_op jit(solution)/shard_map/ppermute | solution.py:52
  110.9 2.7 %collective-permute-done.7 = bf16[64,2432]{1,0:T(8,128)(2,1)S(1)} collective-permute-done((bf16[64,2432]{1,0:T(8,128)(2,1)S(1)}, bf16[64,2432]{1,0:T(8,128)(2,1)S(1)}, u32[]{:S(2)}, u32[]{:S(2)}) %collective-permute-start.7) | collective-permute-done | bytes 311328 | tf_op jit(solution)/shard_map/ppermute | solution.py:52
  126.5 2.4 %collective-permute-done.38 = bf16[64,2304]{1,0:T(8,128)(2,1)S(1)} collective-permute-done((bf16[64,2304]{1,0:T(8,128)(2,1)S(1)}, bf16[64,2304]{1,0:T(8,128)(2,1)S(1)}, u32[]{:S(2)}, u32[]{:S(2)}) %collective-permute-start.38) | collective-permute-done | bytes 294944 | tf_op jit(solution)/shard_map/ppermute | solution.py:52
  130.1 3.4 %collective-permute-done.33 = bf16[64,2432]{1,0:T(8,128)(2,1)S(1)} collective-permute-done((bf16[64,2432]{1,0:T(8,128)(2,1)S(1)}, bf16[64,2432]{1,0:T(8,128)(2,1)S(1)}, u32[]{:S(2)}, u32[]{:S(2)}) %collective-permute-start.33) | collective-permute-done | bytes 311328 | tf_op jit(solution)/shard_map/ppermute | solution.py:52
  134.6 4.3 %collective-permute-done.28 = bf16[64,2432]{1,0:T(8,128)(2,1)S(1)} collective-permute-done((bf16[64,2432]{1,0:T(8,128)(2,1)S(1)}, bf16[64,2432]{1,0:T(8,128)(2,1)S(1)}, u32[]{:S(2)}, u32[]{:S(2)}) %collective-permute-start.28) | collective-permute-done | bytes 311328 | tf_op jit(solution)/shard_map/ppermute | solution.py:52
  140.3 2.0 %collective-permute-start.35 = (bf16[16,2432]{1,0:T(8,128)(2,1)S(1)}, bf16[16,2432]{1,0:T(8,128)(2,1)S(1)}, u32[]{:S(2)}, u32[]{:S(2)}) collective-permute-start(bf16[16,2432]{1,0:T(8,128)(2,1)S(1)} %get-tuple-element.38), channel_id=1, source_target_pairs={{0,8},{1,9},{2,10},{3,11},{4,12},{5,13},{6,14},{7,15},{8,0},{9,1},... | collective-permute-start | bytes 233480 | tf_op jit(solution)/shard_map/ppermute | solution.py:52
  142.3 3.0 %collective-permute-done.40 = bf16[16,2304]{1,0:T(8,128)(2,1)S(1)} collective-permute-done((bf16[16,2304]{1,0:T(8,128)(2,1)S(1)}, bf16[16,2304]{1,0:T(8,128)(2,1)S(1)}, u32[]{:S(2)}, u32[]{:S(2)}) %collective-permute-start.40) | collective-permute-done | bytes 73760 | tf_op jit(solution)/shard_map/ppermute | solution.py:52
  145.4 1.7 %collective-permute-start.30 = (bf16[16,2432]{1,0:T(8,128)(2,1)S(1)}, bf16[16,2432]{1,0:T(8,128)(2,1)S(1)}, u32[]{:S(2)}, u32[]{:S(2)}) collective-permute-start(bf16[16,2432]{1,0:T(8,128)(2,1)S(1)} %get-tuple-element.36), channel_id=1, source_target_pairs={{0,8},{1,9},{2,10},{3,11},{4,12},{5,13},{6,14},{7,15},{8,0},{9,1},... | collective-permute-start | bytes 233480 | tf_op jit(solution)/shard_map/ppermute | solution.py:52
  147.1 3.6 %collective-permute-done.41 = bf16[8,2304]{1,0:T(8,128)(2,1)S(1)} collective-permute-done((bf16[8,2304]{1,0:T(8,128)(2,1)S(1)}, bf16[8,2304]{1,0:T(8,128)(2,1)S(1)}, u32[]{:S(2)}, u32[]{:S(2)}) %collective-permute-start.41) | collective-permute-done | bytes 36896 | tf_op jit(solution)/shard_map/ppermute | solution.py:52
  151.0 2.9 %collective-permute-start.31 = (bf16[8,2432]{1,0:T(8,128)(2,1)S(1)}, bf16[8,2432]{1,0:T(8,128)(2,1)S(1)}, u32[]{:S(2)}, u32[]{:S(2)}) collective-permute-start(bf16[8,2432]{1,0:T(8,128)(2,1)S(1)} %add_convert_fusion.30), channel_id=1, source_target_pairs={{0,16},{1,17},{2,18},{3,19},{4,20},{5,21},{6,22},{7,23},{8,24},{9,... | collective-permute-start | bytes 116744 | tf_op jit(solution)/shard_map/ppermute | solution.py:52
  153.8 1.9 %collective-permute-done.36 = bf16[8,2432]{1,0:T(8,128)(2,1)S(1)} collective-permute-done((bf16[8,2432]{1,0:T(8,128)(2,1)S(1)}, bf16[8,2432]{1,0:T(8,128)(2,1)S(1)}, u32[]{:S(2)}, u32[]{:S(2)}) %collective-permute-start.36) | collective-permute-done | bytes 38944 | tf_op jit(solution)/shard_map/ppermute | solution.py:52
  (172 shorter events, 47.8 us)
Async XLA Ops:
  10.4 33.5 %all-to-all-start = ((bf16[8,128,512]{2,0,1:T(8,128)(2,1)}), bf16[8,128,512]{2,0,1:T(8,128)(2,1)S(1)}, u32[]{:S(2)}, u32[]{:S(2)}) async-start(bf16[8,128,512]{2,0,1:T(8,128)(2,1)} %copy.32), calls=%async_computation | async-start | bytes 2097152 | tf_op jit(solution)/shard_map/all_to_all | solution.py:147
  55.0 5.4 %collective-permute-start = (bf16[128,2432]{1,0:T(8,128)(2,1)S(1)}, bf16[128,2432]{1,0:T(8,128)(2,1)S(1)}, u32[]{:S(2)}, u32[]{:S(2)}) collective-permute-start(bf16[128,2432]{1,0:T(8,128)(2,1)S(1)} %convolution_convert_fusion.5), channel_id=1, source_target_pairs={{0,1},{1,0},{2,3},{3,2},{4,5},{5,4},{6,7},{7,6},{8,9},{9,8},{10,11... | collective-permute-start | bytes 1867784 | tf_op jit(solution)/shard_map/ppermute | solution.py:52
  57.1 6.8 %collective-permute-start.17 = (bf16[64,2304]{1,0:T(8,128)(2,1)S(1)}, bf16[64,2304]{1,0:T(8,128)(2,1)S(1)}, u32[]{:S(2)}, u32[]{:S(2)}) collective-permute-start(bf16[64,2304]{1,0:T(8,128)(2,1)S(1)} %get-tuple-element.22), channel_id=1, source_target_pairs={{0,2},{1,5},{2,0},{3,7},{4,6},{5,1},{6,4},{7,3},{8,10},{9,13},{10,... | collective-permute-start | bytes 884744 | tf_op jit(solution)/shard_map/ppermute | solution.py:52
  58.9 9.6 %collective-permute-start.9 = (bf16[64,2432]{1,0:T(8,128)(2,1)S(1)}, bf16[64,2432]{1,0:T(8,128)(2,1)S(1)}, u32[]{:S(2)}, u32[]{:S(2)}) collective-permute-start(bf16[64,2432]{1,0:T(8,128)(2,1)S(1)} %get-tuple-element.18), channel_id=1, source_target_pairs={{0,2},{1,5},{2,0},{3,7},{4,6},{5,1},{6,4},{7,3},{8,10},{9,13},{10,... | collective-permute-start | bytes 933896 | tf_op jit(solution)/shard_map/ppermute | solution.py:52
  60.5 13.3 %collective-permute-start.1 = (bf16[64,2432]{1,0:T(8,128)(2,1)S(1)}, bf16[64,2432]{1,0:T(8,128)(2,1)S(1)}, u32[]{:S(2)}, u32[]{:S(2)}) collective-permute-start(bf16[64,2432]{1,0:T(8,128)(2,1)S(1)} %get-tuple-element.16), channel_id=1, source_target_pairs={{0,2},{1,5},{2,0},{3,7},{4,6},{5,1},{6,4},{7,3},{8,10},{9,13},{10,... | collective-permute-start | bytes 933896 | tf_op jit(solution)/shard_map/ppermute | solution.py:52
  64.0 11.5 %collective-permute-start.18 = (bf16[32,2304]{1,0:T(8,128)(2,1)S(1)}, bf16[32,2304]{1,0:T(8,128)(2,1)S(1)}, u32[]{:S(2)}, u32[]{:S(2)}) collective-permute-start(bf16[32,2304]{1,0:T(8,128)(2,1)S(1)} %get-tuple-element.34), channel_id=1, source_target_pairs={{0,4},{1,3},{2,6},{3,1},{4,0},{5,7},{6,2},{7,5},{8,12},{9,11},{10,... | collective-permute-start | bytes 442376 | tf_op jit(solution)/shard_map/ppermute | solution.py:52
  68.6 7.5 %collective-permute-start.10 = (bf16[32,2432]{1,0:T(8,128)(2,1)S(1)}, bf16[32,2432]{1,0:T(8,128)(2,1)S(1)}, u32[]{:S(2)}, u32[]{:S(2)}) collective-permute-start(bf16[32,2432]{1,0:T(8,128)(2,1)S(1)} %get-tuple-element.30), channel_id=1, source_target_pairs={{0,4},{1,3},{2,6},{3,1},{4,0},{5,7},{6,2},{7,5},{8,12},{9,11},{10,... | collective-permute-start | bytes 466952 | tf_op jit(solution)/shard_map/ppermute | solution.py:52
  73.9 5.3 %collective-permute-start.2 = (bf16[32,2432]{1,0:T(8,128)(2,1)S(1)}, bf16[32,2432]{1,0:T(8,128)(2,1)S(1)}, u32[]{:S(2)}, u32[]{:S(2)}) collective-permute-start(bf16[32,2432]{1,0:T(8,128)(2,1)S(1)} %get-tuple-element.28), channel_id=1, source_target_pairs={{0,4},{1,3},{2,6},{3,1},{4,0},{5,7},{6,2},{7,5},{8,12},{9,11},{10,... | collective-permute-start | bytes 466952 | tf_op jit(solution)/shard_map/ppermute | solution.py:52
  76.1 5.5 %collective-permute-start.11 = (bf16[16,2432]{1,0:T(8,128)(2,1)S(1)}, bf16[16,2432]{1,0:T(8,128)(2,1)S(1)}, u32[]{:S(2)}, u32[]{:S(2)}) collective-permute-start(bf16[16,2432]{1,0:T(8,128)(2,1)S(1)} %get-tuple-element.42), channel_id=1, source_target_pairs={{0,8},{1,9},{2,10},{3,11},{4,12},{5,13},{6,14},{7,15},{8,0},{9,1},... | collective-permute-start | bytes 233480 | tf_op jit(solution)/shard_map/ppermute | solution.py:52
  79.3 5.9 %collective-permute-start.3 = (bf16[16,2432]{1,0:T(8,128)(2,1)S(1)}, bf16[16,2432]{1,0:T(8,128)(2,1)S(1)}, u32[]{:S(2)}, u32[]{:S(2)}) collective-permute-start(bf16[16,2432]{1,0:T(8,128)(2,1)S(1)} %get-tuple-element.40), channel_id=1, source_target_pairs={{0,8},{1,9},{2,10},{3,11},{4,12},{5,13},{6,14},{7,15},{8,0},{9,1},... | collective-permute-start | bytes 233480 | tf_op jit(solution)/shard_map/ppermute | solution.py:52
  80.1 8.1 %collective-permute-start.20 = (bf16[16,2432]{1,0:T(8,128)(2,1)S(1)}, bf16[16,2432]{1,0:T(8,128)(2,1)S(1)}, u32[]{:S(2)}, u32[]{:S(2)}) collective-permute-start(bf16[16,2432]{1,0:T(8,128)(2,1)S(1)} %fusion.116), channel_id=1, source_target_pairs={{0,16},{1,17},{2,18},{3,19},{4,20},{5,21},{6,22},{7,23},{8,24},{9,... | collective-permute-start | bytes 233480 | tf_op jit(solution)/shard_map/ppermute | solution.py:52
  85.2 6.3 %collective-permute-start.12 = (bf16[16,2432]{1,0:T(8,128)(2,1)S(1)}, bf16[16,2432]{1,0:T(8,128)(2,1)S(1)}, u32[]{:S(2)}, u32[]{:S(2)}) collective-permute-start(bf16[16,2432]{1,0:T(8,128)(2,1)S(1)} %pad_maximum_fusion.11), channel_id=1, source_target_pairs={{0,16},{1,17},{2,18},{3,19},{4,20},{5,21},{6,22},{7,23},{8,24},{9,... | collective-permute-start | bytes 233480 | tf_op jit(solution)/shard_map/ppermute | solution.py:52
  85.6 7.0 %collective-permute-start.4 = (bf16[16,2432]{1,0:T(8,128)(2,1)S(1)}, bf16[16,2432]{1,0:T(8,128)(2,1)S(1)}, u32[]{:S(2)}, u32[]{:S(2)}) collective-permute-start(bf16[16,2432]{1,0:T(8,128)(2,1)S(1)} %pad_maximum_fusion.10), channel_id=1, source_target_pairs={{0,16},{1,17},{2,18},{3,19},{4,20},{5,21},{6,22},{7,23},{8,24},{9,... | collective-permute-start | bytes 233480 | tf_op jit(solution)/shard_map/ppermute | solution.py:52
  88.2 5.5 %collective-permute-start.21 = (bf16[16,2432]{1,0:T(8,128)(2,1)S(1)}, bf16[16,2432]{1,0:T(8,128)(2,1)S(1)}, u32[]{:S(2)}, u32[]{:S(2)}) collective-permute-start(bf16[16,2432]{1,0:T(8,128)(2,1)S(1)} %add_convert_fusion.16), channel_id=1, source_target_pairs={{0,8},{1,9},{2,10},{3,11},{4,12},{5,13},{6,14},{7,15},{8,0},{9,1},... | collective-permute-start | bytes 233480 | tf_op jit(solution)/shard_map/ppermute | solution.py:52
  93.8 6.2 %collective-permute-start.22 = (bf16[32,2432]{1,0:T(8,128)(2,1)S(1)}, bf16[32,2432]{1,0:T(8,128)(2,1)S(1)}, u32[]{:S(2)}, u32[]{:S(2)}) collective-permute-start(bf16[32,2432]{1,0:T(8,128)(2,1)S(1)} %pad_maximum_fusion.8), channel_id=1, source_target_pairs={{0,4},{1,3},{2,6},{3,1},{4,0},{5,7},{6,2},{7,5},{8,12},{9,11},{10,... | collective-permute-start | bytes 466952 | tf_op jit(solution)/shard_map/ppermute | solution.py:52
  96.0 7.3 %collective-permute-start.14 = (bf16[32,2432]{1,0:T(8,128)(2,1)S(1)}, bf16[32,2432]{1,0:T(8,128)(2,1)S(1)}, u32[]{:S(2)}, u32[]{:S(2)}) collective-permute-start(bf16[32,2432]{1,0:T(8,128)(2,1)S(1)} %pad_maximum_fusion.7), channel_id=1, source_target_pairs={{0,4},{1,3},{2,6},{3,1},{4,0},{5,7},{6,2},{7,5},{8,12},{9,11},{10,... | collective-permute-start | bytes 466952 | tf_op jit(solution)/shard_map/ppermute | solution.py:52
  97.4 9.2 %collective-permute-start.6 = (bf16[32,2432]{1,0:T(8,128)(2,1)S(1)}, bf16[32,2432]{1,0:T(8,128)(2,1)S(1)}, u32[]{:S(2)}, u32[]{:S(2)}) collective-permute-start(bf16[32,2432]{1,0:T(8,128)(2,1)S(1)} %pad_maximum_fusion.6), channel_id=1, source_target_pairs={{0,4},{1,3},{2,6},{3,1},{4,0},{5,7},{6,2},{7,5},{8,12},{9,11},{10,... | collective-permute-start | bytes 466952 | tf_op jit(solution)/shard_map/ppermute | solution.py:52
  100.0 7.8 %collective-permute-start.23 = (bf16[64,2432]{1,0:T(8,128)(2,1)S(1)}, bf16[64,2432]{1,0:T(8,128)(2,1)S(1)}, u32[]{:S(2)}, u32[]{:S(2)}) collective-permute-start(bf16[64,2432]{1,0:T(8,128)(2,1)S(1)} %pad_maximum_fusion.5), channel_id=1, source_target_pairs={{0,2},{1,5},{2,0},{3,7},{4,6},{5,1},{6,4},{7,3},{8,10},{9,13},{10,... | collective-permute-start | bytes 933896 | tf_op jit(solution)/shard_map/ppermute | solution.py:52
  103.3 7.0 %collective-permute-start.15 = (bf16[64,2432]{1,0:T(8,128)(2,1)S(1)}, bf16[64,2432]{1,0:T(8,128)(2,1)S(1)}, u32[]{:S(2)}, u32[]{:S(2)}) collective-permute-start(bf16[64,2432]{1,0:T(8,128)(2,1)S(1)} %pad_maximum_fusion.4), channel_id=1, source_target_pairs={{0,2},{1,5},{2,0},{3,7},{4,6},{5,1},{6,4},{7,3},{8,10},{9,13},{10,... | collective-permute-start | bytes 933896 | tf_op jit(solution)/shard_map/ppermute | solution.py:52
  106.6 7.0 %collective-permute-start.7 = (bf16[64,2432]{1,0:T(8,128)(2,1)S(1)}, bf16[64,2432]{1,0:T(8,128)(2,1)S(1)}, u32[]{:S(2)}, u32[]{:S(2)}) collective-permute-start(bf16[64,2432]{1,0:T(8,128)(2,1)S(1)} %pad_maximum_fusion.3), channel_id=1, source_target_pairs={{0,2},{1,5},{2,0},{3,7},{4,6},{5,1},{6,4},{7,3},{8,10},{9,13},{10,... | collective-permute-start | bytes 933896 | tf_op jit(solution)/shard_map/ppermute | solution.py:52
  108.3 6.3 %collective-permute-start.26 = (bf16[128,2432]{1,0:T(8,128)(2,1)S(1)}, bf16[128,2432]{1,0:T(8,128)(2,1)S(1)}, u32[]{:S(2)}, u32[]{:S(2)}) collective-permute-start(bf16[128,2432]{1,0:T(8,128)(2,1)S(1)} %pad_maximum_fusion.2), channel_id=1, source_target_pairs={{0,1},{1,0},{2,3},{3,2},{4,5},{5,4},{6,7},{7,6},{8,9},{9,8},{10,11... | collective-permute-start | bytes 1867784 | tf_op jit(solution)/shard_map/ppermute | solution.py:52
  110.5 7.3 %collective-permute-start.25 = (bf16[128,2432]{1,0:T(8,128)(2,1)S(1)}, bf16[128,2432]{1,0:T(8,128)(2,1)S(1)}, u32[]{:S(2)}, u32[]{:S(2)}) collective-permute-start(bf16[128,2432]{1,0:T(8,128)(2,1)S(1)} %get-tuple-element.8), channel_id=1, source_target_pairs={{0,1},{1,0},{2,3},{3,2},{4,5},{5,4},{6,7},{7,6},{8,9},{9,8},{10,11... | collective-permute-start | bytes 1867784 | tf_op jit(solution)/shard_map/ppermute | solution.py:52
  122.1 6.8 %collective-permute-start.38 = (bf16[64,2304]{1,0:T(8,128)(2,1)S(1)}, bf16[64,2304]{1,0:T(8,128)(2,1)S(1)}, u32[]{:S(2)}, u32[]{:S(2)}) collective-permute-start(bf16[64,2304]{1,0:T(8,128)(2,1)S(1)} %get-tuple-element.20), channel_id=1, source_target_pairs={{0,2},{1,5},{2,0},{3,7},{4,6},{5,1},{6,4},{7,3},{8,10},{9,13},{10,... | collective-permute-start | bytes 884744 | tf_op jit(solution)/shard_map/ppermute | solution.py:52
  124.2 9.2 %collective-permute-start.33 = (bf16[64,2432]{1,0:T(8,128)(2,1)S(1)}, bf16[64,2432]{1,0:T(8,128)(2,1)S(1)}, u32[]{:S(2)}, u32[]{:S(2)}) collective-permute-start(bf16[64,2432]{1,0:T(8,128)(2,1)S(1)} %get-tuple-element.14), channel_id=1, source_target_pairs={{0,2},{1,5},{2,0},{3,7},{4,6},{5,1},{6,4},{7,3},{8,10},{9,13},{10,... | collective-permute-start | bytes 933896 | tf_op jit(solution)/shard_map/ppermute | solution.py:52
  125.5 13.4 %collective-permute-start.28 = (bf16[64,2432]{1,0:T(8,128)(2,1)S(1)}, bf16[64,2432]{1,0:T(8,128)(2,1)S(1)}, u32[]{:S(2)}, u32[]{:S(2)}) collective-permute-start(bf16[64,2432]{1,0:T(8,128)(2,1)S(1)} %get-tuple-element.12), channel_id=1, source_target_pairs={{0,2},{1,5},{2,0},{3,7},{4,6},{5,1},{6,4},{7,3},{8,10},{9,13},{10,... | collective-permute-start | bytes 933896 | tf_op jit(solution)/shard_map/ppermute | solution.py:52
  129.0 11.0 %collective-permute-start.39 = (bf16[32,2304]{1,0:T(8,128)(2,1)S(1)}, bf16[32,2304]{1,0:T(8,128)(2,1)S(1)}, u32[]{:S(2)}, u32[]{:S(2)}) collective-permute-start(bf16[32,2304]{1,0:T(8,128)(2,1)S(1)} %get-tuple-element.32), channel_id=1, source_target_pairs={{0,4},{1,3},{2,6},{3,1},{4,0},{5,7},{6,2},{7,5},{8,12},{9,11},{10,... | collective-permute-start | bytes 442376 | tf_op jit(solution)/shard_map/ppermute | solution.py:52
  133.5 6.7 %collective-permute-start.34 = (bf16[32,2432]{1,0:T(8,128)(2,1)S(1)}, bf16[32,2432]{1,0:T(8,128)(2,1)S(1)}, u32[]{:S(2)}, u32[]{:S(2)}) collective-permute-start(bf16[32,2432]{1,0:T(8,128)(2,1)S(1)} %get-tuple-element.26), channel_id=1, source_target_pairs={{0,4},{1,3},{2,6},{3,1},{4,0},{5,7},{6,2},{7,5},{8,12},{9,11},{10,... | collective-permute-start | bytes 466952 | tf_op jit(solution)/shard_map/ppermute | solution.py:52
  138.9 6.4 %collective-permute-start.29 = (bf16[32,2432]{1,0:T(8,128)(2,1)S(1)}, bf16[32,2432]{1,0:T(8,128)(2,1)S(1)}, u32[]{:S(2)}, u32[]{:S(2)}) collective-permute-start(bf16[32,2432]{1,0:T(8,128)(2,1)S(1)} %get-tuple-element.24), channel_id=1, source_target_pairs={{0,4},{1,3},{2,6},{3,1},{4,0},{5,7},{6,2},{7,5},{8,12},{9,11},{10,... | collective-permute-start | bytes 466952 | tf_op jit(solution)/shard_map/ppermute | solution.py:52
  140.1 5.2 %collective-permute-start.40 = (bf16[16,2304]{1,0:T(8,128)(2,1)S(1)}, bf16[16,2304]{1,0:T(8,128)(2,1)S(1)}, u32[]{:S(2)}, u32[]{:S(2)}) collective-permute-start(bf16[16,2304]{1,0:T(8,128)(2,1)S(1)} %get-tuple-element.44), channel_id=1, source_target_pairs={{0,8},{1,9},{2,10},{3,11},{4,12},{5,13},{6,14},{7,15},{8,0},{9,1},... | collective-permute-start | bytes 221192 | tf_op jit(solution)/shard_map/ppermute | solution.py:52
  140.3 10.4 %collective-permute-start.35 = (bf16[16,2432]{1,0:T(8,128)(2,1)S(1)}, bf16[16,2432]{1,0:T(8,128)(2,1)S(1)}, u32[]{:S(2)}, u32[]{:S(2)}) collective-permute-start(bf16[16,2432]{1,0:T(8,128)(2,1)S(1)} %get-tuple-element.38), channel_id=1, source_target_pairs={{0,8},{1,9},{2,10},{3,11},{4,12},{5,13},{6,14},{7,15},{8,0},{9,1},... | collective-permute-start | bytes 233480 | tf_op jit(solution)/shard_map/ppermute | solution.py:52
  145.3 5.4 %collective-permute-start.41 = (bf16[8,2304]{1,0:T(8,128)(2,1)S(1)}, bf16[8,2304]{1,0:T(8,128)(2,1)S(1)}, u32[]{:S(2)}, u32[]{:S(2)}) collective-permute-start(bf16[8,2304]{1,0:T(8,128)(2,1)S(1)} %add_convert_fusion.36), channel_id=1, source_target_pairs={{0,16},{1,17},{2,18},{3,19},{4,20},{5,21},{6,22},{7,23},{8,24},{9,... | collective-permute-start | bytes 110600 | tf_op jit(solution)/shard_map/ppermute | solution.py:52
  145.4 5.5 %collective-permute-start.30 = (bf16[16,2432]{1,0:T(8,128)(2,1)S(1)}, bf16[16,2432]{1,0:T(8,128)(2,1)S(1)}, u32[]{:S(2)}, u32[]{:S(2)}) collective-permute-start(bf16[16,2432]{1,0:T(8,128)(2,1)S(1)} %get-tuple-element.36), channel_id=1, source_target_pairs={{0,8},{1,9},{2,10},{3,11},{4,12},{5,13},{6,14},{7,15},{8,0},{9,1},... | collective-permute-start | bytes 233480 | tf_op jit(solution)/shard_map/ppermute | solution.py:52
  (22 other events, 109.8 us)

commit v3 on v2

--- a/solution.py
+++ b/solution.py
@@ -1,11 +1,21 @@
+import functools
+
 import jax
 import jax.numpy as jnp
+import numpy as np
 from jax import lax
+from jax.experimental import pallas as pl
+from jax.experimental.pallas import tpu as pltpu
 from jax.sharding import PartitionSpec as P
 
 SHARDS = 8
 LANES = 128
 TILE = 128
+CHAINS = 3
+COLUMNS = 640
+ATTEND_VMEM = 56 << 20
+PROJECT_VMEM = 32 << 20
+FETCH_VMEM = 56 << 20
 
 
 score_scale = 192.0 ** (-0.5)
@@ -29,22 +39,20 @@
     return list(zip(low, high, strict=True))
 
 
-def chain_plans(nbits, width):
-    stages = stage_bits(nbits)
+def chain_parts(width):
     tiles = width // TILE
-    plans, start = [], 0
-    for order, share in (((1, 2, 3), 19), ((1, 2, 3), 19), ((1, 2, 3), 18)):
-        order = [*order, *range(4, nbits - 1)]
-        size = tiles * share // 56 * TILE
-        plans.append((start, size, order, [stages[0], *[stages[k] for k in order], stages[-1]]))
-        start += size
-    return plans
-
-
-def reorder(rows, old, new):
-    shape = rows.shape
-    axes = [*[old.index(k) for k in new], len(old), len(old) + 1]
-    return rows.reshape(*(2,) * len(old), -1, shape[1]).transpose(axes).reshape(shape)
+    sizes = [(tiles + i) // CHAINS * TILE for i in range(CHAINS)][::-1]
+    return [(sum(sizes[:i]), size) for i, size in enumerate(sizes)]
+
+
+def chain_orders(nbits):
+    plain = list(range(1, nbits - 1))
+    return [plain] * (CHAINS - 1) + [[3, 1, 2, *plain[3:]]]
+
+
+def place_rows(order, rows):
+    index = np.arange(rows).reshape(*(2,) * (len(order) + 1), -1)
+    return index.transpose(0, *order, len(order) + 1).reshape(-1)
 
 
 def swap(x, stage, devices):
@@ -95,24 +103,107 @@
     return parts
 
 
+def attend_kernel(lengths_ref, latent_ref, rope_ref, keys_ref, turned_ref, out_ref, held_ref):
+    token = pl.program_id(0)
+    keys = keys_ref[0]
+    scores = lax.dot_general(
+        latent_ref[0], keys, (((1,), (1,)), ((), ())), preferred_element_type=f32
+    )
+    scores = scores + jnp.dot(rope_ref[0], turned_ref[0], preferred_element_type=f32)
+    scores = scores * score_scale
+    column = lax.broadcasted_iota(jnp.int32, scores.shape, 1)
+    scores = jnp.where(column < lengths_ref[token], scores, -jnp.inf)
+    expd = jnp.exp(scores - jnp.max(scores, axis=1, keepdims=True))
+    weights = (expd / jnp.sum(expd, axis=1, keepdims=True)).astype(bf16)
+    held_ref[token] = jnp.dot(weights, keys, preferred_element_type=f32)
+
+    @pl.when(token == pl.num_programs(0) - 1)
+    def _():
+        out_ref[...] = jnp.swapaxes(held_ref[...], 0, 1).astype(bf16)
+
+
 def attend(q_latent, q_rope, cache_latent, cache_rope, lengths):
-    tokens_here, heads_all, _ = q_latent.shape
-    rope_width = cache_rope.shape[1]
-    cache_rows = cache_latent.shape[1]
-    scores = jnp.einsum("thk,tlk->thl", q_latent, cache_latent, preferred_element_type=f32)
-    scores = scores + jnp.einsum(
-        "thr,trl->thl",
-        q_rope.reshape(tokens_here, heads_all, rope_width),
-        cache_rope,
-        preferred_element_type=f32,
-    )
-    scores = scores * score_scale
-    usable = jnp.arange(cache_rows, dtype=jnp.int32)[None, :] < lengths[:, None]
-    scores = jnp.where(usable[:, None, :], scores, -jnp.inf)
-    highest = jnp.max(scores, axis=2, keepdims=True)
-    expd = jnp.exp(scores - highest)
-    weights = (expd / jnp.sum(expd, axis=2, keepdims=True)).astype(bf16)
-    return jnp.einsum("thl,tlk->thk", weights, cache_latent, preferred_element_type=f32).astype(bf16)
+    tokens, heads, rank = q_latent.shape
+    _, turned, cached = cache_rope.shape
+    at = lambda i: (i, 0, 0)
+    return pl.pallas_call(
+        attend_kernel,
+        grid=(tokens,),
+        out_shape=jax.ShapeDtypeStruct((heads, tokens, rank), bf16),
+        in_specs=[
+            pl.BlockSpec(memory_space=pltpu.SMEM),
+            pl.BlockSpec((1, heads, rank), at),
+            pl.BlockSpec((1, heads, turned), at),
+            pl.BlockSpec((1, cached, rank), at),
+            pl.BlockSpec((1, turned, cached), at),
+        ],
+        out_specs=pl.BlockSpec((heads, tokens, rank), lambda i: (0, 0, 0)),
+        scratch_shapes=[pltpu.VMEM((tokens, heads, rank), f32)],
+        compiler_params=pltpu.CompilerParams(vmem_limit_bytes=ATTEND_VMEM),
+        cost_estimate=pl.CostEstimate(
+            flops=2 * tokens * heads * cached * (2 * rank + turned),
+            bytes_accessed=2 * tokens * (2 * heads * rank + cached * (rank + turned)),
+            transcendentals=tokens * heads * cached,
+        ),
+    )(lengths, q_latent, q_rope.reshape(tokens, heads, turned), cache_latent, cache_rope)
+
+
+def fetch_kernel(after_ref, gate_ref, up_ref, down_ref, both_held, down_held, done):
+    width = gate_ref.shape[2]
+    copies = [
+        pltpu.make_async_copy(gate_ref.at[0], both_held.at[:, :width], done.at[0]),
+        pltpu.make_async_copy(up_ref.at[0], both_held.at[:, width:], done.at[1]),
+        pltpu.make_async_copy(down_ref.at[0], down_held, done.at[2]),
+    ]
+    for copy in copies:
+        copy.start()
+    for copy in copies:
+        copy.wait()
+
+
+def fetch(after, gate_weight, up_weight, down_projection_weight):
+    _, model_width, width = gate_weight.shape
+    shapes = [(model_width, 2 * width), (width, model_width)]
+    size = sum(2 * a * b for a, b in shapes)
+    return pl.pallas_call(
+        fetch_kernel,
+        out_shape=[jax.ShapeDtypeStruct(shape, bf16) for shape in shapes],
+        in_specs=[pl.BlockSpec(memory_space=pl.ANY)] * 4,
+        out_specs=[pl.BlockSpec(memory_space=pltpu.VMEM)] * 2,
+        scratch_shapes=[pltpu.SemaphoreType.DMA((3,))],
+        compiler_params=pltpu.CompilerParams(vmem_limit_bytes=FETCH_VMEM),
+        cost_estimate=pl.CostEstimate(flops=0, bytes_accessed=2 * size, transcendentals=0),
+    )(after, gate_weight, up_weight, down_projection_weight)
+
+
+def project_kernel(start, values_ref, weight_ref, keep_ref, send_ref):
+    half, size = keep_ref.shape
+    for at in range(0, size, COLUMNS):
+        width = min(COLUMNS, size - at)
+        out = jnp.dot(
+            values_ref[...],
+            weight_ref[:, start + at : start + at + width],
+            preferred_element_type=f32,
+        ).astype(bf16)
+        keep_ref[:, at : at + width] = out[:half]
+        send_ref[:, at : at + width] = out[half:]
+
+
+def project(values, weight, start, size):
+    rows, depth = values.shape
+    half = jax.ShapeDtypeStruct((rows // 2, size), bf16)
+    return pl.pallas_call(
+        functools.partial(project_kernel, start),
+        out_shape=[half, half],
+        in_specs=[pl.BlockSpec(memory_space=pltpu.VMEM)] * 2,
+        out_specs=[pl.BlockSpec(memory_space=pltpu.VMEM)] * 2,
+        compiler_params=pltpu.CompilerParams(vmem_limit_bytes=PROJECT_VMEM),
+        cost_estimate=pl.CostEstimate(
+            flops=2 * rows * depth * size,
+            bytes_accessed=2 * (rows * depth + depth * size + rows * size),
+            transcendentals=0,
+        ),
+    )(values, weight)
 
 
 def shards(
@@ -138,19 +229,38 @@
     model_width = hidden_in.shape[1]
     top_count = route_ids.shape[1]
     experts = devices // SHARDS
-    plans = chain_plans(nbits, model_width)
-    base_order = plans[0][2]
+    stages = stage_bits(nbits)
+    plans = chain_parts(model_width)
+    orders = chain_orders(nbits)
+    sum_stages = [[stages[0], *[stages[k] for k in order], stages[-1]] for order in orders]
     sigm = jax.nn.sigmoid(route_logits)
     route_weights = route_scale * sigm / jnp.sum(sigm, axis=1, keepdims=True)
 
     latent_out = attend(q_latent, q_rope, cache_latent, cache_rope, lengths)
-    by_head = lax.all_to_all(latent_out, "expert", split_axis=1, concat_axis=0, tiled=True)
+    both_near, down_near = fetch(latent_out, gate_weight, up_weight, down_projection_weight)
+    _, out_after = lax.optimization_barrier((latent_out, out_weight))
+    out_near = [out_after[:, start : start + size] for start, size in plans]
+    value_up_weight, both_near, down_near, *out_near = lax.optimization_barrier(
+        (value_up_weight, both_near, down_near, *out_near)
+    )
+    by_head = lax.all_to_all(latent_out, "expert", split_axis=0, concat_axis=0, tiled=True)
+    heads_here = value_up_weight.shape[0]
+    by_head = by_head.reshape(devices, heads_here, tokens_here, -1)
     head_values = jnp.einsum(
-        "aqg,qge->aqe", by_head, value_up_weight, preferred_element_type=f32
+        "sqtg,qge->stqe", by_head, value_up_weight, preferred_element_type=f32
     ).astype(bf16)
     rows = devices * tokens_here
-    half = rows // 2
     head_values = head_values.reshape(rows, -1)
+    at = jnp.arange(rows, dtype=jnp.int32)
+    values = {}
+    for order, its in zip(orders, sum_stages, strict=True):
+        if tuple(order) not in values:
+            source = row_sources(me, its, devices, tokens_here)
+            shuffle = (source[:, None] == at[None, :]).astype(bf16)
+            values[tuple(order)] = jnp.dot(
+                shuffle, head_values, preferred_element_type=f32
+            ).astype(bf16)
+
     chosen = route_ids[:, :, None] == jnp.arange(experts, dtype=jnp.int32)[None, None, :]
     shares = jnp.sum(jnp.where(chosen, route_weights[:, :, None], 0.0), axis=1)
     extra = jnp.concatenate(three_parts(shares), axis=1)
@@ -158,14 +268,9 @@
     dense = experts <= top_count
 
     residual = []
-    for i, (start, size, _, stages) in enumerate(plans):
-        source = row_sources(me, stages, devices, tokens_here)
-        shuffle = (source[:, None] == jnp.arange(rows, dtype=jnp.int32)[None, :]).astype(bf16)
-        values = jnp.dot(shuffle, head_values, preferred_element_type=f32).astype(bf16)
-        weight = out_weight[:, start : start + size]
-        send = jnp.dot(values[half:], weight, preferred_element_type=f32).astype(bf16)
-        keep = jnp.dot(values[:half], weight, preferred_element_type=f32)
-        own, partners = halve(keep, send, stages, devices)
+    for i, (start, size) in enumerate(plans):
+        keep, send = project(values[tuple(orders[i])], out_near[i], 0, size)
+        own, partners = halve(keep, send, sum_stages[i], devices)
         own = (own + hidden_in[:, start : start + size].astype(f32)).astype(bf16)
         both = jnp.concatenate([own, partners], axis=0)
         if dense and i + 1 == len(plans):
@@ -186,34 +291,19 @@
             down_projection_weight,
         )
 
-    gate_act, up_act, squares = [0.0, 0.0], [0.0, 0.0], [0.0, 0.0]
-    got = [None, None]
-    for i, (start, size, order, stages) in enumerate(plans):
+    acts, squares, got = [0.0, 0.0], [0.0, 0.0], [None, None]
+    for i, (start, size) in enumerate(plans):
         gain = norm_gain[start : start + size].astype(f32)
         for h, taken in enumerate(double(residual[i], stages[:-1], devices)):
             if i + 1 == len(plans):
-                got[h] = reorder(taken[:, size:].astype(f32), order, base_order)
+                got[h] = taken[:, size:].astype(f32)
                 taken = taken[:, :size]
             wide = taken.astype(f32)
-            parts = (
-                jnp.sum(wide * wide, axis=1, keepdims=True),
-                jnp.dot(
-                    (wide * gain).astype(bf16),
-                    gate_weight[0, start : start + size],
-                    preferred_element_type=f32,
-                ),
-                jnp.dot(
-                    (wide * gain).astype(bf16),
-                    up_weight[0, start : start + size],
-                    preferred_element_type=f32,
-                ),
-            )
-            if order != base_order:
-                parts = tuple(reorder(p, order, base_order) for p in parts)
-            squares[h], gate_act[h], up_act[h] = (
-                squares[h] + parts[0],
-                gate_act[h] + parts[1],
-                up_act[h] + parts[2],
+            squares[h] = squares[h] + jnp.sum(wide * wide, axis=1, keepdims=True)
+            acts[h] = acts[h] + jnp.dot(
+                (wide * gain).astype(bf16),
+                both_near[start : start + size],
+                preferred_element_type=f32,
             )
     lane = jnp.arange(LANES, dtype=jnp.int32)
     own = (lane % experts == me // SHARDS) & (lane < 3 * experts)
@@ -221,16 +311,17 @@
     for h in range(2):
         factor = lax.rsqrt(squares[h] / model_width + epsilon)
         share = jnp.sum(jnp.where(own[None, :], got[h], 0.0), axis=1, keepdims=True)
-        hidden.append(
-            (jax.nn.silu(gate_act[h] * factor) * (up_act[h] * factor) * share).astype(bf16)
-        )
+        gate_act, up_act = jnp.split(acts[h] * factor, 2, axis=1)
+        hidden.append((jax.nn.silu(gate_act) * up_act * share).astype(bf16))
+    hidden = jnp.concatenate(hidden, axis=0)
     out = []
-    for (start, size, order, stages), base in zip(plans, residual, strict=True):
-        weight = down_projection_weight[0, :, start : start + size]
-        acts = [reorder(x, base_order, order) for x in hidden] if order != base_order else hidden
-        send = jnp.dot(acts[1], weight, preferred_element_type=f32).astype(bf16)
-        keep = jnp.dot(acts[0], weight, preferred_element_type=f32)
-        own, partners = halve(keep, send, stages, devices)
+    for i, ((start, size), base) in enumerate(zip(plans, residual, strict=True)):
+        acts = hidden
+        if orders[i] != orders[0]:
+            move = np.eye(rows, dtype=np.float32)[place_rows(orders[i], rows)]
+            acts = jnp.dot(jnp.asarray(move, bf16), hidden, preferred_element_type=f32).astype(bf16)
+        keep, send = project(acts, down_near, start, size)
+        own, partners = halve(keep, send, sum_stages[i], devices)
         came = swap(partners, stages[-1], devices)
         total = base[:tokens_here, :size].astype(f32) + own + came.astype(f32)
         out.append(total.astype(bf16))

time: 157 us -> 146 us (0.930)
  waiting for transfers between devices: 75.4 us -> 53.3 us
  Pallas kernels: 0 us -> 18 us
  matrix products: 23.1 us -> 5.16 us
  starting transfers between devices: 46.4 us -> 52.7 us
  local copies, waits for them, and re-layouts: 6.04 us -> 11 us
    dot_general x28 -> x9, matrix products: 22.8 us -> 4.59 us  [the longest x1 2.16 us: shards(): jnp.einsum('sqtg,qge->stqe', by_head, value_up_weight, preferred_element_...]
    pallas_call x0 -> x8, Pallas kernels: none -> 18 us  [the longest x1 8.76 us: attend(): pl.pallas_call(attend_kernel, grid=(tokens,), out_shape=jax.ShapeDtypeStr...]
    all_to_all x1, waiting for transfers between devices: 25.7 us -> 13.3 us  [shards(): lax.all_to_all(latent_out, 'expert', split_axis=0, concat_axis=0, tiled=T...]
    ppermute x42, waiting for transfers between devices: 49.6 us -> 40 us  [swap(): return lax.ppermute(x, 'expert', pairs)]
    slice x0 -> x2, local copies, waits for them, and re-layouts: none -> 7.57 us  [shards(): out_near = [out_after[:, start:start + size] for start, size in plans]]
    ppermute x42, starting transfers between devices: 38.9 us -> 45.3 us  [swap(): return lax.ppermute(x, 'expert', pairs)]
    convert_element_type x1 -> x0, local copies, waits for them, and re-layouts: 2.78 us -> none  [attend(): jnp.einsum('thl,tlk->thk', weights, cache_latent, preferred_element_type=...]
  transfers between devices with their start and end apart: 43 -> 43, of which waited for: 26 -> 23; matrix products, arithmetic and copies ran while one was open for 5% -> 9% of each run, Pallas kernels for 0% -> 5%
where the time goes in v3:
time: 146 us; the launch traced here: 145 us
  waiting for transfers between devices  53.3 us (37%)
  starting transfers between devices  52.7 us (36%)
  Pallas kernels  18 us (12%)
  local copies, waits for them, and re-layouts  11 us (8%)
  matrix products  5.16 us (4%)
  other arithmetic  4.43 us (3%)
    ppermute x42, starting transfers between devices, swap(): return lax.ppermute(x, 'expert', pairs)  45.3 us
    ppermute x42, waiting for transfers between devices, swap(): return lax.ppermute(x, 'expert', pairs)  40 us
    all_to_all x1, waiting for transfers between devices, shards(): lax.all_to_all(latent_out, 'expert', split_axis=0, concat_axis=0, tiled=T...  13.3 us
    pallas_call x1, Pallas kernels, attend(): pl.pallas_call(attend_kernel, grid=(tokens,), out_shape=jax.ShapeDtypeStr...  8.76 us
    slice x2, local copies, waits for them, and re-layouts, shards(): out_near = [out_after[:, start:start + size] for start, size in plans]  7.57 us
    all_to_all x1, starting transfers between devices, shards(): lax.all_to_all(latent_out, 'expert', split_axis=0, concat_axis=0, tiled=T...  7.42 us
    pallas_call x1, Pallas kernels, fetch(): pl.pallas_call(fetch_kernel, out_shape=[jax.ShapeDtypeStruct(shape, bf16)...  5.05 us
    pallas_call x6, Pallas kernels, project(): pl.pallas_call(functools.partial(project_kernel, start), out_shape=[half,...  4.14 us
  transfers between devices with their start and end apart: 43, of which 23 were waited for; matrix products, arithmetic and copies ran while one was open for 9% of the time, Pallas kernels for 5%

profile of v3, /device:TPU:0, one launch (start us, length us, event | category | flops | bytes accessed | tf_op | source)
XLA Modules:
  0.0 145.1 jit_solution(13916354141426805931)
XLA Ops:
  0.0 2.0 %reshape.121.rope_ref = bf16[8,128,64]{2,1,0:T(8,128)(2,1)} reshape(bf16[8,8192]{1,0:T(8,128)(2,1)} %param.17) | data formatting | bytes 262144 | tf_op jit(solution)/shard_map/reshape | solution.py:148
  2.0 8.8 %shard_map.145.after_ref = bf16[128,8,512]{2,1,0:T(8,128)(2,1)} custom-call(s32[8]{0:T(128)} %lengths_ref.1, bf16[8,128,512]{2,1,0:T(8,128)(2,1)} %latent_ref.1, bf16[8,128,64]{2,1,0:T(8,128)(2,1)} %reshape.121.rope_ref, bf16[8,256,512]{2,1,0:T(8,128)(2,1)} %keys_ref.1, bf16[8,64,256]{2,1,0:T(8,128)(2,1)} %turned_ref.1), custom_call_target="tpu_custom_call" | custom-call | flops 570425344 | bytes 4456448 | tf_op jit(solution)/shard_map/pallas_call | solution.py:129
  10.7 7.4 %all-to-all-start = ((bf16[128,8,512]{2,1,0:T(8,128)(2,1)}), bf16[128,8,512]{2,1,0:T(8,128)(2,1)}, u32[]{:S(2)}, u32[]{:S(2)}) async-start(bf16[128,8,512]{2,1,0:T(8,128)(2,1)} %shard_map.145.after_ref), calls=%async_computation | async-start | bytes 2097152 | tf_op jit(solution)/shard_map/all_to_all | solution.py:246
  18.2 3.3 %slice.368.weight_ref = bf16[512,2304]{1,0:T(8,128)(2,1)} slice(bf16[512,7168]{1,0:T(8,128)(2,1)} %param.22), slice={[0:512], [4864:7168]} | slice | bytes 4718592 | tf_op jit(solution)/shard_map/slice | solution.py:242
  21.5 5.1 %shard_map.146 = (bf16[7168,256]{1,0:T(8,128)(2,1)}, bf16[128,7168]{1,0:T(8,128)(2,1)}) custom-call(bf16[128,8,512]{2,1,0:T(8,128)(2,1)} %shard_map.145.after_ref, bf16[1,7168,128]{2,1,0:T(8,128)(2,1)} %gate_ref.1, bf16[1,7168,128]{2,1,0:T(8,128)(2,1)} %up_ref.1, bf16[1,128,7168]{2,1,0:T(8,128)(2,1)} %down_ref.1), custom_call_target="tpu_custom_call" | custom-call | bytes 11010048 | tf_op jit(solution)/shard_map/pallas_call | solution.py:168
  26.6 4.3 %fusion.67 = (bf16[512,2432]{1,0:T(8,128)(2,1)}, bf16[512,2432]{1,0:T(8,128)(2,1)S(1)}) fusion(bf16[512,7168]{1,0:T(8,128)(2,1)} %param.22), kind=kLoop, calls=%fused_computation.178 | loop fusion | bytes 9961472 | tf_op jit(solution)/shard_map/slice | solution.py:242
  31.1 13.3 %all-to-all-done = bf16[128,8,512]{2,1,0:T(8,128)(2,1)} async-done(((bf16[128,8,512]{2,1,0:T(8,128)(2,1)}), bf16[128,8,512]{2,1,0:T(8,128)(2,1)}, u32[]{:S(2)}, u32[]{:S(2)}) %all-to-all-start) | async-done | bytes 1048608 | tf_op jit(solution)/shard_map/all_to_all | solution.py:246
  44.4 2.2 %fusion.12 = bf16[32,8,4,128]{3,0,1,2:T(8,128)(2,1)S(1)} fusion(bf16[32,4,8,512]{3,2,1,0:T(8,128)(2,1)} %bitcast.2, bf16[4,512,128]{2,1,0:T(8,128)(2,1)S(1)} %copy-done), kind=kOutput, calls=%fused_computation.27 | convolution fusion | flops 134348800 | bytes 1835008 | tf_op jit(solution)/shard_map/sqtg,qge->stqe/dot_general | solution.py:249
  54.5 5.8 %collective-permute-done.17 = bf16[64,2304]{1,0:T(8,128)(2,1)S(1)} collective-permute-done((bf16[64,2304]{1,0:T(8,128)(2,1)S(1)}, bf16[64,2304]{1,0:T(8,128)(2,1)S(1)}, u32[]{:S(2)}, u32[]{:S(2)}) %collective-permute-start.17) | collective-permute-done | bytes 294944 | tf_op jit(solution)/shard_map/ppermute | solution.py:60
  62.0 1.6 %collective-permute-start.10 = (bf16[32,2432]{1,0:T(8,128)(2,1)S(1)}, bf16[32,2432]{1,0:T(8,128)(2,1)S(1)}, u32[]{:S(2)}, u32[]{:S(2)}) collective-permute-start(bf16[32,2432]{1,0:T(8,128)(2,1)S(1)} %get-tuple-element.74), channel_id=1, source_target_pairs={{0,4},{1,3},{2,6},{3,1},{4,0},{5,7},{6,2},{7,5},{8,12},{9,11},{10,... | collective-permute-start | bytes 466952 | tf_op jit(solution)/shard_map/ppermute | solution.py:60
  64.2 2.9 %collective-permute-done.18 = bf16[32,2304]{1,0:T(8,128)(2,1)S(1)} collective-permute-done((bf16[32,2304]{1,0:T(8,128)(2,1)S(1)}, bf16[32,2304]{1,0:T(8,128)(2,1)S(1)}, u32[]{:S(2)}, u32[]{:S(2)}) %collective-permute-start.18) | collective-permute-done | bytes 147488 | tf_op jit(solution)/shard_map/ppermute | solution.py:60
  67.2 1.6 %collective-permute-start.19 = (bf16[16,2304]{1,0:T(8,128)(2,1)S(1)}, bf16[16,2304]{1,0:T(8,128)(2,1)S(1)}, u32[]{:S(2)}, u32[]{:S(2)}) collective-permute-start(bf16[16,2304]{1,0:T(8,128)(2,1)S(1)} %get-tuple-element.90), channel_id=1, source_target_pairs={{0,4},{1,3},{2,6},{3,1},{4,0},{5,7},{6,2},{7,5},{8,12},{9,11},{10,... | collective-permute-start | bytes 221192 | tf_op jit(solution)/shard_map/ppermute | solution.py:60
  69.4 1.6 %collective-permute-start.3 = (bf16[16,2432]{1,0:T(8,128)(2,1)S(1)}, bf16[16,2432]{1,0:T(8,128)(2,1)S(1)}, u32[]{:S(2)}, u32[]{:S(2)}) collective-permute-start(bf16[16,2432]{1,0:T(8,128)(2,1)S(1)} %get-tuple-element.84), channel_id=1, source_target_pairs={{0,8},{1,9},{2,10},{3,11},{4,12},{5,13},{6,14},{7,15},{8,0},{9,1},... | collective-permute-start | bytes 233480 | tf_op jit(solution)/shard_map/ppermute | solution.py:60
  76.0 2.0 %collective-permute-start.12 = (bf16[16,2432]{1,0:T(8,128)(2,1)S(1)}, bf16[16,2432]{1,0:T(8,128)(2,1)S(1)}, u32[]{:S(2)}, u32[]{:S(2)}) collective-permute-start(bf16[16,2432]{1,0:T(8,128)(2,1)S(1)} %pad_maximum_fusion.11), channel_id=1, source_target_pairs={{0,16},{1,17},{2,18},{3,19},{4,20},{5,21},{6,22},{7,23},{8,24},{9,... | collective-permute-start | bytes 233480 | tf_op jit(solution)/shard_map/ppermute | solution.py:60
  78.0 2.7 %collective-permute-done.20 = bf16[16,2432]{1,0:T(8,128)(2,1)S(1)} collective-permute-done((bf16[16,2432]{1,0:T(8,128)(2,1)S(1)}, bf16[16,2432]{1,0:T(8,128)(2,1)S(1)}, u32[]{:S(2)}, u32[]{:S(2)}) %collective-permute-start.20) | collective-permute-done | bytes 77856 | tf_op jit(solution)/shard_map/ppermute | solution.py:60
  80.8 2.4 %collective-permute-done.4 = bf16[16,2432]{1,0:T(8,128)(2,1)S(1)} collective-permute-done((bf16[16,2432]{1,0:T(8,128)(2,1)S(1)}, bf16[16,2432]{1,0:T(8,128)(2,1)S(1)}, u32[]{:S(2)}, u32[]{:S(2)}) %collective-permute-start.4) | collective-permute-done | bytes 77856 | tf_op jit(solution)/shard_map/ppermute | solution.py:60
  85.6 2.0 %collective-permute-start.22 = (bf16[32,2432]{1,0:T(8,128)(2,1)S(1)}, bf16[32,2432]{1,0:T(8,128)(2,1)S(1)}, u32[]{:S(2)}, u32[]{:S(2)}) collective-permute-start(bf16[32,2432]{1,0:T(8,128)(2,1)S(1)} %pad_maximum_fusion.8), channel_id=1, source_target_pairs={{0,4},{1,3},{2,6},{3,1},{4,0},{5,7},{6,2},{7,5},{8,12},{9,11},{10,... | collective-permute-start | bytes 466952 | tf_op jit(solution)/shard_map/ppermute | solution.py:60
  89.8 2.1 %collective-permute-done.22 = bf16[32,2432]{1,0:T(8,128)(2,1)S(1)} collective-permute-done((bf16[32,2432]{1,0:T(8,128)(2,1)S(1)}, bf16[32,2432]{1,0:T(8,128)(2,1)S(1)}, u32[]{:S(2)}, u32[]{:S(2)}) %collective-permute-start.22) | collective-permute-done | bytes 155680 | tf_op jit(solution)/shard_map/ppermute | solution.py:60
  92.0 2.7 %collective-permute-start.23 = (bf16[64,2432]{1,0:T(8,128)(2,1)S(1)}, bf16[64,2432]{1,0:T(8,128)(2,1)S(1)}, u32[]{:S(2)}, u32[]{:S(2)}) collective-permute-start(bf16[64,2432]{1,0:T(8,128)(2,1)S(1)} %pad_maximum_fusion.5), channel_id=1, source_target_pairs={{0,2},{1,5},{2,0},{3,7},{4,6},{5,1},{6,4},{7,3},{8,10},{9,13},{10,... | collective-permute-start | bytes 933896 | tf_op jit(solution)/shard_map/ppermute | solution.py:60
  95.3 2.7 %collective-permute-start.7 = (bf16[64,2432]{1,0:T(8,128)(2,1)S(1)}, bf16[64,2432]{1,0:T(8,128)(2,1)S(1)}, u32[]{:S(2)}, u32[]{:S(2)}) collective-permute-start(bf16[64,2432]{1,0:T(8,128)(2,1)S(1)} %pad_maximum_fusion.3), channel_id=1, source_target_pairs={{0,2},{1,5},{2,0},{3,7},{4,6},{5,1},{6,4},{7,3},{8,10},{9,13},{10,... | collective-permute-start | bytes 933896 | tf_op jit(solution)/shard_map/ppermute | solution.py:60
  98.6 2.7 %collective-permute-start.15 = (bf16[64,2432]{1,0:T(8,128)(2,1)S(1)}, bf16[64,2432]{1,0:T(8,128)(2,1)S(1)}, u32[]{:S(2)}, u32[]{:S(2)}) collective-permute-start(bf16[64,2432]{1,0:T(8,128)(2,1)S(1)} %pad_maximum_fusion.4), channel_id=1, source_target_pairs={{0,2},{1,5},{2,0},{3,7},{4,6},{5,1},{6,4},{7,3},{8,10},{9,13},{10,... | collective-permute-start | bytes 933896 | tf_op jit(solution)/shard_map/ppermute | solution.py:60
  103.2 3.1 %collective-permute-done.15 = bf16[64,2432]{1,0:T(8,128)(2,1)S(1)} collective-permute-done((bf16[64,2432]{1,0:T(8,128)(2,1)S(1)}, bf16[64,2432]{1,0:T(8,128)(2,1)S(1)}, u32[]{:S(2)}, u32[]{:S(2)}) %collective-permute-start.15) | collective-permute-done | bytes 311328 | tf_op jit(solution)/shard_map/ppermute | solution.py:60
  114.4 2.1 %collective-permute-start.28 = (bf16[64,2432]{1,0:T(8,128)(2,1)S(1)}, bf16[64,2432]{1,0:T(8,128)(2,1)S(1)}, u32[]{:S(2)}, u32[]{:S(2)}) collective-permute-start(bf16[64,2432]{1,0:T(8,128)(2,1)S(1)} %get-tuple-element.56), channel_id=1, source_target_pairs={{0,2},{1,5},{2,0},{3,7},{4,6},{5,1},{6,4},{7,3},{8,10},{9,13},{10,... | collective-permute-start | bytes 933896 | tf_op jit(solution)/shard_map/ppermute | solution.py:60
  117.4 5.4 %collective-permute-done.38 = bf16[64,2304]{1,0:T(8,128)(2,1)S(1)} collective-permute-done((bf16[64,2304]{1,0:T(8,128)(2,1)S(1)}, bf16[64,2304]{1,0:T(8,128)(2,1)S(1)}, u32[]{:S(2)}, u32[]{:S(2)}) %collective-permute-start.38) | collective-permute-done | bytes 294944 | tf_op jit(solution)/shard_map/ppermute | solution.py:60
  122.9 2.1 %collective-permute-start.39 = (bf16[32,2304]{1,0:T(8,128)(2,1)S(1)}, bf16[32,2304]{1,0:T(8,128)(2,1)S(1)}, u32[]{:S(2)}, u32[]{:S(2)}) collective-permute-start(bf16[32,2304]{1,0:T(8,128)(2,1)S(1)} %get-tuple-element.76), channel_id=1, source_target_pairs={{0,2},{1,5},{2,0},{3,7},{4,6},{5,1},{6,4},{7,3},{8,10},{9,13},{10,... | collective-permute-start | bytes 442376 | tf_op jit(solution)/shard_map/ppermute | solution.py:60
  127.3 2.1 %collective-permute-done.39 = bf16[32,2304]{1,0:T(8,128)(2,1)S(1)} collective-permute-done((bf16[32,2304]{1,0:T(8,128)(2,1)S(1)}, bf16[32,2304]{1,0:T(8,128)(2,1)S(1)}, u32[]{:S(2)}, u32[]{:S(2)}) %collective-permute-start.39) | collective-permute-done | bytes 147488 | tf_op jit(solution)/shard_map/ppermute | solution.py:60
  129.4 2.2 %collective-permute-start.40 = (bf16[16,2304]{1,0:T(8,128)(2,1)S(1)}, bf16[16,2304]{1,0:T(8,128)(2,1)S(1)}, u32[]{:S(2)}, u32[]{:S(2)}) collective-permute-start(bf16[16,2304]{1,0:T(8,128)(2,1)S(1)} %get-tuple-element.88), channel_id=1, source_target_pairs={{0,4},{1,3},{2,6},{3,1},{4,0},{5,7},{6,2},{7,5},{8,12},{9,11},{10,... | collective-permute-start | bytes 221192 | tf_op jit(solution)/shard_map/ppermute | solution.py:60
  131.9 2.0 %collective-permute-done.40 = bf16[16,2304]{1,0:T(8,128)(2,1)S(1)} collective-permute-done((bf16[16,2304]{1,0:T(8,128)(2,1)S(1)}, bf16[16,2304]{1,0:T(8,128)(2,1)S(1)}, u32[]{:S(2)}, u32[]{:S(2)}) %collective-permute-start.40) | collective-permute-done | bytes 73760 | tf_op jit(solution)/shard_map/ppermute | solution.py:60
  134.1 1.9 %collective-permute-start.35 = (bf16[16,2432]{1,0:T(8,128)(2,1)S(1)}, bf16[16,2432]{1,0:T(8,128)(2,1)S(1)}, u32[]{:S(2)}, u32[]{:S(2)}) collective-permute-start(bf16[16,2432]{1,0:T(8,128)(2,1)S(1)} %get-tuple-element.82), channel_id=1, source_target_pairs={{0,8},{1,9},{2,10},{3,11},{4,12},{5,13},{6,14},{7,15},{8,0},{9,1},... | collective-permute-start | bytes 233480 | tf_op jit(solution)/shard_map/ppermute | solution.py:60
  135.9 3.0 %collective-permute-done.41 = bf16[8,2304]{1,0:T(8,128)(2,1)S(1)} collective-permute-done((bf16[8,2304]{1,0:T(8,128)(2,1)S(1)}, bf16[8,2304]{1,0:T(8,128)(2,1)S(1)}, u32[]{:S(2)}, u32[]{:S(2)}) %collective-permute-start.41) | collective-permute-done | bytes 36896 | tf_op jit(solution)/shard_map/ppermute | solution.py:60
  139.1 3.0 %collective-permute-start.36 = (bf16[8,2432]{1,0:T(8,128)(2,1)S(1)}, bf16[8,2432]{1,0:T(8,128)(2,1)S(1)}, u32[]{:S(2)}, u32[]{:S(2)}) collective-permute-start(bf16[8,2432]{1,0:T(8,128)(2,1)S(1)} %add_convert_fusion.40), channel_id=1, source_target_pairs={{0,16},{1,17},{2,18},{3,19},{4,20},{5,21},{6,22},{7,23},{8,24},{9,... | collective-permute-start | bytes 116744 | tf_op jit(solution)/shard_map/ppermute | solution.py:60
  142.1 1.9 %collective-permute-done.31 = bf16[8,2432]{1,0:T(8,128)(2,1)S(1)} collective-permute-done((bf16[8,2432]{1,0:T(8,128)(2,1)S(1)}, bf16[8,2432]{1,0:T(8,128)(2,1)S(1)}, u32[]{:S(2)}, u32[]{:S(2)}) %collective-permute-start.31) | collective-permute-done | bytes 38944 | tf_op jit(solution)/shard_map/ppermute | solution.py:60
  (163 shorter events, 36.9 us)
Async XLA Ops:
  10.7 33.6 %all-to-all-start = ((bf16[128,8,512]{2,1,0:T(8,128)(2,1)}), bf16[128,8,512]{2,1,0:T(8,128)(2,1)}, u32[]{:S(2)}, u32[]{:S(2)}) async-start(bf16[128,8,512]{2,1,0:T(8,128)(2,1)} %shard_map.145.after_ref), calls=%async_computation | async-start | bytes 2097152 | tf_op jit(solution)/shard_map/all_to_all | solution.py:246
  51.2 9.1 %collective-permute-start.17 = (bf16[64,2304]{1,0:T(8,128)(2,1)S(1)}, bf16[64,2304]{1,0:T(8,128)(2,1)S(1)}, u32[]{:S(2)}, u32[]{:S(2)}) collective-permute-start(bf16[64,2304]{1,0:T(8,128)(2,1)S(1)} %get-tuple-element.66), channel_id=1, source_target_pairs={{0,8},{1,9},{2,10},{3,11},{4,12},{5,13},{6,14},{7,15},{8,0},{9,1},... | collective-permute-start | bytes 884744 | tf_op jit(solution)/shard_map/ppermute | solution.py:60
  52.1 9.7 %collective-permute-start.9 = (bf16[64,2432]{1,0:T(8,128)(2,1)S(1)}, bf16[64,2432]{1,0:T(8,128)(2,1)S(1)}, u32[]{:S(2)}, u32[]{:S(2)}) collective-permute-start(bf16[64,2432]{1,0:T(8,128)(2,1)S(1)} %get-tuple-element.62), channel_id=1, source_target_pairs={{0,2},{1,5},{2,0},{3,7},{4,6},{5,1},{6,4},{7,3},{8,10},{9,13},{10,... | collective-permute-start | bytes 933896 | tf_op jit(solution)/shard_map/ppermute | solution.py:60
  53.7 9.9 %collective-permute-start.1 = (bf16[64,2432]{1,0:T(8,128)(2,1)S(1)}, bf16[64,2432]{1,0:T(8,128)(2,1)S(1)}, u32[]{:S(2)}, u32[]{:S(2)}) collective-permute-start(bf16[64,2432]{1,0:T(8,128)(2,1)S(1)} %get-tuple-element.60), channel_id=1, source_target_pairs={{0,2},{1,5},{2,0},{3,7},{4,6},{5,1},{6,4},{7,3},{8,10},{9,13},{10,... | collective-permute-start | bytes 933896 | tf_op jit(solution)/shard_map/ppermute | solution.py:60
  60.3 6.8 %collective-permute-start.18 = (bf16[32,2304]{1,0:T(8,128)(2,1)S(1)}, bf16[32,2304]{1,0:T(8,128)(2,1)S(1)}, u32[]{:S(2)}, u32[]{:S(2)}) collective-permute-start(bf16[32,2304]{1,0:T(8,128)(2,1)S(1)} %get-tuple-element.78), channel_id=1, source_target_pairs={{0,2},{1,5},{2,0},{3,7},{4,6},{5,1},{6,4},{7,3},{8,10},{9,13},{10,... | collective-permute-start | bytes 442376 | tf_op jit(solution)/shard_map/ppermute | solution.py:60
  62.0 6.8 %collective-permute-start.10 = (bf16[32,2432]{1,0:T(8,128)(2,1)S(1)}, bf16[32,2432]{1,0:T(8,128)(2,1)S(1)}, u32[]{:S(2)}, u32[]{:S(2)}) collective-permute-start(bf16[32,2432]{1,0:T(8,128)(2,1)S(1)} %get-tuple-element.74), channel_id=1, source_target_pairs={{0,4},{1,3},{2,6},{3,1},{4,0},{5,7},{6,2},{7,5},{8,12},{9,11},{10,... | collective-permute-start | bytes 466952 | tf_op jit(solution)/shard_map/ppermute | solution.py:60
  63.6 5.7 %collective-permute-start.2 = (bf16[32,2432]{1,0:T(8,128)(2,1)S(1)}, bf16[32,2432]{1,0:T(8,128)(2,1)S(1)}, u32[]{:S(2)}, u32[]{:S(2)}) collective-permute-start(bf16[32,2432]{1,0:T(8,128)(2,1)S(1)} %get-tuple-element.72), channel_id=1, source_target_pairs={{0,4},{1,3},{2,6},{3,1},{4,0},{5,7},{6,2},{7,5},{8,12},{9,11},{10,... | collective-permute-start | bytes 466952 | tf_op jit(solution)/shard_map/ppermute | solution.py:60
  68.8 5.3 %collective-permute-start.11 = (bf16[16,2432]{1,0:T(8,128)(2,1)S(1)}, bf16[16,2432]{1,0:T(8,128)(2,1)S(1)}, u32[]{:S(2)}, u32[]{:S(2)}) collective-permute-start(bf16[16,2432]{1,0:T(8,128)(2,1)S(1)} %get-tuple-element.86), channel_id=1, source_target_pairs={{0,8},{1,9},{2,10},{3,11},{4,12},{5,13},{6,14},{7,15},{8,0},{9,1},... | collective-permute-start | bytes 233480 | tf_op jit(solution)/shard_map/ppermute | solution.py:60
  69.4 5.5 %collective-permute-start.3 = (bf16[16,2432]{1,0:T(8,128)(2,1)S(1)}, bf16[16,2432]{1,0:T(8,128)(2,1)S(1)}, u32[]{:S(2)}, u32[]{:S(2)}) collective-permute-start(bf16[16,2432]{1,0:T(8,128)(2,1)S(1)} %get-tuple-element.84), channel_id=1, source_target_pairs={{0,8},{1,9},{2,10},{3,11},{4,12},{5,13},{6,14},{7,15},{8,0},{9,1},... | collective-permute-start | bytes 233480 | tf_op jit(solution)/shard_map/ppermute | solution.py:60
  71.6 9.0 %collective-permute-start.20 = (bf16[16,2432]{1,0:T(8,128)(2,1)S(1)}, bf16[16,2432]{1,0:T(8,128)(2,1)S(1)}, u32[]{:S(2)}, u32[]{:S(2)}) collective-permute-start(bf16[16,2432]{1,0:T(8,128)(2,1)S(1)} %fusion.52), channel_id=1, source_target_pairs={{0,16},{1,17},{2,18},{3,19},{4,20},{5,21},{6,22},{7,23},{8,24},{9,... | collective-permute-start | bytes 233480 | tf_op jit(solution)/shard_map/ppermute | solution.py:60
  75.0 8.1 %collective-permute-start.4 = (bf16[16,2432]{1,0:T(8,128)(2,1)S(1)}, bf16[16,2432]{1,0:T(8,128)(2,1)S(1)}, u32[]{:S(2)}, u32[]{:S(2)}) collective-permute-start(bf16[16,2432]{1,0:T(8,128)(2,1)S(1)} %pad_maximum_fusion.10), channel_id=1, source_target_pairs={{0,16},{1,17},{2,18},{3,19},{4,20},{5,21},{6,22},{7,23},{8,24},{9,... | collective-permute-start | bytes 233480 | tf_op jit(solution)/shard_map/ppermute | solution.py:60
  76.0 8.1 %collective-permute-start.12 = (bf16[16,2432]{1,0:T(8,128)(2,1)S(1)}, bf16[16,2432]{1,0:T(8,128)(2,1)S(1)}, u32[]{:S(2)}, u32[]{:S(2)}) collective-permute-start(bf16[16,2432]{1,0:T(8,128)(2,1)S(1)} %pad_maximum_fusion.11), channel_id=1, source_target_pairs={{0,16},{1,17},{2,18},{3,19},{4,20},{5,21},{6,22},{7,23},{8,24},{9,... | collective-permute-start | bytes 233480 | tf_op jit(solution)/shard_map/ppermute | solution.py:60
  80.7 4.9 %collective-permute-start.21 = (bf16[16,2432]{1,0:T(8,128)(2,1)S(1)}, bf16[16,2432]{1,0:T(8,128)(2,1)S(1)}, u32[]{:S(2)}, u32[]{:S(2)}) collective-permute-start(bf16[16,2432]{1,0:T(8,128)(2,1)S(1)} %add_convert_fusion.28), channel_id=1, source_target_pairs={{0,8},{1,9},{2,10},{3,11},{4,12},{5,13},{6,14},{7,15},{8,0},{9,1},... | collective-permute-start | bytes 233480 | tf_op jit(solution)/shard_map/ppermute | solution.py:60
  85.6 6.3 %collective-permute-start.22 = (bf16[32,2432]{1,0:T(8,128)(2,1)S(1)}, bf16[32,2432]{1,0:T(8,128)(2,1)S(1)}, u32[]{:S(2)}, u32[]{:S(2)}) collective-permute-start(bf16[32,2432]{1,0:T(8,128)(2,1)S(1)} %pad_maximum_fusion.8), channel_id=1, source_target_pairs={{0,4},{1,3},{2,6},{3,1},{4,0},{5,7},{6,2},{7,5},{8,12},{9,11},{10,... | collective-permute-start | bytes 466952 | tf_op jit(solution)/shard_map/ppermute | solution.py:60
  87.6 7.6 %collective-permute-start.6 = (bf16[32,2432]{1,0:T(8,128)(2,1)S(1)}, bf16[32,2432]{1,0:T(8,128)(2,1)S(1)}, u32[]{:S(2)}, u32[]{:S(2)}) collective-permute-start(bf16[32,2432]{1,0:T(8,128)(2,1)S(1)} %pad_maximum_fusion.6), channel_id=1, source_target_pairs={{0,4},{1,3},{2,6},{3,1},{4,0},{5,7},{6,2},{7,5},{8,12},{9,11},{10,... | collective-permute-start | bytes 466952 | tf_op jit(solution)/shard_map/ppermute | solution.py:60
  88.7 9.9 %collective-permute-start.14 = (bf16[32,2432]{1,0:T(8,128)(2,1)S(1)}, bf16[32,2432]{1,0:T(8,128)(2,1)S(1)}, u32[]{:S(2)}, u32[]{:S(2)}) collective-permute-start(bf16[32,2432]{1,0:T(8,128)(2,1)S(1)} %pad_maximum_fusion.7), channel_id=1, source_target_pairs={{0,4},{1,3},{2,6},{3,1},{4,0},{5,7},{6,2},{7,5},{8,12},{9,11},{10,... | collective-permute-start | bytes 466952 | tf_op jit(solution)/shard_map/ppermute | solution.py:60
  92.0 9.4 %collective-permute-start.23 = (bf16[64,2432]{1,0:T(8,128)(2,1)S(1)}, bf16[64,2432]{1,0:T(8,128)(2,1)S(1)}, u32[]{:S(2)}, u32[]{:S(2)}) collective-permute-start(bf16[64,2432]{1,0:T(8,128)(2,1)S(1)} %pad_maximum_fusion.5), channel_id=1, source_target_pairs={{0,2},{1,5},{2,0},{3,7},{4,6},{5,1},{6,4},{7,3},{8,10},{9,13},{10,... | collective-permute-start | bytes 933896 | tf_op jit(solution)/shard_map/ppermute | solution.py:60
  95.3 7.6 %collective-permute-start.7 = (bf16[64,2432]{1,0:T(8,128)(2,1)S(1)}, bf16[64,2432]{1,0:T(8,128)(2,1)S(1)}, u32[]{:S(2)}, u32[]{:S(2)}) collective-permute-start(bf16[64,2432]{1,0:T(8,128)(2,1)S(1)} %pad_maximum_fusion.3), channel_id=1, source_target_pairs={{0,2},{1,5},{2,0},{3,7},{4,6},{5,1},{6,4},{7,3},{8,10},{9,13},{10,... | collective-permute-start | bytes 933896 | tf_op jit(solution)/shard_map/ppermute | solution.py:60
  98.6 7.6 %collective-permute-start.15 = (bf16[64,2432]{1,0:T(8,128)(2,1)S(1)}, bf16[64,2432]{1,0:T(8,128)(2,1)S(1)}, u32[]{:S(2)}, u32[]{:S(2)}) collective-permute-start(bf16[64,2432]{1,0:T(8,128)(2,1)S(1)} %pad_maximum_fusion.4), channel_id=1, source_target_pairs={{0,2},{1,5},{2,0},{3,7},{4,6},{5,1},{6,4},{7,3},{8,10},{9,13},{10,... | collective-permute-start | bytes 933896 | tf_op jit(solution)/shard_map/ppermute | solution.py:60
  101.4 5.9 %collective-permute-start.26 = (bf16[128,2432]{1,0:T(8,128)(2,1)S(1)}, bf16[128,2432]{1,0:T(8,128)(2,1)S(1)}, u32[]{:S(2)}, u32[]{:S(2)}) collective-permute-start(bf16[128,2432]{1,0:T(8,128)(2,1)S(1)} %pad_maximum_fusion.2), channel_id=1, source_target_pairs={{0,1},{1,0},{2,3},{3,2},{4,5},{5,4},{6,7},{7,6},{8,9},{9,8},{10,11... | collective-permute-start | bytes 1867784 | tf_op jit(solution)/shard_map/ppermute | solution.py:60
  103.1 5.1 %collective-permute-start.24 = (bf16[128,2432]{1,0:T(8,128)(2,1)S(1)}, bf16[128,2432]{1,0:T(8,128)(2,1)S(1)}, u32[]{:S(2)}, u32[]{:S(2)}) collective-permute-start(bf16[128,2432]{1,0:T(8,128)(2,1)S(1)} %get-tuple-element.52), channel_id=1, source_target_pairs={{0,1},{1,0},{2,3},{3,2},{4,5},{5,4},{6,7},{7,6},{8,9},{9,8},{10,11... | collective-permute-start | bytes 1867784 | tf_op jit(solution)/shard_map/ppermute | solution.py:60
  113.4 9.4 %collective-permute-start.38 = (bf16[64,2304]{1,0:T(8,128)(2,1)S(1)}, bf16[64,2304]{1,0:T(8,128)(2,1)S(1)}, u32[]{:S(2)}, u32[]{:S(2)}) collective-permute-start(bf16[64,2304]{1,0:T(8,128)(2,1)S(1)} %get-tuple-element.64), channel_id=1, source_target_pairs={{0,8},{1,9},{2,10},{3,11},{4,12},{5,13},{6,14},{7,15},{8,0},{9,1},... | collective-permute-start | bytes 884744 | tf_op jit(solution)/shard_map/ppermute | solution.py:60
  114.4 10.5 %collective-permute-start.28 = (bf16[64,2432]{1,0:T(8,128)(2,1)S(1)}, bf16[64,2432]{1,0:T(8,128)(2,1)S(1)}, u32[]{:S(2)}, u32[]{:S(2)}) collective-permute-start(bf16[64,2432]{1,0:T(8,128)(2,1)S(1)} %get-tuple-element.56), channel_id=1, source_target_pairs={{0,2},{1,5},{2,0},{3,7},{4,6},{5,1},{6,4},{7,3},{8,10},{9,13},{10,... | collective-permute-start | bytes 933896 | tf_op jit(solution)/shard_map/ppermute | solution.py:60
  116.6 9.9 %collective-permute-start.33 = (bf16[64,2432]{1,0:T(8,128)(2,1)S(1)}, bf16[64,2432]{1,0:T(8,128)(2,1)S(1)}, u32[]{:S(2)}, u32[]{:S(2)}) collective-permute-start(bf16[64,2432]{1,0:T(8,128)(2,1)S(1)} %get-tuple-element.58), channel_id=1, source_target_pairs={{0,2},{1,5},{2,0},{3,7},{4,6},{5,1},{6,4},{7,3},{8,10},{9,13},{10,... | collective-permute-start | bytes 933896 | tf_op jit(solution)/shard_map/ppermute | solution.py:60
  122.9 6.5 %collective-permute-start.39 = (bf16[32,2304]{1,0:T(8,128)(2,1)S(1)}, bf16[32,2304]{1,0:T(8,128)(2,1)S(1)}, u32[]{:S(2)}, u32[]{:S(2)}) collective-permute-start(bf16[32,2304]{1,0:T(8,128)(2,1)S(1)} %get-tuple-element.76), channel_id=1, source_target_pairs={{0,2},{1,5},{2,0},{3,7},{4,6},{5,1},{6,4},{7,3},{8,10},{9,13},{10,... | collective-permute-start | bytes 442376 | tf_op jit(solution)/shard_map/ppermute | solution.py:60
  125.0 6.6 %collective-permute-start.29 = (bf16[32,2432]{1,0:T(8,128)(2,1)S(1)}, bf16[32,2432]{1,0:T(8,128)(2,1)S(1)}, u32[]{:S(2)}, u32[]{:S(2)}) collective-permute-start(bf16[32,2432]{1,0:T(8,128)(2,1)S(1)} %get-tuple-element.68), channel_id=1, source_target_pairs={{0,4},{1,3},{2,6},{3,1},{4,0},{5,7},{6,2},{7,5},{8,12},{9,11},{10,... | collective-permute-start | bytes 466952 | tf_op jit(solution)/shard_map/ppermute | solution.py:60
  126.6 7.4 %collective-permute-start.34 = (bf16[32,2432]{1,0:T(8,128)(2,1)S(1)}, bf16[32,2432]{1,0:T(8,128)(2,1)S(1)}, u32[]{:S(2)}, u32[]{:S(2)}) collective-permute-start(bf16[32,2432]{1,0:T(8,128)(2,1)S(1)} %get-tuple-element.70), channel_id=1, source_target_pairs={{0,4},{1,3},{2,6},{3,1},{4,0},{5,7},{6,2},{7,5},{8,12},{9,11},{10,... | collective-permute-start | bytes 466952 | tf_op jit(solution)/shard_map/ppermute | solution.py:60
  131.6 7.3 %collective-permute-start.30 = (bf16[16,2432]{1,0:T(8,128)(2,1)S(1)}, bf16[16,2432]{1,0:T(8,128)(2,1)S(1)}, u32[]{:S(2)}, u32[]{:S(2)}) collective-permute-start(bf16[16,2432]{1,0:T(8,128)(2,1)S(1)} %get-tuple-element.80), channel_id=1, source_target_pairs={{0,8},{1,9},{2,10},{3,11},{4,12},{5,13},{6,14},{7,15},{8,0},{9,1},... | collective-permute-start | bytes 233480 | tf_op jit(solution)/shard_map/ppermute | solution.py:60
  133.9 5.0 %collective-permute-start.41 = (bf16[8,2304]{1,0:T(8,128)(2,1)S(1)}, bf16[8,2304]{1,0:T(8,128)(2,1)S(1)}, u32[]{:S(2)}, u32[]{:S(2)}) collective-permute-start(bf16[8,2304]{1,0:T(8,128)(2,1)S(1)} %add_convert_fusion.48), channel_id=1, source_target_pairs={{0,16},{1,17},{2,18},{3,19},{4,20},{5,21},{6,22},{7,23},{8,24},{9,... | collective-permute-start | bytes 110600 | tf_op jit(solution)/shard_map/ppermute | solution.py:60
  134.1 5.0 %collective-permute-start.35 = (bf16[16,2432]{1,0:T(8,128)(2,1)S(1)}, bf16[16,2432]{1,0:T(8,128)(2,1)S(1)}, u32[]{:S(2)}, u32[]{:S(2)}) collective-permute-start(bf16[16,2432]{1,0:T(8,128)(2,1)S(1)} %get-tuple-element.82), channel_id=1, source_target_pairs={{0,8},{1,9},{2,10},{3,11},{4,12},{5,13},{6,14},{7,15},{8,0},{9,1},... | collective-permute-start | bytes 233480 | tf_op jit(solution)/shard_map/ppermute | solution.py:60
  139.0 5.0 %collective-permute-start.31 = (bf16[8,2432]{1,0:T(8,128)(2,1)S(1)}, bf16[8,2432]{1,0:T(8,128)(2,1)S(1)}, u32[]{:S(2)}, u32[]{:S(2)}) collective-permute-start(bf16[8,2432]{1,0:T(8,128)(2,1)S(1)} %add_convert_fusion.42), channel_id=1, source_target_pairs={{0,16},{1,17},{2,18},{3,19},{4,20},{5,21},{6,22},{7,23},{8,24},{9,... | collective-permute-start | bytes 116744 | tf_op jit(solution)/shard_map/ppermute | solution.py:60
  139.1 5.3 %collective-permute-start.36 = (bf16[8,2432]{1,0:T(8,128)(2,1)S(1)}, bf16[8,2432]{1,0:T(8,128)(2,1)S(1)}, u32[]{:S(2)}, u32[]{:S(2)}) collective-permute-start(bf16[8,2432]{1,0:T(8,128)(2,1)S(1)} %add_convert_fusion.40), channel_id=1, source_target_pairs={{0,16},{1,17},{2,18},{3,19},{4,20},{5,21},{6,22},{7,23},{8,24},{9,... | collective-permute-start | bytes 116744 | tf_op jit(solution)/shard_map/ppermute | solution.py:60
  (22 other events, 125.3 us)

commit v4 on v3

--- a/solution.py
+++ b/solution.py
@@ -47,7 +47,7 @@
 
 def chain_orders(nbits):
     plain = list(range(1, nbits - 1))
-    return [plain] * (CHAINS - 1) + [[3, 1, 2, *plain[3:]]]
+    return [[3, 1, 2, *plain[3:]]] + [plain] * (CHAINS - 1)
 
 
 def place_rows(order, rows):
@@ -104,20 +104,23 @@
 
 
 def attend_kernel(lengths_ref, latent_ref, rope_ref, keys_ref, turned_ref, out_ref, held_ref):
-    token = pl.program_id(0)
-    keys = keys_ref[0]
-    scores = lax.dot_general(
-        latent_ref[0], keys, (((1,), (1,)), ((), ())), preferred_element_type=f32
-    )
-    scores = scores + jnp.dot(rope_ref[0], turned_ref[0], preferred_element_type=f32)
-    scores = scores * score_scale
-    column = lax.broadcasted_iota(jnp.int32, scores.shape, 1)
-    scores = jnp.where(column < lengths_ref[token], scores, -jnp.inf)
-    expd = jnp.exp(scores - jnp.max(scores, axis=1, keepdims=True))
-    weights = (expd / jnp.sum(expd, axis=1, keepdims=True)).astype(bf16)
-    held_ref[token] = jnp.dot(weights, keys, preferred_element_type=f32)
-
-    @pl.when(token == pl.num_programs(0) - 1)
+    step = pl.program_id(0)
+    group = keys_ref.shape[0]
+    for i in range(group):
+        token = step * group + i
+        keys = keys_ref[i]
+        scores = lax.dot_general(
+            latent_ref[i], keys, (((1,), (1,)), ((), ())), preferred_element_type=f32
+        )
+        scores = scores + jnp.dot(rope_ref[i], turned_ref[i], preferred_element_type=f32)
+        scores = scores * score_scale
+        column = lax.broadcasted_iota(jnp.int32, scores.shape, 1)
+        scores = jnp.where(column < lengths_ref[token], scores, -jnp.inf)
+        expd = jnp.exp(scores - jnp.max(scores, axis=1, keepdims=True))
+        weights = (expd * (1.0 / jnp.sum(expd, axis=1, keepdims=True))).astype(bf16)
+        held_ref[token] = jnp.dot(weights, keys, preferred_element_type=f32)
+
+    @pl.when(step == pl.num_programs(0) - 1)
     def _():
         out_ref[...] = jnp.swapaxes(held_ref[...], 0, 1).astype(bf16)
 
@@ -126,16 +129,17 @@
     tokens, heads, rank = q_latent.shape
     _, turned, cached = cache_rope.shape
     at = lambda i: (i, 0, 0)
+    group = 2 if tokens % 2 == 0 else 1
     return pl.pallas_call(
         attend_kernel,
-        grid=(tokens,),
+        grid=(tokens // group,),
         out_shape=jax.ShapeDtypeStruct((heads, tokens, rank), bf16),
         in_specs=[
             pl.BlockSpec(memory_space=pltpu.SMEM),
-            pl.BlockSpec((1, heads, rank), at),
-            pl.BlockSpec((1, heads, turned), at),
-            pl.BlockSpec((1, cached, rank), at),
-            pl.BlockSpec((1, turned, cached), at),
+            pl.BlockSpec((group, heads, rank), at),
+            pl.BlockSpec((group, heads, turned), at),
+            pl.BlockSpec((group, cached, rank), at),
+            pl.BlockSpec((group, turned, cached), at),
         ],
         out_specs=pl.BlockSpec((heads, tokens, rank), lambda i: (0, 0, 0)),
         scratch_shapes=[pltpu.VMEM((tokens, heads, rank), f32)],
@@ -317,7 +321,7 @@
     out = []
     for i, ((start, size), base) in enumerate(zip(plans, residual, strict=True)):
         acts = hidden
-        if orders[i] != orders[0]:
+        if orders[i] != sorted(orders[i]):
             move = np.eye(rows, dtype=np.float32)[place_rows(orders[i], rows)]
             acts = jnp.dot(jnp.asarray(move, bf16), hidden, preferred_element_type=f32).astype(bf16)
         keep, send = project(acts, down_near, start, size)

time: 146 us -> 141 us (0.966)
  starting transfers between devices: 52.7 us -> 47 us
  waiting for transfers between devices: 53.3 us -> 55.3 us
  Pallas kernels: 18 us -> 16.3 us
    ppermute x42, starting transfers between devices: 45.3 us -> 39.6 us  [swap(): return lax.ppermute(x, 'expert', pairs)]
    ppermute x42, waiting for transfers between devices: 40 us -> 42.1 us  [swap(): return lax.ppermute(x, 'expert', pairs)]
    pallas_call x1, Pallas kernels: 8.76 us -> 7.09 us  [attend(): pl.pallas_call(attend_kernel, grid=(tokens // group,), out_shape=jax.Shap...]
  transfers between devices with their start and end apart: 43 -> 43, of which waited for: 23 -> 25; matrix products, arithmetic and copies ran while one was open for 9% -> 9% of each run, Pallas kernels for 5% -> 6%
where the time goes in v4:
time: 141 us; the launch traced here: 140 us
  waiting for transfers between devices  55.3 us (39%)
  starting transfers between devices  47 us (33%)
  Pallas kernels  16.3 us (12%)
  local copies, waits for them, and re-layouts  11.3 us (8%)
  matrix products  5.16 us (4%)
  other arithmetic  4.42 us (3%)
    ppermute x42, waiting for transfers between devices, swap(): return lax.ppermute(x, 'expert', pairs)  42.1 us
    ppermute x42, starting transfers between devices, swap(): return lax.ppermute(x, 'expert', pairs)  39.6 us
    all_to_all x1, waiting for transfers between devices, shards(): lax.all_to_all(latent_out, 'expert', split_axis=0, concat_axis=0, tiled=T...  13.3 us
    slice x2, local copies, waits for them, and re-layouts, shards(): out_near = [out_after[:, start:start + size] for start, size in plans]  7.57 us
    all_to_all x1, starting transfers between devices, shards(): lax.all_to_all(latent_out, 'expert', split_axis=0, concat_axis=0, tiled=T...  7.42 us
    pallas_call x1, Pallas kernels, attend(): pl.pallas_call(attend_kernel, grid=(tokens // group,), out_shape=jax.Shap...  7.09 us
    pallas_call x1, Pallas kernels, fetch(): pl.pallas_call(fetch_kernel, out_shape=[jax.ShapeDtypeStruct(shape, bf16)...  5.05 us
    pallas_call x6, Pallas kernels, project(): pl.pallas_call(functools.partial(project_kernel, start), out_shape=[half,...  4.15 us
  transfers between devices with their start and end apart: 43, of which 25 were waited for; matrix products, arithmetic and copies ran while one was open for 9% of the time, Pallas kernels for 6%

profile of v4, /device:TPU:0, one launch (start us, length us, event | category | flops | bytes accessed | tf_op | source)
XLA Modules:
  0.0 140.2 jit_solution(8574230328703237604)
XLA Ops:
  0.0 2.0 %reshape.121.rope_ref = bf16[8,128,64]{2,1,0:T(8,128)(2,1)} reshape(bf16[8,8192]{1,0:T(8,128)(2,1)} %param.17) | data formatting | bytes 262144 | tf_op jit(solution)/shard_map/reshape | solution.py:152
  2.0 7.1 %shard_map.145.after_ref = bf16[128,8,512]{2,1,0:T(8,128)(2,1)} custom-call(s32[8]{0:T(128)} %lengths_ref.1, bf16[8,128,512]{2,1,0:T(8,128)(2,1)} %latent_ref.1, bf16[8,128,64]{2,1,0:T(8,128)(2,1)} %reshape.121.rope_ref, bf16[8,256,512]{2,1,0:T(8,128)(2,1)} %keys_ref.1, bf16[8,64,256]{2,1,0:T(8,128)(2,1)} %turned_ref.1), custom_call_target="tpu_custom_call" | custom-call | flops 570425344 | bytes 4456448 | tf_op jit(solution)/shard_map/pallas_call | solution.py:133
  9.1 7.4 %all-to-all-start = ((bf16[128,8,512]{2,1,0:T(8,128)(2,1)}), bf16[128,8,512]{2,1,0:T(8,128)(2,1)}, u32[]{:S(2)}, u32[]{:S(2)}) async-start(bf16[128,8,512]{2,1,0:T(8,128)(2,1)} %shard_map.145.after_ref), calls=%async_computation | async-start | bytes 2097152 | tf_op jit(solution)/shard_map/all_to_all | solution.py:250
  16.5 3.3 %slice.368.weight_ref = bf16[512,2304]{1,0:T(8,128)(2,1)} slice(bf16[512,7168]{1,0:T(8,128)(2,1)} %param.22), slice={[0:512], [4864:7168]} | slice | bytes 4718592 | tf_op jit(solution)/shard_map/slice | solution.py:246
  19.8 5.1 %shard_map.146 = (bf16[7168,256]{1,0:T(8,128)(2,1)}, bf16[128,7168]{1,0:T(8,128)(2,1)}) custom-call(bf16[128,8,512]{2,1,0:T(8,128)(2,1)} %shard_map.145.after_ref, bf16[1,7168,128]{2,1,0:T(8,128)(2,1)} %gate_ref.1, bf16[1,7168,128]{2,1,0:T(8,128)(2,1)} %up_ref.1, bf16[1,128,7168]{2,1,0:T(8,128)(2,1)} %down_ref.1), custom_call_target="tpu_custom_call" | custom-call | bytes 11010048 | tf_op jit(solution)/shard_map/pallas_call | solution.py:172
  24.9 4.3 %fusion.67 = (bf16[512,2432]{1,0:T(8,128)(2,1)}, bf16[512,2432]{1,0:T(8,128)(2,1)S(1)}) fusion(bf16[512,7168]{1,0:T(8,128)(2,1)} %param.22), kind=kLoop, calls=%fused_computation.178 | loop fusion | bytes 9961472 | tf_op jit(solution)/shard_map/slice | solution.py:246
  29.4 13.3 %all-to-all-done = bf16[128,8,512]{2,1,0:T(8,128)(2,1)} async-done(((bf16[128,8,512]{2,1,0:T(8,128)(2,1)}), bf16[128,8,512]{2,1,0:T(8,128)(2,1)}, u32[]{:S(2)}, u32[]{:S(2)}) %all-to-all-start) | async-done | bytes 1048608 | tf_op jit(solution)/shard_map/all_to_all | solution.py:250
  42.7 2.2 %fusion.12 = bf16[32,8,4,128]{3,0,1,2:T(8,128)(2,1)S(1)} fusion(bf16[32,4,8,512]{3,2,1,0:T(8,128)(2,1)} %bitcast.2, bf16[4,512,128]{2,1,0:T(8,128)(2,1)S(1)} %copy-done), kind=kOutput, calls=%fused_computation.27 | convolution fusion | flops 134348800 | bytes 1835008 | tf_op jit(solution)/shard_map/sqtg,qge->stqe/dot_general | solution.py:253
  49.8 1.5 %collective-permute-start.17 = (bf16[64,2304]{1,0:T(8,128)(2,1)S(1)}, bf16[64,2304]{1,0:T(8,128)(2,1)S(1)}, u32[]{:S(2)}, u32[]{:S(2)}) collective-permute-start(bf16[64,2304]{1,0:T(8,128)(2,1)S(1)} %get-tuple-element.66), channel_id=1, source_target_pairs={{0,2},{1,5},{2,0},{3,7},{4,6},{5,1},{6,4},{7,3},{8,10},{9,13},{10,... | collective-permute-start | bytes 884744 | tf_op jit(solution)/shard_map/ppermute | solution.py:60
  53.1 3.5 %collective-permute-done.17 = bf16[64,2304]{1,0:T(8,128)(2,1)S(1)} collective-permute-done((bf16[64,2304]{1,0:T(8,128)(2,1)S(1)}, bf16[64,2304]{1,0:T(8,128)(2,1)S(1)}, u32[]{:S(2)}, u32[]{:S(2)}) %collective-permute-start.17) | collective-permute-done | bytes 294944 | tf_op jit(solution)/shard_map/ppermute | solution.py:60
  56.6 1.5 %collective-permute-start.18 = (bf16[32,2304]{1,0:T(8,128)(2,1)S(1)}, bf16[32,2304]{1,0:T(8,128)(2,1)S(1)}, u32[]{:S(2)}, u32[]{:S(2)}) collective-permute-start(bf16[32,2304]{1,0:T(8,128)(2,1)S(1)} %get-tuple-element.78), channel_id=1, source_target_pairs={{0,4},{1,3},{2,6},{3,1},{4,0},{5,7},{6,2},{7,5},{8,12},{9,11},{10,... | collective-permute-start | bytes 442376 | tf_op jit(solution)/shard_map/ppermute | solution.py:60
  58.2 3.1 %collective-permute-done.9 = bf16[64,2432]{1,0:T(8,128)(2,1)S(1)} collective-permute-done((bf16[64,2432]{1,0:T(8,128)(2,1)S(1)}, bf16[64,2432]{1,0:T(8,128)(2,1)S(1)}, u32[]{:S(2)}, u32[]{:S(2)}) %collective-permute-start.9) | collective-permute-done | bytes 311328 | tf_op jit(solution)/shard_map/ppermute | solution.py:60
  61.4 1.5 %collective-permute-start.10 = (bf16[32,2432]{1,0:T(8,128)(2,1)S(1)}, bf16[32,2432]{1,0:T(8,128)(2,1)S(1)}, u32[]{:S(2)}, u32[]{:S(2)}) collective-permute-start(bf16[32,2432]{1,0:T(8,128)(2,1)S(1)} %get-tuple-element.74), channel_id=1, source_target_pairs={{0,4},{1,3},{2,6},{3,1},{4,0},{5,7},{6,2},{7,5},{8,12},{9,11},{10,... | collective-permute-start | bytes 466952 | tf_op jit(solution)/shard_map/ppermute | solution.py:60
  63.0 1.5 %collective-permute-start.2 = (bf16[32,2432]{1,0:T(8,128)(2,1)S(1)}, bf16[32,2432]{1,0:T(8,128)(2,1)S(1)}, u32[]{:S(2)}, u32[]{:S(2)}) collective-permute-start(bf16[32,2432]{1,0:T(8,128)(2,1)S(1)} %get-tuple-element.72), channel_id=1, source_target_pairs={{0,2},{1,5},{2,0},{3,7},{4,6},{5,1},{6,4},{7,3},{8,10},{9,13},{10,... | collective-permute-start | bytes 466952 | tf_op jit(solution)/shard_map/ppermute | solution.py:60
  64.7 2.0 %collective-permute-done.10 = bf16[32,2432]{1,0:T(8,128)(2,1)S(1)} collective-permute-done((bf16[32,2432]{1,0:T(8,128)(2,1)S(1)}, bf16[32,2432]{1,0:T(8,128)(2,1)S(1)}, u32[]{:S(2)}, u32[]{:S(2)}) %collective-permute-start.10) | collective-permute-done | bytes 155680 | tf_op jit(solution)/shard_map/ppermute | solution.py:60
  67.5 1.6 %collective-permute-done.2 = bf16[32,2432]{1,0:T(8,128)(2,1)S(1)} collective-permute-done((bf16[32,2432]{1,0:T(8,128)(2,1)S(1)}, bf16[32,2432]{1,0:T(8,128)(2,1)S(1)}, u32[]{:S(2)}, u32[]{:S(2)}) %collective-permute-start.2) | collective-permute-done | bytes 155680 | tf_op jit(solution)/shard_map/ppermute | solution.py:60
  71.2 2.5 %collective-permute-done.3 = bf16[16,2432]{1,0:T(8,128)(2,1)S(1)} collective-permute-done((bf16[16,2432]{1,0:T(8,128)(2,1)S(1)}, bf16[16,2432]{1,0:T(8,128)(2,1)S(1)}, u32[]{:S(2)}, u32[]{:S(2)}) %collective-permute-start.3) | collective-permute-done | bytes 77856 | tf_op jit(solution)/shard_map/ppermute | solution.py:60
  73.8 2.9 %collective-permute-start.12 = (bf16[16,2432]{1,0:T(8,128)(2,1)S(1)}, bf16[16,2432]{1,0:T(8,128)(2,1)S(1)}, u32[]{:S(2)}, u32[]{:S(2)}) collective-permute-start(bf16[16,2432]{1,0:T(8,128)(2,1)S(1)} %pad_maximum_fusion.11), channel_id=1, source_target_pairs={{0,16},{1,17},{2,18},{3,19},{4,20},{5,21},{6,22},{7,23},{8,24},{9,... | collective-permute-start | bytes 233480 | tf_op jit(solution)/shard_map/ppermute | solution.py:60
  77.3 1.9 %collective-permute-done.4 = bf16[16,2432]{1,0:T(8,128)(2,1)S(1)} collective-permute-done((bf16[16,2432]{1,0:T(8,128)(2,1)S(1)}, bf16[16,2432]{1,0:T(8,128)(2,1)S(1)}, u32[]{:S(2)}, u32[]{:S(2)}) %collective-permute-start.4) | collective-permute-done | bytes 77856 | tf_op jit(solution)/shard_map/ppermute | solution.py:60
  86.2 2.8 %collective-permute-done.22 = bf16[32,2432]{1,0:T(8,128)(2,1)S(1)} collective-permute-done((bf16[32,2432]{1,0:T(8,128)(2,1)S(1)}, bf16[32,2432]{1,0:T(8,128)(2,1)S(1)}, u32[]{:S(2)}, u32[]{:S(2)}) %collective-permute-start.22) | collective-permute-done | bytes 155680 | tf_op jit(solution)/shard_map/ppermute | solution.py:60
  89.0 2.1 %collective-permute-start.23 = (bf16[64,2432]{1,0:T(8,128)(2,1)S(1)}, bf16[64,2432]{1,0:T(8,128)(2,1)S(1)}, u32[]{:S(2)}, u32[]{:S(2)}) collective-permute-start(bf16[64,2432]{1,0:T(8,128)(2,1)S(1)} %pad_maximum_fusion.5), channel_id=1, source_target_pairs={{0,2},{1,5},{2,0},{3,7},{4,6},{5,1},{6,4},{7,3},{8,10},{9,13},{10,... | collective-permute-start | bytes 933896 | tf_op jit(solution)/shard_map/ppermute | solution.py:60
  92.4 2.1 %collective-permute-start.7 = (bf16[64,2432]{1,0:T(8,128)(2,1)S(1)}, bf16[64,2432]{1,0:T(8,128)(2,1)S(1)}, u32[]{:S(2)}, u32[]{:S(2)}) collective-permute-start(bf16[64,2432]{1,0:T(8,128)(2,1)S(1)} %pad_maximum_fusion.3), channel_id=1, source_target_pairs={{0,2},{1,5},{2,0},{3,7},{4,6},{5,1},{6,4},{7,3},{8,10},{9,13},{10,... | collective-permute-start | bytes 933896 | tf_op jit(solution)/shard_map/ppermute | solution.py:60
  95.7 2.1 %collective-permute-start.15 = (bf16[64,2432]{1,0:T(8,128)(2,1)S(1)}, bf16[64,2432]{1,0:T(8,128)(2,1)S(1)}, u32[]{:S(2)}, u32[]{:S(2)}) collective-permute-start(bf16[64,2432]{1,0:T(8,128)(2,1)S(1)} %pad_maximum_fusion.4), channel_id=1, source_target_pairs={{0,2},{1,5},{2,0},{3,7},{4,6},{5,1},{6,4},{7,3},{8,10},{9,13},{10,... | collective-permute-start | bytes 933896 | tf_op jit(solution)/shard_map/ppermute | solution.py:60
  99.6 3.1 %collective-permute-done.15 = bf16[64,2432]{1,0:T(8,128)(2,1)S(1)} collective-permute-done((bf16[64,2432]{1,0:T(8,128)(2,1)S(1)}, bf16[64,2432]{1,0:T(8,128)(2,1)S(1)}, u32[]{:S(2)}, u32[]{:S(2)}) %collective-permute-start.15) | collective-permute-done | bytes 311328 | tf_op jit(solution)/shard_map/ppermute | solution.py:60
  109.9 2.1 %collective-permute-start.38 = (bf16[64,2304]{1,0:T(8,128)(2,1)S(1)}, bf16[64,2304]{1,0:T(8,128)(2,1)S(1)}, u32[]{:S(2)}, u32[]{:S(2)}) collective-permute-start(bf16[64,2304]{1,0:T(8,128)(2,1)S(1)} %get-tuple-element.64), channel_id=1, source_target_pairs={{0,2},{1,5},{2,0},{3,7},{4,6},{5,1},{6,4},{7,3},{8,10},{9,13},{10,... | collective-permute-start | bytes 884744 | tf_op jit(solution)/shard_map/ppermute | solution.py:60
  114.0 2.7 %collective-permute-done.38 = bf16[64,2304]{1,0:T(8,128)(2,1)S(1)} collective-permute-done((bf16[64,2304]{1,0:T(8,128)(2,1)S(1)}, bf16[64,2304]{1,0:T(8,128)(2,1)S(1)}, u32[]{:S(2)}, u32[]{:S(2)}) %collective-permute-start.38) | collective-permute-done | bytes 294944 | tf_op jit(solution)/shard_map/ppermute | solution.py:60
  117.9 2.7 %collective-permute-done.28 = bf16[64,2432]{1,0:T(8,128)(2,1)S(1)} collective-permute-done((bf16[64,2432]{1,0:T(8,128)(2,1)S(1)}, bf16[64,2432]{1,0:T(8,128)(2,1)S(1)}, u32[]{:S(2)}, u32[]{:S(2)}) %collective-permute-start.28) | collective-permute-done | bytes 311328 | tf_op jit(solution)/shard_map/ppermute | solution.py:60
  120.6 2.1 %collective-permute-start.29 = (bf16[32,2432]{1,0:T(8,128)(2,1)S(1)}, bf16[32,2432]{1,0:T(8,128)(2,1)S(1)}, u32[]{:S(2)}, u32[]{:S(2)}) collective-permute-start(bf16[32,2432]{1,0:T(8,128)(2,1)S(1)} %get-tuple-element.68), channel_id=1, source_target_pairs={{0,2},{1,5},{2,0},{3,7},{4,6},{5,1},{6,4},{7,3},{8,10},{9,13},{10,... | collective-permute-start | bytes 466952 | tf_op jit(solution)/shard_map/ppermute | solution.py:60
  124.7 2.8 %collective-permute-done.29 = bf16[32,2432]{1,0:T(8,128)(2,1)S(1)} collective-permute-done((bf16[32,2432]{1,0:T(8,128)(2,1)S(1)}, bf16[32,2432]{1,0:T(8,128)(2,1)S(1)}, u32[]{:S(2)}, u32[]{:S(2)}) %collective-permute-start.29) | collective-permute-done | bytes 155680 | tf_op jit(solution)/shard_map/ppermute | solution.py:60
  130.5 3.2 %collective-permute-done.41 = bf16[8,2304]{1,0:T(8,128)(2,1)S(1)} collective-permute-done((bf16[8,2304]{1,0:T(8,128)(2,1)S(1)}, bf16[8,2304]{1,0:T(8,128)(2,1)S(1)}, u32[]{:S(2)}, u32[]{:S(2)}) %collective-permute-start.41) | collective-permute-done | bytes 36896 | tf_op jit(solution)/shard_map/ppermute | solution.py:60
  134.4 2.5 %collective-permute-start.36 = (bf16[8,2432]{1,0:T(8,128)(2,1)S(1)}, bf16[8,2432]{1,0:T(8,128)(2,1)S(1)}, u32[]{:S(2)}, u32[]{:S(2)}) collective-permute-start(bf16[8,2432]{1,0:T(8,128)(2,1)S(1)} %add_convert_fusion.40), channel_id=1, source_target_pairs={{0,16},{1,17},{2,18},{3,19},{4,20},{5,21},{6,22},{7,23},{8,24},{9,... | collective-permute-start | bytes 116744 | tf_op jit(solution)/shard_map/ppermute | solution.py:60
  136.9 2.2 %collective-permute-done.31 = bf16[8,2432]{1,0:T(8,128)(2,1)S(1)} collective-permute-done((bf16[8,2432]{1,0:T(8,128)(2,1)S(1)}, bf16[8,2432]{1,0:T(8,128)(2,1)S(1)}, u32[]{:S(2)}, u32[]{:S(2)}) %collective-permute-start.31) | collective-permute-done | bytes 38944 | tf_op jit(solution)/shard_map/ppermute | solution.py:60
  (163 shorter events, 39.1 us)
Async XLA Ops:
  9.1 33.6 %all-to-all-start = ((bf16[128,8,512]{2,1,0:T(8,128)(2,1)}), bf16[128,8,512]{2,1,0:T(8,128)(2,1)}, u32[]{:S(2)}, u32[]{:S(2)}) async-start(bf16[128,8,512]{2,1,0:T(8,128)(2,1)} %shard_map.145.after_ref), calls=%async_computation | async-start | bytes 2097152 | tf_op jit(solution)/shard_map/all_to_all | solution.py:250
  49.8 6.8 %collective-permute-start.17 = (bf16[64,2304]{1,0:T(8,128)(2,1)S(1)}, bf16[64,2304]{1,0:T(8,128)(2,1)S(1)}, u32[]{:S(2)}, u32[]{:S(2)}) collective-permute-start(bf16[64,2304]{1,0:T(8,128)(2,1)S(1)} %get-tuple-element.66), channel_id=1, source_target_pairs={{0,2},{1,5},{2,0},{3,7},{4,6},{5,1},{6,4},{7,3},{8,10},{9,13},{10,... | collective-permute-start | bytes 884744 | tf_op jit(solution)/shard_map/ppermute | solution.py:60
  51.5 9.8 %collective-permute-start.9 = (bf16[64,2432]{1,0:T(8,128)(2,1)S(1)}, bf16[64,2432]{1,0:T(8,128)(2,1)S(1)}, u32[]{:S(2)}, u32[]{:S(2)}) collective-permute-start(bf16[64,2432]{1,0:T(8,128)(2,1)S(1)} %get-tuple-element.62), channel_id=1, source_target_pairs={{0,2},{1,5},{2,0},{3,7},{4,6},{5,1},{6,4},{7,3},{8,10},{9,13},{10,... | collective-permute-start | bytes 933896 | tf_op jit(solution)/shard_map/ppermute | solution.py:60
  52.2 10.7 %collective-permute-start.1 = (bf16[64,2432]{1,0:T(8,128)(2,1)S(1)}, bf16[64,2432]{1,0:T(8,128)(2,1)S(1)}, u32[]{:S(2)}, u32[]{:S(2)}) collective-permute-start(bf16[64,2432]{1,0:T(8,128)(2,1)S(1)} %get-tuple-element.60), channel_id=1, source_target_pairs={{0,8},{1,9},{2,10},{3,11},{4,12},{5,13},{6,14},{7,15},{8,0},{9,1},... | collective-permute-start | bytes 933896 | tf_op jit(solution)/shard_map/ppermute | solution.py:60
  56.6 7.9 %collective-permute-start.18 = (bf16[32,2304]{1,0:T(8,128)(2,1)S(1)}, bf16[32,2304]{1,0:T(8,128)(2,1)S(1)}, u32[]{:S(2)}, u32[]{:S(2)}) collective-permute-start(bf16[32,2304]{1,0:T(8,128)(2,1)S(1)} %get-tuple-element.78), channel_id=1, source_target_pairs={{0,4},{1,3},{2,6},{3,1},{4,0},{5,7},{6,2},{7,5},{8,12},{9,11},{10,... | collective-permute-start | bytes 442376 | tf_op jit(solution)/shard_map/ppermute | solution.py:60
  61.4 5.3 %collective-permute-start.10 = (bf16[32,2432]{1,0:T(8,128)(2,1)S(1)}, bf16[32,2432]{1,0:T(8,128)(2,1)S(1)}, u32[]{:S(2)}, u32[]{:S(2)}) collective-permute-start(bf16[32,2432]{1,0:T(8,128)(2,1)S(1)} %get-tuple-element.74), channel_id=1, source_target_pairs={{0,4},{1,3},{2,6},{3,1},{4,0},{5,7},{6,2},{7,5},{8,12},{9,11},{10,... | collective-permute-start | bytes 466952 | tf_op jit(solution)/shard_map/ppermute | solution.py:60
  63.0 6.1 %collective-permute-start.2 = (bf16[32,2432]{1,0:T(8,128)(2,1)S(1)}, bf16[32,2432]{1,0:T(8,128)(2,1)S(1)}, u32[]{:S(2)}, u32[]{:S(2)}) collective-permute-start(bf16[32,2432]{1,0:T(8,128)(2,1)S(1)} %get-tuple-element.72), channel_id=1, source_target_pairs={{0,2},{1,5},{2,0},{3,7},{4,6},{5,1},{6,4},{7,3},{8,10},{9,13},{10,... | collective-permute-start | bytes 466952 | tf_op jit(solution)/shard_map/ppermute | solution.py:60
  64.6 4.7 %collective-permute-start.19 = (bf16[16,2304]{1,0:T(8,128)(2,1)S(1)}, bf16[16,2304]{1,0:T(8,128)(2,1)S(1)}, u32[]{:S(2)}, u32[]{:S(2)}) collective-permute-start(bf16[16,2304]{1,0:T(8,128)(2,1)S(1)} %get-tuple-element.90), channel_id=1, source_target_pairs={{0,8},{1,9},{2,10},{3,11},{4,12},{5,13},{6,14},{7,15},{8,0},{9,1},... | collective-permute-start | bytes 221192 | tf_op jit(solution)/shard_map/ppermute | solution.py:60
  69.3 7.9 %collective-permute-start.20 = (bf16[16,2432]{1,0:T(8,128)(2,1)S(1)}, bf16[16,2432]{1,0:T(8,128)(2,1)S(1)}, u32[]{:S(2)}, u32[]{:S(2)}) collective-permute-start(bf16[16,2432]{1,0:T(8,128)(2,1)S(1)} %fusion.52), channel_id=1, source_target_pairs={{0,16},{1,17},{2,18},{3,19},{4,20},{5,21},{6,22},{7,23},{8,24},{9,... | collective-permute-start | bytes 233480 | tf_op jit(solution)/shard_map/ppermute | solution.py:60
  73.7 5.5 %collective-permute-start.4 = (bf16[16,2432]{1,0:T(8,128)(2,1)S(1)}, bf16[16,2432]{1,0:T(8,128)(2,1)S(1)}, u32[]{:S(2)}, u32[]{:S(2)}) collective-permute-start(bf16[16,2432]{1,0:T(8,128)(2,1)S(1)} %pad_maximum_fusion.10), channel_id=1, source_target_pairs={{0,16},{1,17},{2,18},{3,19},{4,20},{5,21},{6,22},{7,23},{8,24},{9,... | collective-permute-start | bytes 233480 | tf_op jit(solution)/shard_map/ppermute | solution.py:60
  73.8 7.1 %collective-permute-start.12 = (bf16[16,2432]{1,0:T(8,128)(2,1)S(1)}, bf16[16,2432]{1,0:T(8,128)(2,1)S(1)}, u32[]{:S(2)}, u32[]{:S(2)}) collective-permute-start(bf16[16,2432]{1,0:T(8,128)(2,1)S(1)} %pad_maximum_fusion.11), channel_id=1, source_target_pairs={{0,16},{1,17},{2,18},{3,19},{4,20},{5,21},{6,22},{7,23},{8,24},{9,... | collective-permute-start | bytes 233480 | tf_op jit(solution)/shard_map/ppermute | solution.py:60
  77.2 5.3 %collective-permute-start.21 = (bf16[16,2432]{1,0:T(8,128)(2,1)S(1)}, bf16[16,2432]{1,0:T(8,128)(2,1)S(1)}, u32[]{:S(2)}, u32[]{:S(2)}) collective-permute-start(bf16[16,2432]{1,0:T(8,128)(2,1)S(1)} %add_convert_fusion.28), channel_id=1, source_target_pairs={{0,8},{1,9},{2,10},{3,11},{4,12},{5,13},{6,14},{7,15},{8,0},{9,1},... | collective-permute-start | bytes 233480 | tf_op jit(solution)/shard_map/ppermute | solution.py:60
  82.5 6.5 %collective-permute-start.22 = (bf16[32,2432]{1,0:T(8,128)(2,1)S(1)}, bf16[32,2432]{1,0:T(8,128)(2,1)S(1)}, u32[]{:S(2)}, u32[]{:S(2)}) collective-permute-start(bf16[32,2432]{1,0:T(8,128)(2,1)S(1)} %pad_maximum_fusion.8), channel_id=1, source_target_pairs={{0,4},{1,3},{2,6},{3,1},{4,0},{5,7},{6,2},{7,5},{8,12},{9,11},{10,... | collective-permute-start | bytes 466952 | tf_op jit(solution)/shard_map/ppermute | solution.py:60
  83.7 8.6 %collective-permute-start.6 = (bf16[32,2432]{1,0:T(8,128)(2,1)S(1)}, bf16[32,2432]{1,0:T(8,128)(2,1)S(1)}, u32[]{:S(2)}, u32[]{:S(2)}) collective-permute-start(bf16[32,2432]{1,0:T(8,128)(2,1)S(1)} %pad_maximum_fusion.6), channel_id=1, source_target_pairs={{0,4},{1,3},{2,6},{3,1},{4,0},{5,7},{6,2},{7,5},{8,12},{9,11},{10,... | collective-permute-start | bytes 466952 | tf_op jit(solution)/shard_map/ppermute | solution.py:60
  85.4 10.3 %collective-permute-start.14 = (bf16[32,2432]{1,0:T(8,128)(2,1)S(1)}, bf16[32,2432]{1,0:T(8,128)(2,1)S(1)}, u32[]{:S(2)}, u32[]{:S(2)}) collective-permute-start(bf16[32,2432]{1,0:T(8,128)(2,1)S(1)} %pad_maximum_fusion.7), channel_id=1, source_target_pairs={{0,4},{1,3},{2,6},{3,1},{4,0},{5,7},{6,2},{7,5},{8,12},{9,11},{10,... | collective-permute-start | bytes 466952 | tf_op jit(solution)/shard_map/ppermute | solution.py:60
  89.0 8.8 %collective-permute-start.23 = (bf16[64,2432]{1,0:T(8,128)(2,1)S(1)}, bf16[64,2432]{1,0:T(8,128)(2,1)S(1)}, u32[]{:S(2)}, u32[]{:S(2)}) collective-permute-start(bf16[64,2432]{1,0:T(8,128)(2,1)S(1)} %pad_maximum_fusion.5), channel_id=1, source_target_pairs={{0,2},{1,5},{2,0},{3,7},{4,6},{5,1},{6,4},{7,3},{8,10},{9,13},{10,... | collective-permute-start | bytes 933896 | tf_op jit(solution)/shard_map/ppermute | solution.py:60
  92.4 7.0 %collective-permute-start.7 = (bf16[64,2432]{1,0:T(8,128)(2,1)S(1)}, bf16[64,2432]{1,0:T(8,128)(2,1)S(1)}, u32[]{:S(2)}, u32[]{:S(2)}) collective-permute-start(bf16[64,2432]{1,0:T(8,128)(2,1)S(1)} %pad_maximum_fusion.3), channel_id=1, source_target_pairs={{0,2},{1,5},{2,0},{3,7},{4,6},{5,1},{6,4},{7,3},{8,10},{9,13},{10,... | collective-permute-start | bytes 933896 | tf_op jit(solution)/shard_map/ppermute | solution.py:60
  95.7 7.0 %collective-permute-start.15 = (bf16[64,2432]{1,0:T(8,128)(2,1)S(1)}, bf16[64,2432]{1,0:T(8,128)(2,1)S(1)}, u32[]{:S(2)}, u32[]{:S(2)}) collective-permute-start(bf16[64,2432]{1,0:T(8,128)(2,1)S(1)} %pad_maximum_fusion.4), channel_id=1, source_target_pairs={{0,2},{1,5},{2,0},{3,7},{4,6},{5,1},{6,4},{7,3},{8,10},{9,13},{10,... | collective-permute-start | bytes 933896 | tf_op jit(solution)/shard_map/ppermute | solution.py:60
  97.9 5.9 %collective-permute-start.26 = (bf16[128,2432]{1,0:T(8,128)(2,1)S(1)}, bf16[128,2432]{1,0:T(8,128)(2,1)S(1)}, u32[]{:S(2)}, u32[]{:S(2)}) collective-permute-start(bf16[128,2432]{1,0:T(8,128)(2,1)S(1)} %pad_maximum_fusion.2), channel_id=1, source_target_pairs={{0,1},{1,0},{2,3},{3,2},{4,5},{5,4},{6,7},{7,6},{8,9},{9,8},{10,11... | collective-permute-start | bytes 1867784 | tf_op jit(solution)/shard_map/ppermute | solution.py:60
  99.6 5.0 %collective-permute-start.24 = (bf16[128,2432]{1,0:T(8,128)(2,1)S(1)}, bf16[128,2432]{1,0:T(8,128)(2,1)S(1)}, u32[]{:S(2)}, u32[]{:S(2)}) collective-permute-start(bf16[128,2432]{1,0:T(8,128)(2,1)S(1)} %get-tuple-element.52), channel_id=1, source_target_pairs={{0,1},{1,0},{2,3},{3,2},{4,5},{5,4},{6,7},{7,6},{8,9},{9,8},{10,11... | collective-permute-start | bytes 1867784 | tf_op jit(solution)/shard_map/ppermute | solution.py:60
  109.9 6.8 %collective-permute-start.38 = (bf16[64,2304]{1,0:T(8,128)(2,1)S(1)}, bf16[64,2304]{1,0:T(8,128)(2,1)S(1)}, u32[]{:S(2)}, u32[]{:S(2)}) collective-permute-start(bf16[64,2304]{1,0:T(8,128)(2,1)S(1)} %get-tuple-element.64), channel_id=1, source_target_pairs={{0,2},{1,5},{2,0},{3,7},{4,6},{5,1},{6,4},{7,3},{8,10},{9,13},{10,... | collective-permute-start | bytes 884744 | tf_op jit(solution)/shard_map/ppermute | solution.py:60
  112.2 8.4 %collective-permute-start.28 = (bf16[64,2432]{1,0:T(8,128)(2,1)S(1)}, bf16[64,2432]{1,0:T(8,128)(2,1)S(1)}, u32[]{:S(2)}, u32[]{:S(2)}) collective-permute-start(bf16[64,2432]{1,0:T(8,128)(2,1)S(1)} %get-tuple-element.56), channel_id=1, source_target_pairs={{0,8},{1,9},{2,10},{3,11},{4,12},{5,13},{6,14},{7,15},{8,0},{9,1},... | collective-permute-start | bytes 933896 | tf_op jit(solution)/shard_map/ppermute | solution.py:60
  113.2 9.5 %collective-permute-start.33 = (bf16[64,2432]{1,0:T(8,128)(2,1)S(1)}, bf16[64,2432]{1,0:T(8,128)(2,1)S(1)}, u32[]{:S(2)}, u32[]{:S(2)}) collective-permute-start(bf16[64,2432]{1,0:T(8,128)(2,1)S(1)} %get-tuple-element.58), channel_id=1, source_target_pairs={{0,2},{1,5},{2,0},{3,7},{4,6},{5,1},{6,4},{7,3},{8,10},{9,13},{10,... | collective-permute-start | bytes 933896 | tf_op jit(solution)/shard_map/ppermute | solution.py:60
  116.8 7.1 %collective-permute-start.39 = (bf16[32,2304]{1,0:T(8,128)(2,1)S(1)}, bf16[32,2304]{1,0:T(8,128)(2,1)S(1)}, u32[]{:S(2)}, u32[]{:S(2)}) collective-permute-start(bf16[32,2304]{1,0:T(8,128)(2,1)S(1)} %get-tuple-element.76), channel_id=1, source_target_pairs={{0,4},{1,3},{2,6},{3,1},{4,0},{5,7},{6,2},{7,5},{8,12},{9,11},{10,... | collective-permute-start | bytes 442376 | tf_op jit(solution)/shard_map/ppermute | solution.py:60
  120.6 6.9 %collective-permute-start.29 = (bf16[32,2432]{1,0:T(8,128)(2,1)S(1)}, bf16[32,2432]{1,0:T(8,128)(2,1)S(1)}, u32[]{:S(2)}, u32[]{:S(2)}) collective-permute-start(bf16[32,2432]{1,0:T(8,128)(2,1)S(1)} %get-tuple-element.68), channel_id=1, source_target_pairs={{0,2},{1,5},{2,0},{3,7},{4,6},{5,1},{6,4},{7,3},{8,10},{9,13},{10,... | collective-permute-start | bytes 466952 | tf_op jit(solution)/shard_map/ppermute | solution.py:60
  122.8 6.6 %collective-permute-start.34 = (bf16[32,2432]{1,0:T(8,128)(2,1)S(1)}, bf16[32,2432]{1,0:T(8,128)(2,1)S(1)}, u32[]{:S(2)}, u32[]{:S(2)}) collective-permute-start(bf16[32,2432]{1,0:T(8,128)(2,1)S(1)} %get-tuple-element.70), channel_id=1, source_target_pairs={{0,4},{1,3},{2,6},{3,1},{4,0},{5,7},{6,2},{7,5},{8,12},{9,11},{10,... | collective-permute-start | bytes 466952 | tf_op jit(solution)/shard_map/ppermute | solution.py:60
  123.9 4.5 %collective-permute-start.40 = (bf16[16,2304]{1,0:T(8,128)(2,1)S(1)}, bf16[16,2304]{1,0:T(8,128)(2,1)S(1)}, u32[]{:S(2)}, u32[]{:S(2)}) collective-permute-start(bf16[16,2304]{1,0:T(8,128)(2,1)S(1)} %get-tuple-element.88), channel_id=1, source_target_pairs={{0,8},{1,9},{2,10},{3,11},{4,12},{5,13},{6,14},{7,15},{8,0},{9,1},... | collective-permute-start | bytes 221192 | tf_op jit(solution)/shard_map/ppermute | solution.py:60
  127.5 6.2 %collective-permute-start.30 = (bf16[16,2432]{1,0:T(8,128)(2,1)S(1)}, bf16[16,2432]{1,0:T(8,128)(2,1)S(1)}, u32[]{:S(2)}, u32[]{:S(2)}) collective-permute-start(bf16[16,2432]{1,0:T(8,128)(2,1)S(1)} %get-tuple-element.80), channel_id=1, source_target_pairs={{0,4},{1,3},{2,6},{3,1},{4,0},{5,7},{6,2},{7,5},{8,12},{9,11},{10,... | collective-permute-start | bytes 233480 | tf_op jit(solution)/shard_map/ppermute | solution.py:60
  128.4 5.3 %collective-permute-start.41 = (bf16[8,2304]{1,0:T(8,128)(2,1)S(1)}, bf16[8,2304]{1,0:T(8,128)(2,1)S(1)}, u32[]{:S(2)}, u32[]{:S(2)}) collective-permute-start(bf16[8,2304]{1,0:T(8,128)(2,1)S(1)} %add_convert_fusion.48), channel_id=1, source_target_pairs={{0,16},{1,17},{2,18},{3,19},{4,20},{5,21},{6,22},{7,23},{8,24},{9,... | collective-permute-start | bytes 110600 | tf_op jit(solution)/shard_map/ppermute | solution.py:60
  129.4 5.0 %collective-permute-start.35 = (bf16[16,2432]{1,0:T(8,128)(2,1)S(1)}, bf16[16,2432]{1,0:T(8,128)(2,1)S(1)}, u32[]{:S(2)}, u32[]{:S(2)}) collective-permute-start(bf16[16,2432]{1,0:T(8,128)(2,1)S(1)} %get-tuple-element.82), channel_id=1, source_target_pairs={{0,8},{1,9},{2,10},{3,11},{4,12},{5,13},{6,14},{7,15},{8,0},{9,1},... | collective-permute-start | bytes 233480 | tf_op jit(solution)/shard_map/ppermute | solution.py:60
  133.8 5.3 %collective-permute-start.31 = (bf16[8,2432]{1,0:T(8,128)(2,1)S(1)}, bf16[8,2432]{1,0:T(8,128)(2,1)S(1)}, u32[]{:S(2)}, u32[]{:S(2)}) collective-permute-start(bf16[8,2432]{1,0:T(8,128)(2,1)S(1)} %add_convert_fusion.42), channel_id=1, source_target_pairs={{0,16},{1,17},{2,18},{3,19},{4,20},{5,21},{6,22},{7,23},{8,24},{9,... | collective-permute-start | bytes 116744 | tf_op jit(solution)/shard_map/ppermute | solution.py:60
  134.4 5.1 %collective-permute-start.36 = (bf16[8,2432]{1,0:T(8,128)(2,1)S(1)}, bf16[8,2432]{1,0:T(8,128)(2,1)S(1)}, u32[]{:S(2)}, u32[]{:S(2)}) collective-permute-start(bf16[8,2432]{1,0:T(8,128)(2,1)S(1)} %add_convert_fusion.40), channel_id=1, source_target_pairs={{0,16},{1,17},{2,18},{3,19},{4,20},{5,21},{6,22},{7,23},{8,24},{9,... | collective-permute-start | bytes 116744 | tf_op jit(solution)/shard_map/ppermute | solution.py:60
  (22 other events, 126.7 us)

commit v5 on v4

--- a/solution.py
+++ b/solution.py
@@ -15,7 +15,6 @@
 COLUMNS = 640
 ATTEND_VMEM = 56 << 20
 PROJECT_VMEM = 32 << 20
-FETCH_VMEM = 56 << 20
 
 
 score_scale = 192.0 ** (-0.5)
@@ -150,34 +149,6 @@
             transcendentals=tokens * heads * cached,
         ),
     )(lengths, q_latent, q_rope.reshape(tokens, heads, turned), cache_latent, cache_rope)
-
-
-def fetch_kernel(after_ref, gate_ref, up_ref, down_ref, both_held, down_held, done):
-    width = gate_ref.shape[2]
-    copies = [
-        pltpu.make_async_copy(gate_ref.at[0], both_held.at[:, :width], done.at[0]),
-        pltpu.make_async_copy(up_ref.at[0], both_held.at[:, width:], done.at[1]),
-        pltpu.make_async_copy(down_ref.at[0], down_held, done.at[2]),
-    ]
-    for copy in copies:
-        copy.start()
-    for copy in copies:
-        copy.wait()
-
-
-def fetch(after, gate_weight, up_weight, down_projection_weight):
-    _, model_width, width = gate_weight.shape
-    shapes = [(model_width, 2 * width), (width, model_width)]
-    size = sum(2 * a * b for a, b in shapes)
-    return pl.pallas_call(
-        fetch_kernel,
-        out_shape=[jax.ShapeDtypeStruct(shape, bf16) for shape in shapes],
-        in_specs=[pl.BlockSpec(memory_space=pl.ANY)] * 4,
-        out_specs=[pl.BlockSpec(memory_space=pltpu.VMEM)] * 2,
-        scratch_shapes=[pltpu.SemaphoreType.DMA((3,))],
-        compiler_params=pltpu.CompilerParams(vmem_limit_bytes=FETCH_VMEM),
-        cost_estimate=pl.CostEstimate(flops=0, bytes_accessed=2 * size, transcendentals=0),
-    )(after, gate_weight, up_weight, down_projection_weight)
 
 
 def project_kernel(start, values_ref, weight_ref, keep_ref, send_ref):
@@ -241,13 +212,16 @@
     route_weights = route_scale * sigm / jnp.sum(sigm, axis=1, keepdims=True)
 
     latent_out = attend(q_latent, q_rope, cache_latent, cache_rope, lengths)
-    both_near, down_near = fetch(latent_out, gate_weight, up_weight, down_projection_weight)
-    _, out_after = lax.optimization_barrier((latent_out, out_weight))
+    _, out_after, down_after, gate_after, up_after = lax.optimization_barrier(
+        (latent_out, out_weight, down_projection_weight, gate_weight, up_weight)
+    )
+    both_near = jnp.concatenate([gate_after[0], up_after[0]], axis=1)
     out_near = [out_after[:, start : start + size] for start, size in plans]
-    value_up_weight, both_near, down_near, *out_near = lax.optimization_barrier(
-        (value_up_weight, both_near, down_near, *out_near)
-    )
+    down_near = [down_after[0, :, start : start + size] for start, size in plans]
     by_head = lax.all_to_all(latent_out, "expert", split_axis=0, concat_axis=0, tiled=True)
+    by_head, both_near, out_near, down_near = lax.optimization_barrier(
+        (by_head, both_near, out_near, down_near)
+    )
     heads_here = value_up_weight.shape[0]
     by_head = by_head.reshape(devices, heads_here, tokens_here, -1)
     head_values = jnp.einsum(
@@ -324,7 +298,7 @@
         if orders[i] != sorted(orders[i]):
             move = np.eye(rows, dtype=np.float32)[place_rows(orders[i], rows)]
             acts = jnp.dot(jnp.asarray(move, bf16), hidden, preferred_element_type=f32).astype(bf16)
-        keep, send = project(acts, down_near, start, size)
+        keep, send = project(acts, down_near[i], 0, size)
         own, partners = halve(keep, send, sum_stages[i], devices)
         came = swap(partners, stages[-1], devices)
         total = base[:tokens_here, :size].astype(f32) + own + came.astype(f32)

time: 141 us -> 140 us (level)
  Pallas kernels: 16.3 us -> 11.2 us
  other arithmetic: 4.42 us -> 8.14 us
  local copies, waits for them, and re-layouts: 11.3 us -> 12.8 us
    pallas_call x1 -> x0, Pallas kernels: 5.05 us -> none  [fetch(): pl.pallas_call(fetch_kernel, out_shape=[jax.ShapeDtypeStruct(shape, bf16)...]
    concatenate x0 -> x1, other arithmetic: none -> 3.7 us  [shards(): both_near = jnp.concatenate([gate_after[0], up_after[0]], axis=1)]
    squeeze x0 -> x2, local copies, waits for them, and re-layouts: none -> 2.06 us  [shards(): down_near = [down_after[0, :, start:start + size] for start, size in plans]]
  transfers between devices with their start and end apart: 43 -> 43, of which waited for: 25 -> 22; matrix products, arithmetic and copies ran while one was open for 9% -> 14% of each run, Pallas kernels for 6% -> 2%
where the time goes in v5:
time: 140 us
  waiting for transfers between devices  54.6 us (39%)
  starting transfers between devices  47.5 us (34%)
  local copies, waits for them, and re-layouts  12.8 us (9%)
  Pallas kernels  11.2 us (8%)
  other arithmetic  8.14 us (6%)
  matrix products  4.74 us (3%)
    ppermute x42, waiting for transfers between devices, swap(): return lax.ppermute(x, 'expert', pairs)  42.2 us
    ppermute x42, starting transfers between devices, swap(): return lax.ppermute(x, 'expert', pairs)  40 us
    all_to_all x1, waiting for transfers between devices, shards(): lax.all_to_all(latent_out, 'expert', split_axis=0, concat_axis=0, tiled=T...  12.4 us
    slice x2, local copies, waits for them, and re-layouts, shards(): out_near = [out_after[:, start:start + size] for start, size in plans]  7.71 us
    all_to_all x1, starting transfers between devices, shards(): lax.all_to_all(latent_out, 'expert', split_axis=0, concat_axis=0, tiled=T...  7.42 us
    pallas_call x1, Pallas kernels, attend(): pl.pallas_call(attend_kernel, grid=(tokens // group,), out_shape=jax.Shap...  7.09 us
    pallas_call x6, Pallas kernels, project(): pl.pallas_call(functools.partial(project_kernel, start), out_shape=[half,...  4.14 us
    concatenate x1, other arithmetic, shards(): both_near = jnp.concatenate([gate_after[0], up_after[0]], axis=1)  3.7 us
  transfers between devices with their start and end apart: 43, of which 22 were waited for; matrix products, arithmetic and copies ran while one was open for 14% of the time, Pallas kernels for 2%

profile of v5, /device:TPU:0, one launch (start us, length us, event | category | flops | bytes accessed | tf_op | source)
XLA Modules:
  0.0 139.6 jit_solution(4930479710234201274)
XLA Ops:
  0.0 2.0 %reshape.121.rope_ref = bf16[8,128,64]{2,1,0:T(8,128)(2,1)} reshape(bf16[8,8192]{1,0:T(8,128)(2,1)} %param.17) | data formatting | bytes 262144 | tf_op jit(solution)/shard_map/reshape | solution.py:151
  2.0 7.1 %shard_map.145 = bf16[128,8,512]{2,1,0:T(8,128)(2,1)} custom-call(s32[8]{0:T(128)} %lengths_ref.1, bf16[8,128,512]{2,1,0:T(8,128)(2,1)} %latent_ref.1, bf16[8,128,64]{2,1,0:T(8,128)(2,1)} %reshape.121.rope_ref, bf16[8,256,512]{2,1,0:T(8,128)(2,1)} %keys_ref.1, bf16[8,64,256]{2,1,0:T(8,128)(2,1)} %turned_ref.1), custom_call_target="tpu_custom_call" | custom-call | flops 570425344 | bytes 4456448 | tf_op jit(solution)/shard_map/pallas_call | solution.py:132
  9.0 7.4 %all-to-all-start = ((bf16[128,8,512]{2,1,0:T(8,128)(2,1)}), bf16[128,8,512]{2,1,0:T(8,128)(2,1)}, u32[]{:S(2)}, u32[]{:S(2)}) async-start(bf16[128,8,512]{2,1,0:T(8,128)(2,1)} %shard_map.145), calls=%async_computation | async-start | bytes 2097152 | tf_op jit(solution)/shard_map/all_to_all | solution.py:221
  18.8 3.4 %slice.377.weight_ref = bf16[512,2304]{1,0:T(8,128)(2,1)} slice(bf16[512,7168]{1,0:T(8,128)(2,1)} %param.22), slice={[0:512], [4864:7168]} | slice | bytes 4718592 | tf_op jit(solution)/shard_map/slice | solution.py:219
  22.3 3.7 %pad_maximum_fusion = bf16[7168,256]{1,0:T(8,128)(2,1)} fusion(bf16[7168,128]{1,0:T(8,128)(2,1)S(1)} %bitcast.27, bf16[7168,128]{1,0:T(8,128)(2,1)} %bitcast.28), kind=kLoop, calls=%fused_computation | loop fusion | flops 7340032 | bytes 7340032 | tf_op jit(solution)/shard_map/concatenate | solution.py:218
  26.0 4.3 %fusion.67 = (bf16[512,2432]{1,0:T(8,128)(2,1)S(1)}, bf16[512,2432]{1,0:T(8,128)(2,1)}) fusion(bf16[512,7168]{1,0:T(8,128)(2,1)} %param.22), kind=kLoop, calls=%fused_computation.182 | loop fusion | bytes 9961472 | tf_op jit(solution)/shard_map/slice | solution.py:219
  30.3 12.4 %all-to-all-done = bf16[128,8,512]{2,1,0:T(8,128)(2,1)} async-done(((bf16[128,8,512]{2,1,0:T(8,128)(2,1)}), bf16[128,8,512]{2,1,0:T(8,128)(2,1)}, u32[]{:S(2)}, u32[]{:S(2)}) %all-to-all-start) | async-done | bytes 1048608 | tf_op jit(solution)/shard_map/all_to_all | solution.py:221
  42.7 1.8 %fusion.12 = bf16[32,8,4,128]{3,1,0,2:T(8,128)(2,1)S(1)} fusion(bf16[32,4,8,512]{3,2,1,0:T(8,128)(2,1)} %bitcast.5, bf16[4,512,128]{2,1,0:T(8,128)(2,1)S(1)} %copy-done), kind=kOutput, calls=%fused_computation.28 | convolution fusion | flops 134348800 | bytes 1835008 | tf_op jit(solution)/shard_map/sqtg,qge->stqe/dot_general | solution.py:227
  52.4 3.5 %collective-permute-done.17 = bf16[64,2304]{1,0:T(8,128)(2,1)S(1)} collective-permute-done((bf16[64,2304]{1,0:T(8,128)(2,1)S(1)}, bf16[64,2304]{1,0:T(8,128)(2,1)S(1)}, u32[]{:S(2)}, u32[]{:S(2)}) %collective-permute-start.17) | collective-permute-done | bytes 294944 | tf_op jit(solution)/shard_map/ppermute | solution.py:59
  57.5 2.4 %collective-permute-done.1 = bf16[64,2432]{1,0:T(8,128)(2,1)S(1)} collective-permute-done((bf16[64,2432]{1,0:T(8,128)(2,1)S(1)}, bf16[64,2432]{1,0:T(8,128)(2,1)S(1)}, u32[]{:S(2)}, u32[]{:S(2)}) %collective-permute-start.1) | collective-permute-done | bytes 311328 | tf_op jit(solution)/shard_map/ppermute | solution.py:59
  63.3 2.6 %collective-permute-done.2 = bf16[32,2432]{1,0:T(8,128)(2,1)S(1)} collective-permute-done((bf16[32,2432]{1,0:T(8,128)(2,1)S(1)}, bf16[32,2432]{1,0:T(8,128)(2,1)S(1)}, u32[]{:S(2)}, u32[]{:S(2)}) %collective-permute-start.2) | collective-permute-done | bytes 155680 | tf_op jit(solution)/shard_map/ppermute | solution.py:59
  65.9 1.9 %collective-permute-start.3 = (bf16[16,2432]{1,0:T(8,128)(2,1)S(1)}, bf16[16,2432]{1,0:T(8,128)(2,1)S(1)}, u32[]{:S(2)}, u32[]{:S(2)}) collective-permute-start(bf16[16,2432]{1,0:T(8,128)(2,1)S(1)} %get-tuple-element.92), channel_id=1, source_target_pairs={{0,4},{1,3},{2,6},{3,1},{4,0},{5,7},{6,2},{7,5},{8,12},{9,11},{10,... | collective-permute-start | bytes 233480 | tf_op jit(solution)/shard_map/ppermute | solution.py:59
  68.0 2.1 %collective-permute-start.20 = (bf16[16,2432]{1,0:T(8,128)(2,1)S(1)}, bf16[16,2432]{1,0:T(8,128)(2,1)S(1)}, u32[]{:S(2)}, u32[]{:S(2)}) collective-permute-start(bf16[16,2432]{1,0:T(8,128)(2,1)S(1)} %fusion.52), channel_id=1, source_target_pairs={{0,16},{1,17},{2,18},{3,19},{4,20},{5,21},{6,22},{7,23},{8,24},{9,... | collective-permute-start | bytes 233480 | tf_op jit(solution)/shard_map/ppermute | solution.py:59
  70.4 1.9 %collective-permute-done.11 = bf16[16,2432]{1,0:T(8,128)(2,1)S(1)} collective-permute-done((bf16[16,2432]{1,0:T(8,128)(2,1)S(1)}, bf16[16,2432]{1,0:T(8,128)(2,1)S(1)}, u32[]{:S(2)}, u32[]{:S(2)}) %collective-permute-start.11) | collective-permute-done | bytes 77856 | tf_op jit(solution)/shard_map/ppermute | solution.py:59
  72.4 1.8 %collective-permute-start.12 = (bf16[16,2432]{1,0:T(8,128)(2,1)S(1)}, bf16[16,2432]{1,0:T(8,128)(2,1)S(1)}, u32[]{:S(2)}, u32[]{:S(2)}) collective-permute-start(bf16[16,2432]{1,0:T(8,128)(2,1)S(1)} %pad_maximum_fusion.12), channel_id=1, source_target_pairs={{0,16},{1,17},{2,18},{3,19},{4,20},{5,21},{6,22},{7,23},{8,24},{9,... | collective-permute-start | bytes 233480 | tf_op jit(solution)/shard_map/ppermute | solution.py:59
  76.8 2.3 %collective-permute-done.12 = bf16[16,2432]{1,0:T(8,128)(2,1)S(1)} collective-permute-done((bf16[16,2432]{1,0:T(8,128)(2,1)S(1)}, bf16[16,2432]{1,0:T(8,128)(2,1)S(1)}, u32[]{:S(2)}, u32[]{:S(2)}) %collective-permute-start.12) | collective-permute-done | bytes 77856 | tf_op jit(solution)/shard_map/ppermute | solution.py:59
  80.0 2.8 %collective-permute-start.5 = (bf16[16,2432]{1,0:T(8,128)(2,1)S(1)}, bf16[16,2432]{1,0:T(8,128)(2,1)S(1)}, u32[]{:S(2)}, u32[]{:S(2)}) collective-permute-start(bf16[16,2432]{1,0:T(8,128)(2,1)S(1)} %add_convert_fusion.32), channel_id=1, source_target_pairs={{0,8},{1,9},{2,10},{3,11},{4,12},{5,13},{6,14},{7,15},{8,0},{9,1},... | collective-permute-start | bytes 233480 | tf_op jit(solution)/shard_map/ppermute | solution.py:59
  83.7 2.0 %collective-permute-start.14 = (bf16[32,2432]{1,0:T(8,128)(2,1)S(1)}, bf16[32,2432]{1,0:T(8,128)(2,1)S(1)}, u32[]{:S(2)}, u32[]{:S(2)}) collective-permute-start(bf16[32,2432]{1,0:T(8,128)(2,1)S(1)} %pad_maximum_fusion.8), channel_id=1, source_target_pairs={{0,4},{1,3},{2,6},{3,1},{4,0},{5,7},{6,2},{7,5},{8,12},{9,11},{10,... | collective-permute-start | bytes 466952 | tf_op jit(solution)/shard_map/ppermute | solution.py:59
  89.3 2.1 %collective-permute-done.14 = bf16[32,2432]{1,0:T(8,128)(2,1)S(1)} collective-permute-done((bf16[32,2432]{1,0:T(8,128)(2,1)S(1)}, bf16[32,2432]{1,0:T(8,128)(2,1)S(1)}, u32[]{:S(2)}, u32[]{:S(2)}) %collective-permute-start.14) | collective-permute-done | bytes 155680 | tf_op jit(solution)/shard_map/ppermute | solution.py:59
  91.4 1.6 %collective-permute-start.15 = (bf16[64,2432]{1,0:T(8,128)(2,1)S(1)}, bf16[64,2432]{1,0:T(8,128)(2,1)S(1)}, u32[]{:S(2)}, u32[]{:S(2)}) collective-permute-start(bf16[64,2432]{1,0:T(8,128)(2,1)S(1)} %pad_maximum_fusion.5), channel_id=1, source_target_pairs={{0,2},{1,5},{2,0},{3,7},{4,6},{5,1},{6,4},{7,3},{8,10},{9,13},{10,... | collective-permute-start | bytes 933896 | tf_op jit(solution)/shard_map/ppermute | solution.py:59
  93.0 1.7 %collective-permute-done.6 = bf16[32,2432]{1,0:T(8,128)(2,1)S(1)} collective-permute-done((bf16[32,2432]{1,0:T(8,128)(2,1)S(1)}, bf16[32,2432]{1,0:T(8,128)(2,1)S(1)}, u32[]{:S(2)}, u32[]{:S(2)}) %collective-permute-start.6) | collective-permute-done | bytes 155680 | tf_op jit(solution)/shard_map/ppermute | solution.py:59
  94.7 1.6 %collective-permute-start.7 = (bf16[64,2432]{1,0:T(8,128)(2,1)S(1)}, bf16[64,2432]{1,0:T(8,128)(2,1)S(1)}, u32[]{:S(2)}, u32[]{:S(2)}) collective-permute-start(bf16[64,2432]{1,0:T(8,128)(2,1)S(1)} %pad_maximum_fusion.4), channel_id=1, source_target_pairs={{0,2},{1,5},{2,0},{3,7},{4,6},{5,1},{6,4},{7,3},{8,10},{9,13},{10,... | collective-permute-start | bytes 933896 | tf_op jit(solution)/shard_map/ppermute | solution.py:59
  98.7 3.1 %collective-permute-done.7 = bf16[64,2432]{1,0:T(8,128)(2,1)S(1)} collective-permute-done((bf16[64,2432]{1,0:T(8,128)(2,1)S(1)}, bf16[64,2432]{1,0:T(8,128)(2,1)S(1)}, u32[]{:S(2)}, u32[]{:S(2)}) %collective-permute-start.7) | collective-permute-done | bytes 311328 | tf_op jit(solution)/shard_map/ppermute | solution.py:59
  111.4 4.1 %collective-permute-done.38 = bf16[64,2304]{1,0:T(8,128)(2,1)S(1)} collective-permute-done((bf16[64,2304]{1,0:T(8,128)(2,1)S(1)}, bf16[64,2304]{1,0:T(8,128)(2,1)S(1)}, u32[]{:S(2)}, u32[]{:S(2)}) %collective-permute-start.38) | collective-permute-done | bytes 294944 | tf_op jit(solution)/shard_map/ppermute | solution.py:59
  116.7 3.2 %collective-permute-done.33 = bf16[64,2432]{1,0:T(8,128)(2,1)S(1)} collective-permute-done((bf16[64,2432]{1,0:T(8,128)(2,1)S(1)}, bf16[64,2432]{1,0:T(8,128)(2,1)S(1)}, u32[]{:S(2)}, u32[]{:S(2)}) %collective-permute-start.33) | collective-permute-done | bytes 311328 | tf_op jit(solution)/shard_map/ppermute | solution.py:59
  120.9 2.4 %collective-permute-start.29 = (bf16[32,2432]{1,0:T(8,128)(2,1)S(1)}, bf16[32,2432]{1,0:T(8,128)(2,1)S(1)}, u32[]{:S(2)}, u32[]{:S(2)}) collective-permute-start(bf16[32,2432]{1,0:T(8,128)(2,1)S(1)} %get-tuple-element.76), channel_id=1, source_target_pairs={{0,2},{1,5},{2,0},{3,7},{4,6},{5,1},{6,4},{7,3},{8,10},{9,13},{10,... | collective-permute-start | bytes 466952 | tf_op jit(solution)/shard_map/ppermute | solution.py:59
  123.3 2.4 %collective-permute-done.34 = bf16[32,2432]{1,0:T(8,128)(2,1)S(1)} collective-permute-done((bf16[32,2432]{1,0:T(8,128)(2,1)S(1)}, bf16[32,2432]{1,0:T(8,128)(2,1)S(1)}, u32[]{:S(2)}, u32[]{:S(2)}) %collective-permute-start.34) | collective-permute-done | bytes 155680 | tf_op jit(solution)/shard_map/ppermute | solution.py:59
  126.0 1.7 %collective-permute-done.40 = bf16[16,2304]{1,0:T(8,128)(2,1)S(1)} collective-permute-done((bf16[16,2304]{1,0:T(8,128)(2,1)S(1)}, bf16[16,2304]{1,0:T(8,128)(2,1)S(1)}, u32[]{:S(2)}, u32[]{:S(2)}) %collective-permute-start.40) | collective-permute-done | bytes 73760 | tf_op jit(solution)/shard_map/ppermute | solution.py:59
  128.4 1.6 %collective-permute-start.30 = (bf16[16,2432]{1,0:T(8,128)(2,1)S(1)}, bf16[16,2432]{1,0:T(8,128)(2,1)S(1)}, u32[]{:S(2)}, u32[]{:S(2)}) collective-permute-start(bf16[16,2432]{1,0:T(8,128)(2,1)S(1)} %get-tuple-element.88), channel_id=1, source_target_pairs={{0,4},{1,3},{2,6},{3,1},{4,0},{5,7},{6,2},{7,5},{8,12},{9,11},{10,... | collective-permute-start | bytes 233480 | tf_op jit(solution)/shard_map/ppermute | solution.py:59
  130.0 3.5 %collective-permute-done.41 = bf16[8,2304]{1,0:T(8,128)(2,1)S(1)} collective-permute-done((bf16[8,2304]{1,0:T(8,128)(2,1)S(1)}, bf16[8,2304]{1,0:T(8,128)(2,1)S(1)}, u32[]{:S(2)}, u32[]{:S(2)}) %collective-permute-start.41) | collective-permute-done | bytes 36896 | tf_op jit(solution)/shard_map/ppermute | solution.py:59
  133.7 2.9 %collective-permute-start.31 = (bf16[8,2432]{1,0:T(8,128)(2,1)S(1)}, bf16[8,2432]{1,0:T(8,128)(2,1)S(1)}, u32[]{:S(2)}, u32[]{:S(2)}) collective-permute-start(bf16[8,2432]{1,0:T(8,128)(2,1)S(1)} %add_convert_fusion.42), channel_id=1, source_target_pairs={{0,16},{1,17},{2,18},{3,19},{4,20},{5,21},{6,22},{7,23},{8,24},{9,... | collective-permute-start | bytes 116744 | tf_op jit(solution)/shard_map/ppermute | solution.py:59
  136.6 1.9 %collective-permute-done.36 = bf16[8,2432]{1,0:T(8,128)(2,1)S(1)} collective-permute-done((bf16[8,2432]{1,0:T(8,128)(2,1)S(1)}, bf16[8,2432]{1,0:T(8,128)(2,1)S(1)}, u32[]{:S(2)}, u32[]{:S(2)}) %collective-permute-start.36) | collective-permute-done | bytes 38944 | tf_op jit(solution)/shard_map/ppermute | solution.py:59
  (173 shorter events, 40.1 us)
Async XLA Ops:
  9.0 33.6 %all-to-all-start = ((bf16[128,8,512]{2,1,0:T(8,128)(2,1)}), bf16[128,8,512]{2,1,0:T(8,128)(2,1)}, u32[]{:S(2)}, u32[]{:S(2)}) async-start(bf16[128,8,512]{2,1,0:T(8,128)(2,1)} %shard_map.145), calls=%async_computation | async-start | bytes 2097152 | tf_op jit(solution)/shard_map/all_to_all | solution.py:221
  49.1 6.8 %collective-permute-start.17 = (bf16[64,2304]{1,0:T(8,128)(2,1)S(1)}, bf16[64,2304]{1,0:T(8,128)(2,1)S(1)}, u32[]{:S(2)}, u32[]{:S(2)}) collective-permute-start(bf16[64,2304]{1,0:T(8,128)(2,1)S(1)} %get-tuple-element.74), channel_id=1, source_target_pairs={{0,2},{1,5},{2,0},{3,7},{4,6},{5,1},{6,4},{7,3},{8,10},{9,13},{10,... | collective-permute-start | bytes 884744 | tf_op jit(solution)/shard_map/ppermute | solution.py:59
  50.8 9.2 %collective-permute-start.1 = (bf16[64,2432]{1,0:T(8,128)(2,1)S(1)}, bf16[64,2432]{1,0:T(8,128)(2,1)S(1)}, u32[]{:S(2)}, u32[]{:S(2)}) collective-permute-start(bf16[64,2432]{1,0:T(8,128)(2,1)S(1)} %get-tuple-element.68), channel_id=1, source_target_pairs={{0,8},{1,9},{2,10},{3,11},{4,12},{5,13},{6,14},{7,15},{8,0},{9,1},... | collective-permute-start | bytes 933896 | tf_op jit(solution)/shard_map/ppermute | solution.py:59
  51.6 10.0 %collective-permute-start.9 = (bf16[64,2432]{1,0:T(8,128)(2,1)S(1)}, bf16[64,2432]{1,0:T(8,128)(2,1)S(1)}, u32[]{:S(2)}, u32[]{:S(2)}) collective-permute-start(bf16[64,2432]{1,0:T(8,128)(2,1)S(1)} %get-tuple-element.70), channel_id=1, source_target_pairs={{0,2},{1,5},{2,0},{3,7},{4,6},{5,1},{6,4},{7,3},{8,10},{9,13},{10,... | collective-permute-start | bytes 933896 | tf_op jit(solution)/shard_map/ppermute | solution.py:59
  56.0 6.4 %collective-permute-start.18 = (bf16[32,2304]{1,0:T(8,128)(2,1)S(1)}, bf16[32,2304]{1,0:T(8,128)(2,1)S(1)}, u32[]{:S(2)}, u32[]{:S(2)}) collective-permute-start(bf16[32,2304]{1,0:T(8,128)(2,1)S(1)} %get-tuple-element.86), channel_id=1, source_target_pairs={{0,4},{1,3},{2,6},{3,1},{4,0},{5,7},{6,2},{7,5},{8,12},{9,11},{10,... | collective-permute-start | bytes 442376 | tf_op jit(solution)/shard_map/ppermute | solution.py:59
  60.1 5.8 %collective-permute-start.2 = (bf16[32,2432]{1,0:T(8,128)(2,1)S(1)}, bf16[32,2432]{1,0:T(8,128)(2,1)S(1)}, u32[]{:S(2)}, u32[]{:S(2)}) collective-permute-start(bf16[32,2432]{1,0:T(8,128)(2,1)S(1)} %get-tuple-element.80), channel_id=1, source_target_pairs={{0,2},{1,5},{2,0},{3,7},{4,6},{5,1},{6,4},{7,3},{8,10},{9,13},{10,... | collective-permute-start | bytes 466952 | tf_op jit(solution)/shard_map/ppermute | solution.py:59
  61.7 6.1 %collective-permute-start.10 = (bf16[32,2432]{1,0:T(8,128)(2,1)S(1)}, bf16[32,2432]{1,0:T(8,128)(2,1)S(1)}, u32[]{:S(2)}, u32[]{:S(2)}) collective-permute-start(bf16[32,2432]{1,0:T(8,128)(2,1)S(1)} %get-tuple-element.82), channel_id=1, source_target_pairs={{0,4},{1,3},{2,6},{3,1},{4,0},{5,7},{6,2},{7,5},{8,12},{9,11},{10,... | collective-permute-start | bytes 466952 | tf_op jit(solution)/shard_map/ppermute | solution.py:59
  62.4 5.5 %collective-permute-start.19 = (bf16[16,2304]{1,0:T(8,128)(2,1)S(1)}, bf16[16,2304]{1,0:T(8,128)(2,1)S(1)}, u32[]{:S(2)}, u32[]{:S(2)}) collective-permute-start(bf16[16,2304]{1,0:T(8,128)(2,1)S(1)} %get-tuple-element.98), channel_id=1, source_target_pairs={{0,8},{1,9},{2,10},{3,11},{4,12},{5,13},{6,14},{7,15},{8,0},{9,1},... | collective-permute-start | bytes 221192 | tf_op jit(solution)/shard_map/ppermute | solution.py:59
  68.0 8.6 %collective-permute-start.20 = (bf16[16,2432]{1,0:T(8,128)(2,1)S(1)}, bf16[16,2432]{1,0:T(8,128)(2,1)S(1)}, u32[]{:S(2)}, u32[]{:S(2)}) collective-permute-start(bf16[16,2432]{1,0:T(8,128)(2,1)S(1)} %fusion.52), channel_id=1, source_target_pairs={{0,16},{1,17},{2,18},{3,19},{4,20},{5,21},{6,22},{7,23},{8,24},{9,... | collective-permute-start | bytes 233480 | tf_op jit(solution)/shard_map/ppermute | solution.py:59
  72.4 6.7 %collective-permute-start.12 = (bf16[16,2432]{1,0:T(8,128)(2,1)S(1)}, bf16[16,2432]{1,0:T(8,128)(2,1)S(1)}, u32[]{:S(2)}, u32[]{:S(2)}) collective-permute-start(bf16[16,2432]{1,0:T(8,128)(2,1)S(1)} %pad_maximum_fusion.12), channel_id=1, source_target_pairs={{0,16},{1,17},{2,18},{3,19},{4,20},{5,21},{6,22},{7,23},{8,24},{9,... | collective-permute-start | bytes 233480 | tf_op jit(solution)/shard_map/ppermute | solution.py:59
  74.2 5.8 %collective-permute-start.4 = (bf16[16,2432]{1,0:T(8,128)(2,1)S(1)}, bf16[16,2432]{1,0:T(8,128)(2,1)S(1)}, u32[]{:S(2)}, u32[]{:S(2)}) collective-permute-start(bf16[16,2432]{1,0:T(8,128)(2,1)S(1)} %pad_maximum_fusion.11), channel_id=1, source_target_pairs={{0,16},{1,17},{2,18},{3,19},{4,20},{5,21},{6,22},{7,23},{8,24},{9,... | collective-permute-start | bytes 233480 | tf_op jit(solution)/shard_map/ppermute | solution.py:59
  76.6 6.2 %collective-permute-start.21 = (bf16[16,2432]{1,0:T(8,128)(2,1)S(1)}, bf16[16,2432]{1,0:T(8,128)(2,1)S(1)}, u32[]{:S(2)}, u32[]{:S(2)}) collective-permute-start(bf16[16,2432]{1,0:T(8,128)(2,1)S(1)} %add_convert_fusion.28), channel_id=1, source_target_pairs={{0,8},{1,9},{2,10},{3,11},{4,12},{5,13},{6,14},{7,15},{8,0},{9,1},... | collective-permute-start | bytes 233480 | tf_op jit(solution)/shard_map/ppermute | solution.py:59
  80.0 5.6 %collective-permute-start.5 = (bf16[16,2432]{1,0:T(8,128)(2,1)S(1)}, bf16[16,2432]{1,0:T(8,128)(2,1)S(1)}, u32[]{:S(2)}, u32[]{:S(2)}) collective-permute-start(bf16[16,2432]{1,0:T(8,128)(2,1)S(1)} %add_convert_fusion.32), channel_id=1, source_target_pairs={{0,8},{1,9},{2,10},{3,11},{4,12},{5,13},{6,14},{7,15},{8,0},{9,1},... | collective-permute-start | bytes 233480 | tf_op jit(solution)/shard_map/ppermute | solution.py:59
  82.8 5.3 %collective-permute-start.22 = (bf16[32,2432]{1,0:T(8,128)(2,1)S(1)}, bf16[32,2432]{1,0:T(8,128)(2,1)S(1)}, u32[]{:S(2)}, u32[]{:S(2)}) collective-permute-start(bf16[32,2432]{1,0:T(8,128)(2,1)S(1)} %pad_maximum_fusion.9), channel_id=1, source_target_pairs={{0,4},{1,3},{2,6},{3,1},{4,0},{5,7},{6,2},{7,5},{8,12},{9,11},{10,... | collective-permute-start | bytes 466952 | tf_op jit(solution)/shard_map/ppermute | solution.py:59
  83.7 7.7 %collective-permute-start.14 = (bf16[32,2432]{1,0:T(8,128)(2,1)S(1)}, bf16[32,2432]{1,0:T(8,128)(2,1)S(1)}, u32[]{:S(2)}, u32[]{:S(2)}) collective-permute-start(bf16[32,2432]{1,0:T(8,128)(2,1)S(1)} %pad_maximum_fusion.8), channel_id=1, source_target_pairs={{0,4},{1,3},{2,6},{3,1},{4,0},{5,7},{6,2},{7,5},{8,12},{9,11},{10,... | collective-permute-start | bytes 466952 | tf_op jit(solution)/shard_map/ppermute | solution.py:59
  85.7 9.0 %collective-permute-start.6 = (bf16[32,2432]{1,0:T(8,128)(2,1)S(1)}, bf16[32,2432]{1,0:T(8,128)(2,1)S(1)}, u32[]{:S(2)}, u32[]{:S(2)}) collective-permute-start(bf16[32,2432]{1,0:T(8,128)(2,1)S(1)} %pad_maximum_fusion.7), channel_id=1, source_target_pairs={{0,4},{1,3},{2,6},{3,1},{4,0},{5,7},{6,2},{7,5},{8,12},{9,11},{10,... | collective-permute-start | bytes 466952 | tf_op jit(solution)/shard_map/ppermute | solution.py:59
  88.2 8.2 %collective-permute-start.23 = (bf16[64,2432]{1,0:T(8,128)(2,1)S(1)}, bf16[64,2432]{1,0:T(8,128)(2,1)S(1)}, u32[]{:S(2)}, u32[]{:S(2)}) collective-permute-start(bf16[64,2432]{1,0:T(8,128)(2,1)S(1)} %pad_maximum_fusion.6), channel_id=1, source_target_pairs={{0,2},{1,5},{2,0},{3,7},{4,6},{5,1},{6,4},{7,3},{8,10},{9,13},{10,... | collective-permute-start | bytes 933896 | tf_op jit(solution)/shard_map/ppermute | solution.py:59
  91.4 7.1 %collective-permute-start.15 = (bf16[64,2432]{1,0:T(8,128)(2,1)S(1)}, bf16[64,2432]{1,0:T(8,128)(2,1)S(1)}, u32[]{:S(2)}, u32[]{:S(2)}) collective-permute-start(bf16[64,2432]{1,0:T(8,128)(2,1)S(1)} %pad_maximum_fusion.5), channel_id=1, source_target_pairs={{0,2},{1,5},{2,0},{3,7},{4,6},{5,1},{6,4},{7,3},{8,10},{9,13},{10,... | collective-permute-start | bytes 933896 | tf_op jit(solution)/shard_map/ppermute | solution.py:59
  94.7 7.1 %collective-permute-start.7 = (bf16[64,2432]{1,0:T(8,128)(2,1)S(1)}, bf16[64,2432]{1,0:T(8,128)(2,1)S(1)}, u32[]{:S(2)}, u32[]{:S(2)}) collective-permute-start(bf16[64,2432]{1,0:T(8,128)(2,1)S(1)} %pad_maximum_fusion.4), channel_id=1, source_target_pairs={{0,2},{1,5},{2,0},{3,7},{4,6},{5,1},{6,4},{7,3},{8,10},{9,13},{10,... | collective-permute-start | bytes 933896 | tf_op jit(solution)/shard_map/ppermute | solution.py:59
  96.4 6.4 %collective-permute-start.26 = (bf16[128,2432]{1,0:T(8,128)(2,1)S(1)}, bf16[128,2432]{1,0:T(8,128)(2,1)S(1)}, u32[]{:S(2)}, u32[]{:S(2)}) collective-permute-start(bf16[128,2432]{1,0:T(8,128)(2,1)S(1)} %pad_maximum_fusion.3), channel_id=1, source_target_pairs={{0,1},{1,0},{2,3},{3,2},{4,5},{5,4},{6,7},{7,6},{8,9},{9,8},{10,11... | collective-permute-start | bytes 1867784 | tf_op jit(solution)/shard_map/ppermute | solution.py:59
  98.7 5.7 %collective-permute-start.25 = (bf16[128,2432]{1,0:T(8,128)(2,1)S(1)}, bf16[128,2432]{1,0:T(8,128)(2,1)S(1)}, u32[]{:S(2)}, u32[]{:S(2)}) collective-permute-start(bf16[128,2432]{1,0:T(8,128)(2,1)S(1)} %get-tuple-element.56), channel_id=1, source_target_pairs={{0,1},{1,0},{2,3},{3,2},{4,5},{5,4},{6,7},{7,6},{8,9},{9,8},{10,11... | collective-permute-start | bytes 1867784 | tf_op jit(solution)/shard_map/ppermute | solution.py:59
  108.7 6.8 %collective-permute-start.38 = (bf16[64,2304]{1,0:T(8,128)(2,1)S(1)}, bf16[64,2304]{1,0:T(8,128)(2,1)S(1)}, u32[]{:S(2)}, u32[]{:S(2)}) collective-permute-start(bf16[64,2304]{1,0:T(8,128)(2,1)S(1)} %get-tuple-element.72), channel_id=1, source_target_pairs={{0,2},{1,5},{2,0},{3,7},{4,6},{5,1},{6,4},{7,3},{8,10},{9,13},{10,... | collective-permute-start | bytes 884744 | tf_op jit(solution)/shard_map/ppermute | solution.py:59
  110.4 9.5 %collective-permute-start.33 = (bf16[64,2432]{1,0:T(8,128)(2,1)S(1)}, bf16[64,2432]{1,0:T(8,128)(2,1)S(1)}, u32[]{:S(2)}, u32[]{:S(2)}) collective-permute-start(bf16[64,2432]{1,0:T(8,128)(2,1)S(1)} %get-tuple-element.66), channel_id=1, source_target_pairs={{0,2},{1,5},{2,0},{3,7},{4,6},{5,1},{6,4},{7,3},{8,10},{9,13},{10,... | collective-permute-start | bytes 933896 | tf_op jit(solution)/shard_map/ppermute | solution.py:59
  111.2 9.6 %collective-permute-start.28 = (bf16[64,2432]{1,0:T(8,128)(2,1)S(1)}, bf16[64,2432]{1,0:T(8,128)(2,1)S(1)}, u32[]{:S(2)}, u32[]{:S(2)}) collective-permute-start(bf16[64,2432]{1,0:T(8,128)(2,1)S(1)} %get-tuple-element.64), channel_id=1, source_target_pairs={{0,8},{1,9},{2,10},{3,11},{4,12},{5,13},{6,14},{7,15},{8,0},{9,1},... | collective-permute-start | bytes 933896 | tf_op jit(solution)/shard_map/ppermute | solution.py:59
  115.6 7.6 %collective-permute-start.39 = (bf16[32,2304]{1,0:T(8,128)(2,1)S(1)}, bf16[32,2304]{1,0:T(8,128)(2,1)S(1)}, u32[]{:S(2)}, u32[]{:S(2)}) collective-permute-start(bf16[32,2304]{1,0:T(8,128)(2,1)S(1)} %get-tuple-element.84), channel_id=1, source_target_pairs={{0,4},{1,3},{2,6},{3,1},{4,0},{5,7},{6,2},{7,5},{8,12},{9,11},{10,... | collective-permute-start | bytes 442376 | tf_op jit(solution)/shard_map/ppermute | solution.py:59
  119.9 5.8 %collective-permute-start.34 = (bf16[32,2432]{1,0:T(8,128)(2,1)S(1)}, bf16[32,2432]{1,0:T(8,128)(2,1)S(1)}, u32[]{:S(2)}, u32[]{:S(2)}) collective-permute-start(bf16[32,2432]{1,0:T(8,128)(2,1)S(1)} %get-tuple-element.78), channel_id=1, source_target_pairs={{0,4},{1,3},{2,6},{3,1},{4,0},{5,7},{6,2},{7,5},{8,12},{9,11},{10,... | collective-permute-start | bytes 466952 | tf_op jit(solution)/shard_map/ppermute | solution.py:59
  120.9 7.5 %collective-permute-start.29 = (bf16[32,2432]{1,0:T(8,128)(2,1)S(1)}, bf16[32,2432]{1,0:T(8,128)(2,1)S(1)}, u32[]{:S(2)}, u32[]{:S(2)}) collective-permute-start(bf16[32,2432]{1,0:T(8,128)(2,1)S(1)} %get-tuple-element.76), channel_id=1, source_target_pairs={{0,2},{1,5},{2,0},{3,7},{4,6},{5,1},{6,4},{7,3},{8,10},{9,13},{10,... | collective-permute-start | bytes 466952 | tf_op jit(solution)/shard_map/ppermute | solution.py:59
  125.8 7.7 %collective-permute-start.35 = (bf16[16,2432]{1,0:T(8,128)(2,1)S(1)}, bf16[16,2432]{1,0:T(8,128)(2,1)S(1)}, u32[]{:S(2)}, u32[]{:S(2)}) collective-permute-start(bf16[16,2432]{1,0:T(8,128)(2,1)S(1)} %get-tuple-element.90), channel_id=1, source_target_pairs={{0,8},{1,9},{2,10},{3,11},{4,12},{5,13},{6,14},{7,15},{8,0},{9,1},... | collective-permute-start | bytes 233480 | tf_op jit(solution)/shard_map/ppermute | solution.py:59
  127.7 5.8 %collective-permute-start.41 = (bf16[8,2304]{1,0:T(8,128)(2,1)S(1)}, bf16[8,2304]{1,0:T(8,128)(2,1)S(1)}, u32[]{:S(2)}, u32[]{:S(2)}) collective-permute-start(bf16[8,2304]{1,0:T(8,128)(2,1)S(1)} %add_convert_fusion.48), channel_id=1, source_target_pairs={{0,16},{1,17},{2,18},{3,19},{4,20},{5,21},{6,22},{7,23},{8,24},{9,... | collective-permute-start | bytes 110600 | tf_op jit(solution)/shard_map/ppermute | solution.py:59
  128.4 5.3 %collective-permute-start.30 = (bf16[16,2432]{1,0:T(8,128)(2,1)S(1)}, bf16[16,2432]{1,0:T(8,128)(2,1)S(1)}, u32[]{:S(2)}, u32[]{:S(2)}) collective-permute-start(bf16[16,2432]{1,0:T(8,128)(2,1)S(1)} %get-tuple-element.88), channel_id=1, source_target_pairs={{0,4},{1,3},{2,6},{3,1},{4,0},{5,7},{6,2},{7,5},{8,12},{9,11},{10,... | collective-permute-start | bytes 233480 | tf_op jit(solution)/shard_map/ppermute | solution.py:59
  133.5 4.9 %collective-permute-start.36 = (bf16[8,2432]{1,0:T(8,128)(2,1)S(1)}, bf16[8,2432]{1,0:T(8,128)(2,1)S(1)}, u32[]{:S(2)}, u32[]{:S(2)}) collective-permute-start(bf16[8,2432]{1,0:T(8,128)(2,1)S(1)} %add_convert_fusion.40), channel_id=1, source_target_pairs={{0,16},{1,17},{2,18},{3,19},{4,20},{5,21},{6,22},{7,23},{8,24},{9,... | collective-permute-start | bytes 116744 | tf_op jit(solution)/shard_map/ppermute | solution.py:59
  133.7 5.2 %collective-permute-start.31 = (bf16[8,2432]{1,0:T(8,128)(2,1)S(1)}, bf16[8,2432]{1,0:T(8,128)(2,1)S(1)}, u32[]{:S(2)}, u32[]{:S(2)}) collective-permute-start(bf16[8,2432]{1,0:T(8,128)(2,1)S(1)} %add_convert_fusion.42), channel_id=1, source_target_pairs={{0,16},{1,17},{2,18},{3,19},{4,20},{5,21},{6,22},{7,23},{8,24},{9,... | collective-permute-start | bytes 116744 | tf_op jit(solution)/shard_map/ppermute | solution.py:59
  (26 other events, 132.5 us)

commit v6 on v5

--- a/solution.py
+++ b/solution.py
@@ -296,8 +296,9 @@
     for i, ((start, size), base) in enumerate(zip(plans, residual, strict=True)):
         acts = hidden
         if orders[i] != sorted(orders[i]):
-            move = np.eye(rows, dtype=np.float32)[place_rows(orders[i], rows)]
-            acts = jnp.dot(jnp.asarray(move, bf16), hidden, preferred_element_type=f32).astype(bf16)
+            moved = place_rows(orders[i], rows)
+            run = rows // 2 ** (len(orders[i]) + 1)
+            acts = jnp.concatenate([hidden[k : k + run] for k in moved[::run].tolist()], axis=0)
         keep, send = project(acts, down_near[i], 0, size)
         own, partners = halve(keep, send, sum_stages[i], devices)
         came = swap(partners, stages[-1], devices)

time: 140 us -> 140 us (level)
  transfers between devices with their start and end apart: 43 -> 43, of which waited for: 22 -> 23; matrix products, arithmetic and copies ran while one was open for 14% -> 13% of each run, Pallas kernels for 2% -> 2%
where the time goes in v6:
time: 140 us; the launch traced here: 139 us
  waiting for transfers between devices  55 us (39%)
  starting transfers between devices  47.1 us (34%)
  local copies, waits for them, and re-layouts  13 us (9%)
  Pallas kernels  11.2 us (8%)
  other arithmetic  8.12 us (6%)
  matrix products  4.43 us (3%)
    ppermute x42, waiting for transfers between devices, swap(): return lax.ppermute(x, 'expert', pairs)  42.6 us
    ppermute x42, starting transfers between devices, swap(): return lax.ppermute(x, 'expert', pairs)  39.7 us
    all_to_all x1, waiting for transfers between devices, shards(): lax.all_to_all(latent_out, 'expert', split_axis=0, concat_axis=0, tiled=T...  12.4 us
    slice x2, local copies, waits for them, and re-layouts, shards(): out_near = [out_after[:, start:start + size] for start, size in plans]  7.71 us
    all_to_all x1, starting transfers between devices, shards(): lax.all_to_all(latent_out, 'expert', split_axis=0, concat_axis=0, tiled=T...  7.43 us
    pallas_call x1, Pallas kernels, attend(): pl.pallas_call(attend_kernel, grid=(tokens // group,), out_shape=jax.Shap...  7.09 us
    pallas_call x6, Pallas kernels, project(): pl.pallas_call(functools.partial(project_kernel, start), out_shape=[half,...  4.14 us
    concatenate x1, other arithmetic, shards(): both_near = jnp.concatenate([gate_after[0], up_after[0]], axis=1)  3.69 us
  transfers between devices with their start and end apart: 43, of which 23 were waited for; matrix products, arithmetic and copies ran while one was open for 13% of the time, Pallas kernels for 2%

profile of v6, /device:TPU:0, one launch (start us, length us, event | category | flops | bytes accessed | tf_op | source)
XLA Modules:
  0.0 139.4 jit_solution(15197795698007442753)
XLA Ops:
  0.0 2.0 %reshape.121.rope_ref = bf16[8,128,64]{2,1,0:T(8,128)(2,1)} reshape(bf16[8,8192]{1,0:T(8,128)(2,1)} %param.16) | data formatting | bytes 262144 | tf_op jit(solution)/shard_map/reshape | solution.py:151
  2.0 7.1 %shard_map.136 = bf16[128,8,512]{2,1,0:T(8,128)(2,1)} custom-call(s32[8]{0:T(128)} %lengths_ref.1, bf16[8,128,512]{2,1,0:T(8,128)(2,1)} %latent_ref.1, bf16[8,128,64]{2,1,0:T(8,128)(2,1)} %reshape.121.rope_ref, bf16[8,256,512]{2,1,0:T(8,128)(2,1)} %keys_ref.1, bf16[8,64,256]{2,1,0:T(8,128)(2,1)} %turned_ref.1), custom_call_target="tpu_custom_call" | custom-call | flops 570425344 | bytes 4456448 | tf_op jit(solution)/shard_map/pallas_call | solution.py:132
  9.0 7.4 %all-to-all-start = ((bf16[128,8,512]{2,1,0:T(8,128)(2,1)}), bf16[128,8,512]{2,1,0:T(8,128)(2,1)}, u32[]{:S(2)}, u32[]{:S(2)}) async-start(bf16[128,8,512]{2,1,0:T(8,128)(2,1)} %shard_map.136), calls=%async_computation | async-start | bytes 2097152 | tf_op jit(solution)/shard_map/all_to_all | solution.py:221
  18.9 3.4 %slice.425.weight_ref = bf16[512,2304]{1,0:T(8,128)(2,1)} slice(bf16[512,7168]{1,0:T(8,128)(2,1)} %param.21), slice={[0:512], [4864:7168]} | slice | bytes 4718592 | tf_op jit(solution)/shard_map/slice | solution.py:219
  22.3 3.7 %pad_maximum_fusion = bf16[7168,256]{1,0:T(8,128)(2,1)} fusion(bf16[7168,128]{1,0:T(8,128)(2,1)S(1)} %bitcast.21, bf16[7168,128]{1,0:T(8,128)(2,1)} %bitcast.22), kind=kLoop, calls=%fused_computation | loop fusion | flops 7340032 | bytes 7340032 | tf_op jit(solution)/shard_map/concatenate | solution.py:218
  26.0 4.3 %fusion.65 = (bf16[512,2432]{1,0:T(8,128)(2,1)S(1)}, bf16[512,2432]{1,0:T(8,128)(2,1)}) fusion(bf16[512,7168]{1,0:T(8,128)(2,1)} %param.21), kind=kLoop, calls=%fused_computation.195 | loop fusion | bytes 9961472 | tf_op jit(solution)/shard_map/slice | solution.py:219
  30.3 12.4 %all-to-all-done = bf16[128,8,512]{2,1,0:T(8,128)(2,1)} async-done(((bf16[128,8,512]{2,1,0:T(8,128)(2,1)}), bf16[128,8,512]{2,1,0:T(8,128)(2,1)}, u32[]{:S(2)}, u32[]{:S(2)}) %all-to-all-start) | async-done | bytes 1048608 | tf_op jit(solution)/shard_map/all_to_all | solution.py:221
  42.7 1.8 %fusion.12 = bf16[32,8,4,128]{3,1,0,2:T(8,128)(2,1)S(1)} fusion(bf16[32,4,8,512]{3,2,1,0:T(8,128)(2,1)} %bitcast.5, bf16[4,512,128]{2,1,0:T(8,128)(2,1)S(1)} %copy-done), kind=kOutput, calls=%fused_computation.28 | convolution fusion | flops 134348800 | bytes 1835008 | tf_op jit(solution)/shard_map/sqtg,qge->stqe/dot_general | solution.py:227
  52.4 3.5 %collective-permute-done.17 = bf16[64,2304]{1,0:T(8,128)(2,1)S(1)} collective-permute-done((bf16[64,2304]{1,0:T(8,128)(2,1)S(1)}, bf16[64,2304]{1,0:T(8,128)(2,1)S(1)}, u32[]{:S(2)}, u32[]{:S(2)}) %collective-permute-start.17) | collective-permute-done | bytes 294944 | tf_op jit(solution)/shard_map/ppermute | solution.py:59
  57.5 2.4 %collective-permute-done.1 = bf16[64,2432]{1,0:T(8,128)(2,1)S(1)} collective-permute-done((bf16[64,2432]{1,0:T(8,128)(2,1)S(1)}, bf16[64,2432]{1,0:T(8,128)(2,1)S(1)}, u32[]{:S(2)}, u32[]{:S(2)}) %collective-permute-start.1) | collective-permute-done | bytes 311328 | tf_op jit(solution)/shard_map/ppermute | solution.py:59
  63.3 2.6 %collective-permute-done.2 = bf16[32,2432]{1,0:T(8,128)(2,1)S(1)} collective-permute-done((bf16[32,2432]{1,0:T(8,128)(2,1)S(1)}, bf16[32,2432]{1,0:T(8,128)(2,1)S(1)}, u32[]{:S(2)}, u32[]{:S(2)}) %collective-permute-start.2) | collective-permute-done | bytes 155680 | tf_op jit(solution)/shard_map/ppermute | solution.py:59
  65.9 1.9 %collective-permute-start.3 = (bf16[16,2432]{1,0:T(8,128)(2,1)S(1)}, bf16[16,2432]{1,0:T(8,128)(2,1)S(1)}, u32[]{:S(2)}, u32[]{:S(2)}) collective-permute-start(bf16[16,2432]{1,0:T(8,128)(2,1)S(1)} %get-tuple-element.92), channel_id=1, source_target_pairs={{0,4},{1,3},{2,6},{3,1},{4,0},{5,7},{6,2},{7,5},{8,12},{9,11},{10,... | collective-permute-start | bytes 233480 | tf_op jit(solution)/shard_map/ppermute | solution.py:59
  68.0 2.1 %collective-permute-start.20 = (bf16[16,2432]{1,0:T(8,128)(2,1)S(1)}, bf16[16,2432]{1,0:T(8,128)(2,1)S(1)}, u32[]{:S(2)}, u32[]{:S(2)}) collective-permute-start(bf16[16,2432]{1,0:T(8,128)(2,1)S(1)} %fusion.50), channel_id=1, source_target_pairs={{0,16},{1,17},{2,18},{3,19},{4,20},{5,21},{6,22},{7,23},{8,24},{9,... | collective-permute-start | bytes 233480 | tf_op jit(solution)/shard_map/ppermute | solution.py:59
  70.4 1.9 %collective-permute-done.11 = bf16[16,2432]{1,0:T(8,128)(2,1)S(1)} collective-permute-done((bf16[16,2432]{1,0:T(8,128)(2,1)S(1)}, bf16[16,2432]{1,0:T(8,128)(2,1)S(1)}, u32[]{:S(2)}, u32[]{:S(2)}) %collective-permute-start.11) | collective-permute-done | bytes 77856 | tf_op jit(solution)/shard_map/ppermute | solution.py:59
  72.4 1.8 %collective-permute-start.12 = (bf16[16,2432]{1,0:T(8,128)(2,1)S(1)}, bf16[16,2432]{1,0:T(8,128)(2,1)S(1)}, u32[]{:S(2)}, u32[]{:S(2)}) collective-permute-start(bf16[16,2432]{1,0:T(8,128)(2,1)S(1)} %pad_maximum_fusion.12), channel_id=1, source_target_pairs={{0,16},{1,17},{2,18},{3,19},{4,20},{5,21},{6,22},{7,23},{8,24},{9,... | collective-permute-start | bytes 233480 | tf_op jit(solution)/shard_map/ppermute | solution.py:59
  76.8 2.3 %collective-permute-done.12 = bf16[16,2432]{1,0:T(8,128)(2,1)S(1)} collective-permute-done((bf16[16,2432]{1,0:T(8,128)(2,1)S(1)}, bf16[16,2432]{1,0:T(8,128)(2,1)S(1)}, u32[]{:S(2)}, u32[]{:S(2)}) %collective-permute-start.12) | collective-permute-done | bytes 77856 | tf_op jit(solution)/shard_map/ppermute | solution.py:59
  80.0 2.8 %collective-permute-start.5 = (bf16[16,2432]{1,0:T(8,128)(2,1)S(1)}, bf16[16,2432]{1,0:T(8,128)(2,1)S(1)}, u32[]{:S(2)}, u32[]{:S(2)}) collective-permute-start(bf16[16,2432]{1,0:T(8,128)(2,1)S(1)} %add_convert_fusion.32), channel_id=1, source_target_pairs={{0,8},{1,9},{2,10},{3,11},{4,12},{5,13},{6,14},{7,15},{8,0},{9,1},... | collective-permute-start | bytes 233480 | tf_op jit(solution)/shard_map/ppermute | solution.py:59
  83.7 2.0 %collective-permute-start.14 = (bf16[32,2432]{1,0:T(8,128)(2,1)S(1)}, bf16[32,2432]{1,0:T(8,128)(2,1)S(1)}, u32[]{:S(2)}, u32[]{:S(2)}) collective-permute-start(bf16[32,2432]{1,0:T(8,128)(2,1)S(1)} %pad_maximum_fusion.8), channel_id=1, source_target_pairs={{0,4},{1,3},{2,6},{3,1},{4,0},{5,7},{6,2},{7,5},{8,12},{9,11},{10,... | collective-permute-start | bytes 466952 | tf_op jit(solution)/shard_map/ppermute | solution.py:59
  86.6 1.6 %collective-permute-done.22 = bf16[32,2432]{1,0:T(8,128)(2,1)S(1)} collective-permute-done((bf16[32,2432]{1,0:T(8,128)(2,1)S(1)}, bf16[32,2432]{1,0:T(8,128)(2,1)S(1)}, u32[]{:S(2)}, u32[]{:S(2)}) %collective-permute-start.22) | collective-permute-done | bytes 155680 | tf_op jit(solution)/shard_map/ppermute | solution.py:59
  89.3 2.1 %collective-permute-done.14 = bf16[32,2432]{1,0:T(8,128)(2,1)S(1)} collective-permute-done((bf16[32,2432]{1,0:T(8,128)(2,1)S(1)}, bf16[32,2432]{1,0:T(8,128)(2,1)S(1)}, u32[]{:S(2)}, u32[]{:S(2)}) %collective-permute-start.14) | collective-permute-done | bytes 155680 | tf_op jit(solution)/shard_map/ppermute | solution.py:59
  91.4 1.6 %collective-permute-start.15 = (bf16[64,2432]{1,0:T(8,128)(2,1)S(1)}, bf16[64,2432]{1,0:T(8,128)(2,1)S(1)}, u32[]{:S(2)}, u32[]{:S(2)}) collective-permute-start(bf16[64,2432]{1,0:T(8,128)(2,1)S(1)} %pad_maximum_fusion.5), channel_id=1, source_target_pairs={{0,2},{1,5},{2,0},{3,7},{4,6},{5,1},{6,4},{7,3},{8,10},{9,13},{10,... | collective-permute-start | bytes 933896 | tf_op jit(solution)/shard_map/ppermute | solution.py:59
  93.0 1.7 %collective-permute-done.6 = bf16[32,2432]{1,0:T(8,128)(2,1)S(1)} collective-permute-done((bf16[32,2432]{1,0:T(8,128)(2,1)S(1)}, bf16[32,2432]{1,0:T(8,128)(2,1)S(1)}, u32[]{:S(2)}, u32[]{:S(2)}) %collective-permute-start.6) | collective-permute-done | bytes 155680 | tf_op jit(solution)/shard_map/ppermute | solution.py:59
  94.7 1.6 %collective-permute-start.7 = (bf16[64,2432]{1,0:T(8,128)(2,1)S(1)}, bf16[64,2432]{1,0:T(8,128)(2,1)S(1)}, u32[]{:S(2)}, u32[]{:S(2)}) collective-permute-start(bf16[64,2432]{1,0:T(8,128)(2,1)S(1)} %pad_maximum_fusion.4), channel_id=1, source_target_pairs={{0,2},{1,5},{2,0},{3,7},{4,6},{5,1},{6,4},{7,3},{8,10},{9,13},{10,... | collective-permute-start | bytes 933896 | tf_op jit(solution)/shard_map/ppermute | solution.py:59
  98.7 3.1 %collective-permute-done.7 = bf16[64,2432]{1,0:T(8,128)(2,1)S(1)} collective-permute-done((bf16[64,2432]{1,0:T(8,128)(2,1)S(1)}, bf16[64,2432]{1,0:T(8,128)(2,1)S(1)}, u32[]{:S(2)}, u32[]{:S(2)}) %collective-permute-start.7) | collective-permute-done | bytes 311328 | tf_op jit(solution)/shard_map/ppermute | solution.py:59
  111.5 4.0 %collective-permute-done.38 = bf16[64,2304]{1,0:T(8,128)(2,1)S(1)} collective-permute-done((bf16[64,2304]{1,0:T(8,128)(2,1)S(1)}, bf16[64,2304]{1,0:T(8,128)(2,1)S(1)}, u32[]{:S(2)}, u32[]{:S(2)}) %collective-permute-start.38) | collective-permute-done | bytes 294944 | tf_op jit(solution)/shard_map/ppermute | solution.py:59
  116.7 3.3 %collective-permute-done.33 = bf16[64,2432]{1,0:T(8,128)(2,1)S(1)} collective-permute-done((bf16[64,2432]{1,0:T(8,128)(2,1)S(1)}, bf16[64,2432]{1,0:T(8,128)(2,1)S(1)}, u32[]{:S(2)}, u32[]{:S(2)}) %collective-permute-start.33) | collective-permute-done | bytes 311328 | tf_op jit(solution)/shard_map/ppermute | solution.py:59
  121.0 2.4 %collective-permute-start.29 = (bf16[32,2432]{1,0:T(8,128)(2,1)S(1)}, bf16[32,2432]{1,0:T(8,128)(2,1)S(1)}, u32[]{:S(2)}, u32[]{:S(2)}) collective-permute-start(bf16[32,2432]{1,0:T(8,128)(2,1)S(1)} %get-tuple-element.76), channel_id=1, source_target_pairs={{0,2},{1,5},{2,0},{3,7},{4,6},{5,1},{6,4},{7,3},{8,10},{9,13},{10,... | collective-permute-start | bytes 466952 | tf_op jit(solution)/shard_map/ppermute | solution.py:59
  123.5 2.0 %collective-permute-done.34 = bf16[32,2432]{1,0:T(8,128)(2,1)S(1)} collective-permute-done((bf16[32,2432]{1,0:T(8,128)(2,1)S(1)}, bf16[32,2432]{1,0:T(8,128)(2,1)S(1)}, u32[]{:S(2)}, u32[]{:S(2)}) %collective-permute-start.34) | collective-permute-done | bytes 155680 | tf_op jit(solution)/shard_map/ppermute | solution.py:59
  125.8 2.0 %collective-permute-done.40 = bf16[16,2304]{1,0:T(8,128)(2,1)S(1)} collective-permute-done((bf16[16,2304]{1,0:T(8,128)(2,1)S(1)}, bf16[16,2304]{1,0:T(8,128)(2,1)S(1)}, u32[]{:S(2)}, u32[]{:S(2)}) %collective-permute-start.40) | collective-permute-done | bytes 73760 | tf_op jit(solution)/shard_map/ppermute | solution.py:59
  129.7 3.6 %collective-permute-done.41 = bf16[8,2304]{1,0:T(8,128)(2,1)S(1)} collective-permute-done((bf16[8,2304]{1,0:T(8,128)(2,1)S(1)}, bf16[8,2304]{1,0:T(8,128)(2,1)S(1)}, u32[]{:S(2)}, u32[]{:S(2)}) %collective-permute-start.41) | collective-permute-done | bytes 36896 | tf_op jit(solution)/shard_map/ppermute | solution.py:59
  133.6 2.9 %collective-permute-start.31 = (bf16[8,2432]{1,0:T(8,128)(2,1)S(1)}, bf16[8,2432]{1,0:T(8,128)(2,1)S(1)}, u32[]{:S(2)}, u32[]{:S(2)}) collective-permute-start(bf16[8,2432]{1,0:T(8,128)(2,1)S(1)} %add_convert_fusion.42), channel_id=1, source_target_pairs={{0,16},{1,17},{2,18},{3,19},{4,20},{5,21},{6,22},{7,23},{8,24},{9,... | collective-permute-start | bytes 116744 | tf_op jit(solution)/shard_map/ppermute | solution.py:59
  136.5 1.9 %collective-permute-done.36 = bf16[8,2432]{1,0:T(8,128)(2,1)S(1)} collective-permute-done((bf16[8,2432]{1,0:T(8,128)(2,1)S(1)}, bf16[8,2432]{1,0:T(8,128)(2,1)S(1)}, u32[]{:S(2)}, u32[]{:S(2)}) %collective-permute-start.36) | collective-permute-done | bytes 38944 | tf_op jit(solution)/shard_map/ppermute | solution.py:59
  (183 shorter events, 39.7 us)
Async XLA Ops:
  9.0 33.6 %all-to-all-start = ((bf16[128,8,512]{2,1,0:T(8,128)(2,1)}), bf16[128,8,512]{2,1,0:T(8,128)(2,1)}, u32[]{:S(2)}, u32[]{:S(2)}) async-start(bf16[128,8,512]{2,1,0:T(8,128)(2,1)} %shard_map.136), calls=%async_computation | async-start | bytes 2097152 | tf_op jit(solution)/shard_map/all_to_all | solution.py:221
  49.1 6.8 %collective-permute-start.17 = (bf16[64,2304]{1,0:T(8,128)(2,1)S(1)}, bf16[64,2304]{1,0:T(8,128)(2,1)S(1)}, u32[]{:S(2)}, u32[]{:S(2)}) collective-permute-start(bf16[64,2304]{1,0:T(8,128)(2,1)S(1)} %get-tuple-element.74), channel_id=1, source_target_pairs={{0,2},{1,5},{2,0},{3,7},{4,6},{5,1},{6,4},{7,3},{8,10},{9,13},{10,... | collective-permute-start | bytes 884744 | tf_op jit(solution)/shard_map/ppermute | solution.py:59
  50.8 9.2 %collective-permute-start.1 = (bf16[64,2432]{1,0:T(8,128)(2,1)S(1)}, bf16[64,2432]{1,0:T(8,128)(2,1)S(1)}, u32[]{:S(2)}, u32[]{:S(2)}) collective-permute-start(bf16[64,2432]{1,0:T(8,128)(2,1)S(1)} %get-tuple-element.68), channel_id=1, source_target_pairs={{0,8},{1,9},{2,10},{3,11},{4,12},{5,13},{6,14},{7,15},{8,0},{9,1},... | collective-permute-start | bytes 933896 | tf_op jit(solution)/shard_map/ppermute | solution.py:59
  51.6 10.0 %collective-permute-start.9 = (bf16[64,2432]{1,0:T(8,128)(2,1)S(1)}, bf16[64,2432]{1,0:T(8,128)(2,1)S(1)}, u32[]{:S(2)}, u32[]{:S(2)}) collective-permute-start(bf16[64,2432]{1,0:T(8,128)(2,1)S(1)} %get-tuple-element.70), channel_id=1, source_target_pairs={{0,2},{1,5},{2,0},{3,7},{4,6},{5,1},{6,4},{7,3},{8,10},{9,13},{10,... | collective-permute-start | bytes 933896 | tf_op jit(solution)/shard_map/ppermute | solution.py:59
  56.0 6.4 %collective-permute-start.18 = (bf16[32,2304]{1,0:T(8,128)(2,1)S(1)}, bf16[32,2304]{1,0:T(8,128)(2,1)S(1)}, u32[]{:S(2)}, u32[]{:S(2)}) collective-permute-start(bf16[32,2304]{1,0:T(8,128)(2,1)S(1)} %get-tuple-element.86), channel_id=1, source_target_pairs={{0,4},{1,3},{2,6},{3,1},{4,0},{5,7},{6,2},{7,5},{8,12},{9,11},{10,... | collective-permute-start | bytes 442376 | tf_op jit(solution)/shard_map/ppermute | solution.py:59
  60.1 5.8 %collective-permute-start.2 = (bf16[32,2432]{1,0:T(8,128)(2,1)S(1)}, bf16[32,2432]{1,0:T(8,128)(2,1)S(1)}, u32[]{:S(2)}, u32[]{:S(2)}) collective-permute-start(bf16[32,2432]{1,0:T(8,128)(2,1)S(1)} %get-tuple-element.80), channel_id=1, source_target_pairs={{0,2},{1,5},{2,0},{3,7},{4,6},{5,1},{6,4},{7,3},{8,10},{9,13},{10,... | collective-permute-start | bytes 466952 | tf_op jit(solution)/shard_map/ppermute | solution.py:59
  61.7 6.1 %collective-permute-start.10 = (bf16[32,2432]{1,0:T(8,128)(2,1)S(1)}, bf16[32,2432]{1,0:T(8,128)(2,1)S(1)}, u32[]{:S(2)}, u32[]{:S(2)}) collective-permute-start(bf16[32,2432]{1,0:T(8,128)(2,1)S(1)} %get-tuple-element.82), channel_id=1, source_target_pairs={{0,4},{1,3},{2,6},{3,1},{4,0},{5,7},{6,2},{7,5},{8,12},{9,11},{10,... | collective-permute-start | bytes 466952 | tf_op jit(solution)/shard_map/ppermute | solution.py:59
  62.5 5.5 %collective-permute-start.19 = (bf16[16,2304]{1,0:T(8,128)(2,1)S(1)}, bf16[16,2304]{1,0:T(8,128)(2,1)S(1)}, u32[]{:S(2)}, u32[]{:S(2)}) collective-permute-start(bf16[16,2304]{1,0:T(8,128)(2,1)S(1)} %get-tuple-element.98), channel_id=1, source_target_pairs={{0,8},{1,9},{2,10},{3,11},{4,12},{5,13},{6,14},{7,15},{8,0},{9,1},... | collective-permute-start | bytes 221192 | tf_op jit(solution)/shard_map/ppermute | solution.py:59
  68.0 8.6 %collective-permute-start.20 = (bf16[16,2432]{1,0:T(8,128)(2,1)S(1)}, bf16[16,2432]{1,0:T(8,128)(2,1)S(1)}, u32[]{:S(2)}, u32[]{:S(2)}) collective-permute-start(bf16[16,2432]{1,0:T(8,128)(2,1)S(1)} %fusion.50), channel_id=1, source_target_pairs={{0,16},{1,17},{2,18},{3,19},{4,20},{5,21},{6,22},{7,23},{8,24},{9,... | collective-permute-start | bytes 233480 | tf_op jit(solution)/shard_map/ppermute | solution.py:59
  72.4 6.7 %collective-permute-start.12 = (bf16[16,2432]{1,0:T(8,128)(2,1)S(1)}, bf16[16,2432]{1,0:T(8,128)(2,1)S(1)}, u32[]{:S(2)}, u32[]{:S(2)}) collective-permute-start(bf16[16,2432]{1,0:T(8,128)(2,1)S(1)} %pad_maximum_fusion.12), channel_id=1, source_target_pairs={{0,16},{1,17},{2,18},{3,19},{4,20},{5,21},{6,22},{7,23},{8,24},{9,... | collective-permute-start | bytes 233480 | tf_op jit(solution)/shard_map/ppermute | solution.py:59
  74.2 5.8 %collective-permute-start.4 = (bf16[16,2432]{1,0:T(8,128)(2,1)S(1)}, bf16[16,2432]{1,0:T(8,128)(2,1)S(1)}, u32[]{:S(2)}, u32[]{:S(2)}) collective-permute-start(bf16[16,2432]{1,0:T(8,128)(2,1)S(1)} %pad_maximum_fusion.11), channel_id=1, source_target_pairs={{0,16},{1,17},{2,18},{3,19},{4,20},{5,21},{6,22},{7,23},{8,24},{9,... | collective-permute-start | bytes 233480 | tf_op jit(solution)/shard_map/ppermute | solution.py:59
  76.6 6.2 %collective-permute-start.21 = (bf16[16,2432]{1,0:T(8,128)(2,1)S(1)}, bf16[16,2432]{1,0:T(8,128)(2,1)S(1)}, u32[]{:S(2)}, u32[]{:S(2)}) collective-permute-start(bf16[16,2432]{1,0:T(8,128)(2,1)S(1)} %add_convert_fusion.28), channel_id=1, source_target_pairs={{0,8},{1,9},{2,10},{3,11},{4,12},{5,13},{6,14},{7,15},{8,0},{9,1},... | collective-permute-start | bytes 233480 | tf_op jit(solution)/shard_map/ppermute | solution.py:59
  80.0 5.7 %collective-permute-start.5 = (bf16[16,2432]{1,0:T(8,128)(2,1)S(1)}, bf16[16,2432]{1,0:T(8,128)(2,1)S(1)}, u32[]{:S(2)}, u32[]{:S(2)}) collective-permute-start(bf16[16,2432]{1,0:T(8,128)(2,1)S(1)} %add_convert_fusion.32), channel_id=1, source_target_pairs={{0,8},{1,9},{2,10},{3,11},{4,12},{5,13},{6,14},{7,15},{8,0},{9,1},... | collective-permute-start | bytes 233480 | tf_op jit(solution)/shard_map/ppermute | solution.py:59
  82.8 5.3 %collective-permute-start.22 = (bf16[32,2432]{1,0:T(8,128)(2,1)S(1)}, bf16[32,2432]{1,0:T(8,128)(2,1)S(1)}, u32[]{:S(2)}, u32[]{:S(2)}) collective-permute-start(bf16[32,2432]{1,0:T(8,128)(2,1)S(1)} %pad_maximum_fusion.9), channel_id=1, source_target_pairs={{0,4},{1,3},{2,6},{3,1},{4,0},{5,7},{6,2},{7,5},{8,12},{9,11},{10,... | collective-permute-start | bytes 466952 | tf_op jit(solution)/shard_map/ppermute | solution.py:59
  83.7 7.7 %collective-permute-start.14 = (bf16[32,2432]{1,0:T(8,128)(2,1)S(1)}, bf16[32,2432]{1,0:T(8,128)(2,1)S(1)}, u32[]{:S(2)}, u32[]{:S(2)}) collective-permute-start(bf16[32,2432]{1,0:T(8,128)(2,1)S(1)} %pad_maximum_fusion.8), channel_id=1, source_target_pairs={{0,4},{1,3},{2,6},{3,1},{4,0},{5,7},{6,2},{7,5},{8,12},{9,11},{10,... | collective-permute-start | bytes 466952 | tf_op jit(solution)/shard_map/ppermute | solution.py:59
  85.7 9.0 %collective-permute-start.6 = (bf16[32,2432]{1,0:T(8,128)(2,1)S(1)}, bf16[32,2432]{1,0:T(8,128)(2,1)S(1)}, u32[]{:S(2)}, u32[]{:S(2)}) collective-permute-start(bf16[32,2432]{1,0:T(8,128)(2,1)S(1)} %pad_maximum_fusion.7), channel_id=1, source_target_pairs={{0,4},{1,3},{2,6},{3,1},{4,0},{5,7},{6,2},{7,5},{8,12},{9,11},{10,... | collective-permute-start | bytes 466952 | tf_op jit(solution)/shard_map/ppermute | solution.py:59
  88.2 8.2 %collective-permute-start.23 = (bf16[64,2432]{1,0:T(8,128)(2,1)S(1)}, bf16[64,2432]{1,0:T(8,128)(2,1)S(1)}, u32[]{:S(2)}, u32[]{:S(2)}) collective-permute-start(bf16[64,2432]{1,0:T(8,128)(2,1)S(1)} %pad_maximum_fusion.6), channel_id=1, source_target_pairs={{0,2},{1,5},{2,0},{3,7},{4,6},{5,1},{6,4},{7,3},{8,10},{9,13},{10,... | collective-permute-start | bytes 933896 | tf_op jit(solution)/shard_map/ppermute | solution.py:59
  91.4 7.1 %collective-permute-start.15 = (bf16[64,2432]{1,0:T(8,128)(2,1)S(1)}, bf16[64,2432]{1,0:T(8,128)(2,1)S(1)}, u32[]{:S(2)}, u32[]{:S(2)}) collective-permute-start(bf16[64,2432]{1,0:T(8,128)(2,1)S(1)} %pad_maximum_fusion.5), channel_id=1, source_target_pairs={{0,2},{1,5},{2,0},{3,7},{4,6},{5,1},{6,4},{7,3},{8,10},{9,13},{10,... | collective-permute-start | bytes 933896 | tf_op jit(solution)/shard_map/ppermute | solution.py:59
  94.7 7.1 %collective-permute-start.7 = (bf16[64,2432]{1,0:T(8,128)(2,1)S(1)}, bf16[64,2432]{1,0:T(8,128)(2,1)S(1)}, u32[]{:S(2)}, u32[]{:S(2)}) collective-permute-start(bf16[64,2432]{1,0:T(8,128)(2,1)S(1)} %pad_maximum_fusion.4), channel_id=1, source_target_pairs={{0,2},{1,5},{2,0},{3,7},{4,6},{5,1},{6,4},{7,3},{8,10},{9,13},{10,... | collective-permute-start | bytes 933896 | tf_op jit(solution)/shard_map/ppermute | solution.py:59
  96.4 6.4 %collective-permute-start.26 = (bf16[128,2432]{1,0:T(8,128)(2,1)S(1)}, bf16[128,2432]{1,0:T(8,128)(2,1)S(1)}, u32[]{:S(2)}, u32[]{:S(2)}) collective-permute-start(bf16[128,2432]{1,0:T(8,128)(2,1)S(1)} %pad_maximum_fusion.3), channel_id=1, source_target_pairs={{0,1},{1,0},{2,3},{3,2},{4,5},{5,4},{6,7},{7,6},{8,9},{9,8},{10,11... | collective-permute-start | bytes 1867784 | tf_op jit(solution)/shard_map/ppermute | solution.py:59
  98.7 5.7 %collective-permute-start.25 = (bf16[128,2432]{1,0:T(8,128)(2,1)S(1)}, bf16[128,2432]{1,0:T(8,128)(2,1)S(1)}, u32[]{:S(2)}, u32[]{:S(2)}) collective-permute-start(bf16[128,2432]{1,0:T(8,128)(2,1)S(1)} %get-tuple-element.56), channel_id=1, source_target_pairs={{0,1},{1,0},{2,3},{3,2},{4,5},{5,4},{6,7},{7,6},{8,9},{9,8},{10,11... | collective-permute-start | bytes 1867784 | tf_op jit(solution)/shard_map/ppermute | solution.py:59
  108.7 6.8 %collective-permute-start.38 = (bf16[64,2304]{1,0:T(8,128)(2,1)S(1)}, bf16[64,2304]{1,0:T(8,128)(2,1)S(1)}, u32[]{:S(2)}, u32[]{:S(2)}) collective-permute-start(bf16[64,2304]{1,0:T(8,128)(2,1)S(1)} %get-tuple-element.72), channel_id=1, source_target_pairs={{0,2},{1,5},{2,0},{3,7},{4,6},{5,1},{6,4},{7,3},{8,10},{9,13},{10,... | collective-permute-start | bytes 884744 | tf_op jit(solution)/shard_map/ppermute | solution.py:59
  110.3 9.7 %collective-permute-start.33 = (bf16[64,2432]{1,0:T(8,128)(2,1)S(1)}, bf16[64,2432]{1,0:T(8,128)(2,1)S(1)}, u32[]{:S(2)}, u32[]{:S(2)}) collective-permute-start(bf16[64,2432]{1,0:T(8,128)(2,1)S(1)} %get-tuple-element.66), channel_id=1, source_target_pairs={{0,2},{1,5},{2,0},{3,7},{4,6},{5,1},{6,4},{7,3},{8,10},{9,13},{10,... | collective-permute-start | bytes 933896 | tf_op jit(solution)/shard_map/ppermute | solution.py:59
  111.2 9.7 %collective-permute-start.28 = (bf16[64,2432]{1,0:T(8,128)(2,1)S(1)}, bf16[64,2432]{1,0:T(8,128)(2,1)S(1)}, u32[]{:S(2)}, u32[]{:S(2)}) collective-permute-start(bf16[64,2432]{1,0:T(8,128)(2,1)S(1)} %get-tuple-element.64), channel_id=1, source_target_pairs={{0,8},{1,9},{2,10},{3,11},{4,12},{5,13},{6,14},{7,15},{8,0},{9,1},... | collective-permute-start | bytes 933896 | tf_op jit(solution)/shard_map/ppermute | solution.py:59
  115.5 7.8 %collective-permute-start.39 = (bf16[32,2304]{1,0:T(8,128)(2,1)S(1)}, bf16[32,2304]{1,0:T(8,128)(2,1)S(1)}, u32[]{:S(2)}, u32[]{:S(2)}) collective-permute-start(bf16[32,2304]{1,0:T(8,128)(2,1)S(1)} %get-tuple-element.84), channel_id=1, source_target_pairs={{0,4},{1,3},{2,6},{3,1},{4,0},{5,7},{6,2},{7,5},{8,12},{9,11},{10,... | collective-permute-start | bytes 442376 | tf_op jit(solution)/shard_map/ppermute | solution.py:59
  120.1 5.4 %collective-permute-start.34 = (bf16[32,2432]{1,0:T(8,128)(2,1)S(1)}, bf16[32,2432]{1,0:T(8,128)(2,1)S(1)}, u32[]{:S(2)}, u32[]{:S(2)}) collective-permute-start(bf16[32,2432]{1,0:T(8,128)(2,1)S(1)} %get-tuple-element.78), channel_id=1, source_target_pairs={{0,4},{1,3},{2,6},{3,1},{4,0},{5,7},{6,2},{7,5},{8,12},{9,11},{10,... | collective-permute-start | bytes 466952 | tf_op jit(solution)/shard_map/ppermute | solution.py:59
  121.0 7.4 %collective-permute-start.29 = (bf16[32,2432]{1,0:T(8,128)(2,1)S(1)}, bf16[32,2432]{1,0:T(8,128)(2,1)S(1)}, u32[]{:S(2)}, u32[]{:S(2)}) collective-permute-start(bf16[32,2432]{1,0:T(8,128)(2,1)S(1)} %get-tuple-element.76), channel_id=1, source_target_pairs={{0,2},{1,5},{2,0},{3,7},{4,6},{5,1},{6,4},{7,3},{8,10},{9,13},{10,... | collective-permute-start | bytes 466952 | tf_op jit(solution)/shard_map/ppermute | solution.py:59
  125.6 7.8 %collective-permute-start.35 = (bf16[16,2432]{1,0:T(8,128)(2,1)S(1)}, bf16[16,2432]{1,0:T(8,128)(2,1)S(1)}, u32[]{:S(2)}, u32[]{:S(2)}) collective-permute-start(bf16[16,2432]{1,0:T(8,128)(2,1)S(1)} %get-tuple-element.90), channel_id=1, source_target_pairs={{0,8},{1,9},{2,10},{3,11},{4,12},{5,13},{6,14},{7,15},{8,0},{9,1},... | collective-permute-start | bytes 233480 | tf_op jit(solution)/shard_map/ppermute | solution.py:59
  127.8 5.5 %collective-permute-start.41 = (bf16[8,2304]{1,0:T(8,128)(2,1)S(1)}, bf16[8,2304]{1,0:T(8,128)(2,1)S(1)}, u32[]{:S(2)}, u32[]{:S(2)}) collective-permute-start(bf16[8,2304]{1,0:T(8,128)(2,1)S(1)} %add_convert_fusion.48), channel_id=1, source_target_pairs={{0,16},{1,17},{2,18},{3,19},{4,20},{5,21},{6,22},{7,23},{8,24},{9,... | collective-permute-start | bytes 110600 | tf_op jit(solution)/shard_map/ppermute | solution.py:59
  128.4 5.2 %collective-permute-start.30 = (bf16[16,2432]{1,0:T(8,128)(2,1)S(1)}, bf16[16,2432]{1,0:T(8,128)(2,1)S(1)}, u32[]{:S(2)}, u32[]{:S(2)}) collective-permute-start(bf16[16,2432]{1,0:T(8,128)(2,1)S(1)} %get-tuple-element.88), channel_id=1, source_target_pairs={{0,4},{1,3},{2,6},{3,1},{4,0},{5,7},{6,2},{7,5},{8,12},{9,11},{10,... | collective-permute-start | bytes 233480 | tf_op jit(solution)/shard_map/ppermute | solution.py:59
  133.4 4.9 %collective-permute-start.36 = (bf16[8,2432]{1,0:T(8,128)(2,1)S(1)}, bf16[8,2432]{1,0:T(8,128)(2,1)S(1)}, u32[]{:S(2)}, u32[]{:S(2)}) collective-permute-start(bf16[8,2432]{1,0:T(8,128)(2,1)S(1)} %add_convert_fusion.40), channel_id=1, source_target_pairs={{0,16},{1,17},{2,18},{3,19},{4,20},{5,21},{6,22},{7,23},{8,24},{9,... | collective-permute-start | bytes 116744 | tf_op jit(solution)/shard_map/ppermute | solution.py:59
  133.6 5.2 %collective-permute-start.31 = (bf16[8,2432]{1,0:T(8,128)(2,1)S(1)}, bf16[8,2432]{1,0:T(8,128)(2,1)S(1)}, u32[]{:S(2)}, u32[]{:S(2)}) collective-permute-start(bf16[8,2432]{1,0:T(8,128)(2,1)S(1)} %add_convert_fusion.42), channel_id=1, source_target_pairs={{0,16},{1,17},{2,18},{3,19},{4,20},{5,21},{6,22},{7,23},{8,24},{9,... | collective-permute-start | bytes 116744 | tf_op jit(solution)/shard_map/ppermute | solution.py:59
  (24 other events, 128.3 us)

commit v7 on v6

--- a/solution.py
+++ b/solution.py
@@ -293,7 +293,7 @@
         hidden.append((jax.nn.silu(gate_act) * up_act * share).astype(bf16))
     hidden = jnp.concatenate(hidden, axis=0)
     out = []
-    for i, ((start, size), base) in enumerate(zip(plans, residual, strict=True)):
+    for i, ((start, size), base) in list(enumerate(zip(plans, residual, strict=True)))[::-1]:
         acts = hidden
         if orders[i] != sorted(orders[i]):
             moved = place_rows(orders[i], rows)
@@ -304,7 +304,7 @@
         came = swap(partners, stages[-1], devices)
         total = base[:tokens_here, :size].astype(f32) + own + came.astype(f32)
         out.append(total.astype(bf16))
-    return jnp.concatenate(out, axis=1)
+    return jnp.concatenate(out[::-1], axis=1)
 
 
 def routed(

time: 140 us -> 140 us (level)
  no operation moved by 1% of the time
where the time goes in v7:
time: 140 us; the launch traced here: 139 us
  waiting for transfers between devices  55 us (39%)
  starting transfers between devices  47.1 us (34%)
  local copies, waits for them, and re-layouts  13 us (9%)
  Pallas kernels  11.2 us (8%)
  other arithmetic  8.12 us (6%)
  matrix products  4.43 us (3%)
    ppermute x42, waiting for transfers between devices, swap(): return lax.ppermute(x, 'expert', pairs)  42.6 us
    ppermute x42, starting transfers between devices, swap(): return lax.ppermute(x, 'expert', pairs)  39.7 us
    all_to_all x1, waiting for transfers between devices, shards(): lax.all_to_all(latent_out, 'expert', split_axis=0, concat_axis=0, tiled=T...  12.4 us
    slice x2, local copies, waits for them, and re-layouts, shards(): out_near = [out_after[:, start:start + size] for start, size in plans]  7.71 us
    all_to_all x1, starting transfers between devices, shards(): lax.all_to_all(latent_out, 'expert', split_axis=0, concat_axis=0, tiled=T...  7.43 us
    pallas_call x1, Pallas kernels, attend(): pl.pallas_call(attend_kernel, grid=(tokens // group,), out_shape=jax.Shap...  7.09 us
    pallas_call x6, Pallas kernels, project(): pl.pallas_call(functools.partial(project_kernel, start), out_shape=[half,...  4.14 us
    concatenate x1, other arithmetic, shards(): both_near = jnp.concatenate([gate_after[0], up_after[0]], axis=1)  3.69 us
  transfers between devices with their start and end apart: 43, of which 23 were waited for; matrix products, arithmetic and copies ran while one was open for 13% of the time, Pallas kernels for 2%

profile of v7, /device:TPU:0, one launch (start us, length us, event | category | flops | bytes accessed | tf_op | source)
XLA Modules:
  0.0 139.4 jit_solution(15197795698007442753)
XLA Ops:
  0.0 2.0 %reshape.121.rope_ref = bf16[8,128,64]{2,1,0:T(8,128)(2,1)} reshape(bf16[8,8192]{1,0:T(8,128)(2,1)} %param.16) | data formatting | bytes 262144 | tf_op jit(solution)/shard_map/reshape | solution.py:151
  2.0 7.1 %shard_map.136 = bf16[128,8,512]{2,1,0:T(8,128)(2,1)} custom-call(s32[8]{0:T(128)} %lengths_ref.1, bf16[8,128,512]{2,1,0:T(8,128)(2,1)} %latent_ref.1, bf16[8,128,64]{2,1,0:T(8,128)(2,1)} %reshape.121.rope_ref, bf16[8,256,512]{2,1,0:T(8,128)(2,1)} %keys_ref.1, bf16[8,64,256]{2,1,0:T(8,128)(2,1)} %turned_ref.1), custom_call_target="tpu_custom_call" | custom-call | flops 570425344 | bytes 4456448 | tf_op jit(solution)/shard_map/pallas_call | solution.py:132
  9.0 7.4 %all-to-all-start = ((bf16[128,8,512]{2,1,0:T(8,128)(2,1)}), bf16[128,8,512]{2,1,0:T(8,128)(2,1)}, u32[]{:S(2)}, u32[]{:S(2)}) async-start(bf16[128,8,512]{2,1,0:T(8,128)(2,1)} %shard_map.136), calls=%async_computation | async-start | bytes 2097152 | tf_op jit(solution)/shard_map/all_to_all | solution.py:221
  18.9 3.4 %slice.425.weight_ref = bf16[512,2304]{1,0:T(8,128)(2,1)} slice(bf16[512,7168]{1,0:T(8,128)(2,1)} %param.21), slice={[0:512], [4864:7168]} | slice | bytes 4718592 | tf_op jit(solution)/shard_map/slice | solution.py:219
  22.3 3.7 %pad_maximum_fusion = bf16[7168,256]{1,0:T(8,128)(2,1)} fusion(bf16[7168,128]{1,0:T(8,128)(2,1)S(1)} %bitcast.21, bf16[7168,128]{1,0:T(8,128)(2,1)} %bitcast.22), kind=kLoop, calls=%fused_computation | loop fusion | flops 7340032 | bytes 7340032 | tf_op jit(solution)/shard_map/concatenate | solution.py:218
  26.0 4.3 %fusion.65 = (bf16[512,2432]{1,0:T(8,128)(2,1)S(1)}, bf16[512,2432]{1,0:T(8,128)(2,1)}) fusion(bf16[512,7168]{1,0:T(8,128)(2,1)} %param.21), kind=kLoop, calls=%fused_computation.195 | loop fusion | bytes 9961472 | tf_op jit(solution)/shard_map/slice | solution.py:219
  30.3 12.4 %all-to-all-done = bf16[128,8,512]{2,1,0:T(8,128)(2,1)} async-done(((bf16[128,8,512]{2,1,0:T(8,128)(2,1)}), bf16[128,8,512]{2,1,0:T(8,128)(2,1)}, u32[]{:S(2)}, u32[]{:S(2)}) %all-to-all-start) | async-done | bytes 1048608 | tf_op jit(solution)/shard_map/all_to_all | solution.py:221
  42.7 1.8 %fusion.12 = bf16[32,8,4,128]{3,1,0,2:T(8,128)(2,1)S(1)} fusion(bf16[32,4,8,512]{3,2,1,0:T(8,128)(2,1)} %bitcast.5, bf16[4,512,128]{2,1,0:T(8,128)(2,1)S(1)} %copy-done), kind=kOutput, calls=%fused_computation.28 | convolution fusion | flops 134348800 | bytes 1835008 | tf_op jit(solution)/shard_map/sqtg,qge->stqe/dot_general | solution.py:227
  52.4 3.5 %collective-permute-done.17 = bf16[64,2304]{1,0:T(8,128)(2,1)S(1)} collective-permute-done((bf16[64,2304]{1,0:T(8,128)(2,1)S(1)}, bf16[64,2304]{1,0:T(8,128)(2,1)S(1)}, u32[]{:S(2)}, u32[]{:S(2)}) %collective-permute-start.17) | collective-permute-done | bytes 294944 | tf_op jit(solution)/shard_map/ppermute | solution.py:59
  57.5 2.4 %collective-permute-done.1 = bf16[64,2432]{1,0:T(8,128)(2,1)S(1)} collective-permute-done((bf16[64,2432]{1,0:T(8,128)(2,1)S(1)}, bf16[64,2432]{1,0:T(8,128)(2,1)S(1)}, u32[]{:S(2)}, u32[]{:S(2)}) %collective-permute-start.1) | collective-permute-done | bytes 311328 | tf_op jit(solution)/shard_map/ppermute | solution.py:59
  63.3 2.6 %collective-permute-done.2 = bf16[32,2432]{1,0:T(8,128)(2,1)S(1)} collective-permute-done((bf16[32,2432]{1,0:T(8,128)(2,1)S(1)}, bf16[32,2432]{1,0:T(8,128)(2,1)S(1)}, u32[]{:S(2)}, u32[]{:S(2)}) %collective-permute-start.2) | collective-permute-done | bytes 155680 | tf_op jit(solution)/shard_map/ppermute | solution.py:59
  65.9 1.9 %collective-permute-start.3 = (bf16[16,2432]{1,0:T(8,128)(2,1)S(1)}, bf16[16,2432]{1,0:T(8,128)(2,1)S(1)}, u32[]{:S(2)}, u32[]{:S(2)}) collective-permute-start(bf16[16,2432]{1,0:T(8,128)(2,1)S(1)} %get-tuple-element.92), channel_id=1, source_target_pairs={{0,4},{1,3},{2,6},{3,1},{4,0},{5,7},{6,2},{7,5},{8,12},{9,11},{10,... | collective-permute-start | bytes 233480 | tf_op jit(solution)/shard_map/ppermute | solution.py:59
  68.0 2.1 %collective-permute-start.20 = (bf16[16,2432]{1,0:T(8,128)(2,1)S(1)}, bf16[16,2432]{1,0:T(8,128)(2,1)S(1)}, u32[]{:S(2)}, u32[]{:S(2)}) collective-permute-start(bf16[16,2432]{1,0:T(8,128)(2,1)S(1)} %fusion.50), channel_id=1, source_target_pairs={{0,16},{1,17},{2,18},{3,19},{4,20},{5,21},{6,22},{7,23},{8,24},{9,... | collective-permute-start | bytes 233480 | tf_op jit(solution)/shard_map/ppermute | solution.py:59
  70.4 1.9 %collective-permute-done.11 = bf16[16,2432]{1,0:T(8,128)(2,1)S(1)} collective-permute-done((bf16[16,2432]{1,0:T(8,128)(2,1)S(1)}, bf16[16,2432]{1,0:T(8,128)(2,1)S(1)}, u32[]{:S(2)}, u32[]{:S(2)}) %collective-permute-start.11) | collective-permute-done | bytes 77856 | tf_op jit(solution)/shard_map/ppermute | solution.py:59
  72.4 1.8 %collective-permute-start.12 = (bf16[16,2432]{1,0:T(8,128)(2,1)S(1)}, bf16[16,2432]{1,0:T(8,128)(2,1)S(1)}, u32[]{:S(2)}, u32[]{:S(2)}) collective-permute-start(bf16[16,2432]{1,0:T(8,128)(2,1)S(1)} %pad_maximum_fusion.12), channel_id=1, source_target_pairs={{0,16},{1,17},{2,18},{3,19},{4,20},{5,21},{6,22},{7,23},{8,24},{9,... | collective-permute-start | bytes 233480 | tf_op jit(solution)/shard_map/ppermute | solution.py:59
  76.8 2.3 %collective-permute-done.12 = bf16[16,2432]{1,0:T(8,128)(2,1)S(1)} collective-permute-done((bf16[16,2432]{1,0:T(8,128)(2,1)S(1)}, bf16[16,2432]{1,0:T(8,128)(2,1)S(1)}, u32[]{:S(2)}, u32[]{:S(2)}) %collective-permute-start.12) | collective-permute-done | bytes 77856 | tf_op jit(solution)/shard_map/ppermute | solution.py:59
  80.0 2.8 %collective-permute-start.5 = (bf16[16,2432]{1,0:T(8,128)(2,1)S(1)}, bf16[16,2432]{1,0:T(8,128)(2,1)S(1)}, u32[]{:S(2)}, u32[]{:S(2)}) collective-permute-start(bf16[16,2432]{1,0:T(8,128)(2,1)S(1)} %add_convert_fusion.32), channel_id=1, source_target_pairs={{0,8},{1,9},{2,10},{3,11},{4,12},{5,13},{6,14},{7,15},{8,0},{9,1},... | collective-permute-start | bytes 233480 | tf_op jit(solution)/shard_map/ppermute | solution.py:59
  83.7 2.0 %collective-permute-start.14 = (bf16[32,2432]{1,0:T(8,128)(2,1)S(1)}, bf16[32,2432]{1,0:T(8,128)(2,1)S(1)}, u32[]{:S(2)}, u32[]{:S(2)}) collective-permute-start(bf16[32,2432]{1,0:T(8,128)(2,1)S(1)} %pad_maximum_fusion.8), channel_id=1, source_target_pairs={{0,4},{1,3},{2,6},{3,1},{4,0},{5,7},{6,2},{7,5},{8,12},{9,11},{10,... | collective-permute-start | bytes 466952 | tf_op jit(solution)/shard_map/ppermute | solution.py:59
  86.6 1.6 %collective-permute-done.22 = bf16[32,2432]{1,0:T(8,128)(2,1)S(1)} collective-permute-done((bf16[32,2432]{1,0:T(8,128)(2,1)S(1)}, bf16[32,2432]{1,0:T(8,128)(2,1)S(1)}, u32[]{:S(2)}, u32[]{:S(2)}) %collective-permute-start.22) | collective-permute-done | bytes 155680 | tf_op jit(solution)/shard_map/ppermute | solution.py:59
  89.3 2.1 %collective-permute-done.14 = bf16[32,2432]{1,0:T(8,128)(2,1)S(1)} collective-permute-done((bf16[32,2432]{1,0:T(8,128)(2,1)S(1)}, bf16[32,2432]{1,0:T(8,128)(2,1)S(1)}, u32[]{:S(2)}, u32[]{:S(2)}) %collective-permute-start.14) | collective-permute-done | bytes 155680 | tf_op jit(solution)/shard_map/ppermute | solution.py:59
  91.4 1.6 %collective-permute-start.15 = (bf16[64,2432]{1,0:T(8,128)(2,1)S(1)}, bf16[64,2432]{1,0:T(8,128)(2,1)S(1)}, u32[]{:S(2)}, u32[]{:S(2)}) collective-permute-start(bf16[64,2432]{1,0:T(8,128)(2,1)S(1)} %pad_maximum_fusion.5), channel_id=1, source_target_pairs={{0,2},{1,5},{2,0},{3,7},{4,6},{5,1},{6,4},{7,3},{8,10},{9,13},{10,... | collective-permute-start | bytes 933896 | tf_op jit(solution)/shard_map/ppermute | solution.py:59
  93.0 1.7 %collective-permute-done.6 = bf16[32,2432]{1,0:T(8,128)(2,1)S(1)} collective-permute-done((bf16[32,2432]{1,0:T(8,128)(2,1)S(1)}, bf16[32,2432]{1,0:T(8,128)(2,1)S(1)}, u32[]{:S(2)}, u32[]{:S(2)}) %collective-permute-start.6) | collective-permute-done | bytes 155680 | tf_op jit(solution)/shard_map/ppermute | solution.py:59
  94.7 1.6 %collective-permute-start.7 = (bf16[64,2432]{1,0:T(8,128)(2,1)S(1)}, bf16[64,2432]{1,0:T(8,128)(2,1)S(1)}, u32[]{:S(2)}, u32[]{:S(2)}) collective-permute-start(bf16[64,2432]{1,0:T(8,128)(2,1)S(1)} %pad_maximum_fusion.4), channel_id=1, source_target_pairs={{0,2},{1,5},{2,0},{3,7},{4,6},{5,1},{6,4},{7,3},{8,10},{9,13},{10,... | collective-permute-start | bytes 933896 | tf_op jit(solution)/shard_map/ppermute | solution.py:59
  98.7 3.1 %collective-permute-done.7 = bf16[64,2432]{1,0:T(8,128)(2,1)S(1)} collective-permute-done((bf16[64,2432]{1,0:T(8,128)(2,1)S(1)}, bf16[64,2432]{1,0:T(8,128)(2,1)S(1)}, u32[]{:S(2)}, u32[]{:S(2)}) %collective-permute-start.7) | collective-permute-done | bytes 311328 | tf_op jit(solution)/shard_map/ppermute | solution.py:59
  111.5 4.0 %collective-permute-done.38 = bf16[64,2304]{1,0:T(8,128)(2,1)S(1)} collective-permute-done((bf16[64,2304]{1,0:T(8,128)(2,1)S(1)}, bf16[64,2304]{1,0:T(8,128)(2,1)S(1)}, u32[]{:S(2)}, u32[]{:S(2)}) %collective-permute-start.38) | collective-permute-done | bytes 294944 | tf_op jit(solution)/shard_map/ppermute | solution.py:59
  116.7 3.3 %collective-permute-done.33 = bf16[64,2432]{1,0:T(8,128)(2,1)S(1)} collective-permute-done((bf16[64,2432]{1,0:T(8,128)(2,1)S(1)}, bf16[64,2432]{1,0:T(8,128)(2,1)S(1)}, u32[]{:S(2)}, u32[]{:S(2)}) %collective-permute-start.33) | collective-permute-done | bytes 311328 | tf_op jit(solution)/shard_map/ppermute | solution.py:59
  121.0 2.4 %collective-permute-start.29 = (bf16[32,2432]{1,0:T(8,128)(2,1)S(1)}, bf16[32,2432]{1,0:T(8,128)(2,1)S(1)}, u32[]{:S(2)}, u32[]{:S(2)}) collective-permute-start(bf16[32,2432]{1,0:T(8,128)(2,1)S(1)} %get-tuple-element.76), channel_id=1, source_target_pairs={{0,2},{1,5},{2,0},{3,7},{4,6},{5,1},{6,4},{7,3},{8,10},{9,13},{10,... | collective-permute-start | bytes 466952 | tf_op jit(solution)/shard_map/ppermute | solution.py:59
  123.5 2.0 %collective-permute-done.34 = bf16[32,2432]{1,0:T(8,128)(2,1)S(1)} collective-permute-done((bf16[32,2432]{1,0:T(8,128)(2,1)S(1)}, bf16[32,2432]{1,0:T(8,128)(2,1)S(1)}, u32[]{:S(2)}, u32[]{:S(2)}) %collective-permute-start.34) | collective-permute-done | bytes 155680 | tf_op jit(solution)/shard_map/ppermute | solution.py:59
  125.8 2.0 %collective-permute-done.40 = bf16[16,2304]{1,0:T(8,128)(2,1)S(1)} collective-permute-done((bf16[16,2304]{1,0:T(8,128)(2,1)S(1)}, bf16[16,2304]{1,0:T(8,128)(2,1)S(1)}, u32[]{:S(2)}, u32[]{:S(2)}) %collective-permute-start.40) | collective-permute-done | bytes 73760 | tf_op jit(solution)/shard_map/ppermute | solution.py:59
  129.7 3.6 %collective-permute-done.41 = bf16[8,2304]{1,0:T(8,128)(2,1)S(1)} collective-permute-done((bf16[8,2304]{1,0:T(8,128)(2,1)S(1)}, bf16[8,2304]{1,0:T(8,128)(2,1)S(1)}, u32[]{:S(2)}, u32[]{:S(2)}) %collective-permute-start.41) | collective-permute-done | bytes 36896 | tf_op jit(solution)/shard_map/ppermute | solution.py:59
  133.6 2.9 %collective-permute-start.31 = (bf16[8,2432]{1,0:T(8,128)(2,1)S(1)}, bf16[8,2432]{1,0:T(8,128)(2,1)S(1)}, u32[]{:S(2)}, u32[]{:S(2)}) collective-permute-start(bf16[8,2432]{1,0:T(8,128)(2,1)S(1)} %add_convert_fusion.42), channel_id=1, source_target_pairs={{0,16},{1,17},{2,18},{3,19},{4,20},{5,21},{6,22},{7,23},{8,24},{9,... | collective-permute-start | bytes 116744 | tf_op jit(solution)/shard_map/ppermute | solution.py:59
  136.5 1.9 %collective-permute-done.36 = bf16[8,2432]{1,0:T(8,128)(2,1)S(1)} collective-permute-done((bf16[8,2432]{1,0:T(8,128)(2,1)S(1)}, bf16[8,2432]{1,0:T(8,128)(2,1)S(1)}, u32[]{:S(2)}, u32[]{:S(2)}) %collective-permute-start.36) | collective-permute-done | bytes 38944 | tf_op jit(solution)/shard_map/ppermute | solution.py:59
  (183 shorter events, 39.7 us)
Async XLA Ops:
  9.0 33.6 %all-to-all-start = ((bf16[128,8,512]{2,1,0:T(8,128)(2,1)}), bf16[128,8,512]{2,1,0:T(8,128)(2,1)}, u32[]{:S(2)}, u32[]{:S(2)}) async-start(bf16[128,8,512]{2,1,0:T(8,128)(2,1)} %shard_map.136), calls=%async_computation | async-start | bytes 2097152 | tf_op jit(solution)/shard_map/all_to_all | solution.py:221
  49.1 6.8 %collective-permute-start.17 = (bf16[64,2304]{1,0:T(8,128)(2,1)S(1)}, bf16[64,2304]{1,0:T(8,128)(2,1)S(1)}, u32[]{:S(2)}, u32[]{:S(2)}) collective-permute-start(bf16[64,2304]{1,0:T(8,128)(2,1)S(1)} %get-tuple-element.74), channel_id=1, source_target_pairs={{0,2},{1,5},{2,0},{3,7},{4,6},{5,1},{6,4},{7,3},{8,10},{9,13},{10,... | collective-permute-start | bytes 884744 | tf_op jit(solution)/shard_map/ppermute | solution.py:59
  50.8 9.2 %collective-permute-start.1 = (bf16[64,2432]{1,0:T(8,128)(2,1)S(1)}, bf16[64,2432]{1,0:T(8,128)(2,1)S(1)}, u32[]{:S(2)}, u32[]{:S(2)}) collective-permute-start(bf16[64,2432]{1,0:T(8,128)(2,1)S(1)} %get-tuple-element.68), channel_id=1, source_target_pairs={{0,8},{1,9},{2,10},{3,11},{4,12},{5,13},{6,14},{7,15},{8,0},{9,1},... | collective-permute-start | bytes 933896 | tf_op jit(solution)/shard_map/ppermute | solution.py:59
  51.6 10.0 %collective-permute-start.9 = (bf16[64,2432]{1,0:T(8,128)(2,1)S(1)}, bf16[64,2432]{1,0:T(8,128)(2,1)S(1)}, u32[]{:S(2)}, u32[]{:S(2)}) collective-permute-start(bf16[64,2432]{1,0:T(8,128)(2,1)S(1)} %get-tuple-element.70), channel_id=1, source_target_pairs={{0,2},{1,5},{2,0},{3,7},{4,6},{5,1},{6,4},{7,3},{8,10},{9,13},{10,... | collective-permute-start | bytes 933896 | tf_op jit(solution)/shard_map/ppermute | solution.py:59
  56.0 6.4 %collective-permute-start.18 = (bf16[32,2304]{1,0:T(8,128)(2,1)S(1)}, bf16[32,2304]{1,0:T(8,128)(2,1)S(1)}, u32[]{:S(2)}, u32[]{:S(2)}) collective-permute-start(bf16[32,2304]{1,0:T(8,128)(2,1)S(1)} %get-tuple-element.86), channel_id=1, source_target_pairs={{0,4},{1,3},{2,6},{3,1},{4,0},{5,7},{6,2},{7,5},{8,12},{9,11},{10,... | collective-permute-start | bytes 442376 | tf_op jit(solution)/shard_map/ppermute | solution.py:59
  60.1 5.8 %collective-permute-start.2 = (bf16[32,2432]{1,0:T(8,128)(2,1)S(1)}, bf16[32,2432]{1,0:T(8,128)(2,1)S(1)}, u32[]{:S(2)}, u32[]{:S(2)}) collective-permute-start(bf16[32,2432]{1,0:T(8,128)(2,1)S(1)} %get-tuple-element.80), channel_id=1, source_target_pairs={{0,2},{1,5},{2,0},{3,7},{4,6},{5,1},{6,4},{7,3},{8,10},{9,13},{10,... | collective-permute-start | bytes 466952 | tf_op jit(solution)/shard_map/ppermute | solution.py:59
  61.7 6.1 %collective-permute-start.10 = (bf16[32,2432]{1,0:T(8,128)(2,1)S(1)}, bf16[32,2432]{1,0:T(8,128)(2,1)S(1)}, u32[]{:S(2)}, u32[]{:S(2)}) collective-permute-start(bf16[32,2432]{1,0:T(8,128)(2,1)S(1)} %get-tuple-element.82), channel_id=1, source_target_pairs={{0,4},{1,3},{2,6},{3,1},{4,0},{5,7},{6,2},{7,5},{8,12},{9,11},{10,... | collective-permute-start | bytes 466952 | tf_op jit(solution)/shard_map/ppermute | solution.py:59
  62.5 5.5 %collective-permute-start.19 = (bf16[16,2304]{1,0:T(8,128)(2,1)S(1)}, bf16[16,2304]{1,0:T(8,128)(2,1)S(1)}, u32[]{:S(2)}, u32[]{:S(2)}) collective-permute-start(bf16[16,2304]{1,0:T(8,128)(2,1)S(1)} %get-tuple-element.98), channel_id=1, source_target_pairs={{0,8},{1,9},{2,10},{3,11},{4,12},{5,13},{6,14},{7,15},{8,0},{9,1},... | collective-permute-start | bytes 221192 | tf_op jit(solution)/shard_map/ppermute | solution.py:59
  68.0 8.6 %collective-permute-start.20 = (bf16[16,2432]{1,0:T(8,128)(2,1)S(1)}, bf16[16,2432]{1,0:T(8,128)(2,1)S(1)}, u32[]{:S(2)}, u32[]{:S(2)}) collective-permute-start(bf16[16,2432]{1,0:T(8,128)(2,1)S(1)} %fusion.50), channel_id=1, source_target_pairs={{0,16},{1,17},{2,18},{3,19},{4,20},{5,21},{6,22},{7,23},{8,24},{9,... | collective-permute-start | bytes 233480 | tf_op jit(solution)/shard_map/ppermute | solution.py:59
  72.4 6.7 %collective-permute-start.12 = (bf16[16,2432]{1,0:T(8,128)(2,1)S(1)}, bf16[16,2432]{1,0:T(8,128)(2,1)S(1)}, u32[]{:S(2)}, u32[]{:S(2)}) collective-permute-start(bf16[16,2432]{1,0:T(8,128)(2,1)S(1)} %pad_maximum_fusion.12), channel_id=1, source_target_pairs={{0,16},{1,17},{2,18},{3,19},{4,20},{5,21},{6,22},{7,23},{8,24},{9,... | collective-permute-start | bytes 233480 | tf_op jit(solution)/shard_map/ppermute | solution.py:59
  74.2 5.8 %collective-permute-start.4 = (bf16[16,2432]{1,0:T(8,128)(2,1)S(1)}, bf16[16,2432]{1,0:T(8,128)(2,1)S(1)}, u32[]{:S(2)}, u32[]{:S(2)}) collective-permute-start(bf16[16,2432]{1,0:T(8,128)(2,1)S(1)} %pad_maximum_fusion.11), channel_id=1, source_target_pairs={{0,16},{1,17},{2,18},{3,19},{4,20},{5,21},{6,22},{7,23},{8,24},{9,... | collective-permute-start | bytes 233480 | tf_op jit(solution)/shard_map/ppermute | solution.py:59
  76.6 6.2 %collective-permute-start.21 = (bf16[16,2432]{1,0:T(8,128)(2,1)S(1)}, bf16[16,2432]{1,0:T(8,128)(2,1)S(1)}, u32[]{:S(2)}, u32[]{:S(2)}) collective-permute-start(bf16[16,2432]{1,0:T(8,128)(2,1)S(1)} %add_convert_fusion.28), channel_id=1, source_target_pairs={{0,8},{1,9},{2,10},{3,11},{4,12},{5,13},{6,14},{7,15},{8,0},{9,1},... | collective-permute-start | bytes 233480 | tf_op jit(solution)/shard_map/ppermute | solution.py:59
  80.0 5.7 %collective-permute-start.5 = (bf16[16,2432]{1,0:T(8,128)(2,1)S(1)}, bf16[16,2432]{1,0:T(8,128)(2,1)S(1)}, u32[]{:S(2)}, u32[]{:S(2)}) collective-permute-start(bf16[16,2432]{1,0:T(8,128)(2,1)S(1)} %add_convert_fusion.32), channel_id=1, source_target_pairs={{0,8},{1,9},{2,10},{3,11},{4,12},{5,13},{6,14},{7,15},{8,0},{9,1},... | collective-permute-start | bytes 233480 | tf_op jit(solution)/shard_map/ppermute | solution.py:59
  82.8 5.3 %collective-permute-start.22 = (bf16[32,2432]{1,0:T(8,128)(2,1)S(1)}, bf16[32,2432]{1,0:T(8,128)(2,1)S(1)}, u32[]{:S(2)}, u32[]{:S(2)}) collective-permute-start(bf16[32,2432]{1,0:T(8,128)(2,1)S(1)} %pad_maximum_fusion.9), channel_id=1, source_target_pairs={{0,4},{1,3},{2,6},{3,1},{4,0},{5,7},{6,2},{7,5},{8,12},{9,11},{10,... | collective-permute-start | bytes 466952 | tf_op jit(solution)/shard_map/ppermute | solution.py:59
  83.7 7.7 %collective-permute-start.14 = (bf16[32,2432]{1,0:T(8,128)(2,1)S(1)}, bf16[32,2432]{1,0:T(8,128)(2,1)S(1)}, u32[]{:S(2)}, u32[]{:S(2)}) collective-permute-start(bf16[32,2432]{1,0:T(8,128)(2,1)S(1)} %pad_maximum_fusion.8), channel_id=1, source_target_pairs={{0,4},{1,3},{2,6},{3,1},{4,0},{5,7},{6,2},{7,5},{8,12},{9,11},{10,... | collective-permute-start | bytes 466952 | tf_op jit(solution)/shard_map/ppermute | solution.py:59
  85.7 9.0 %collective-permute-start.6 = (bf16[32,2432]{1,0:T(8,128)(2,1)S(1)}, bf16[32,2432]{1,0:T(8,128)(2,1)S(1)}, u32[]{:S(2)}, u32[]{:S(2)}) collective-permute-start(bf16[32,2432]{1,0:T(8,128)(2,1)S(1)} %pad_maximum_fusion.7), channel_id=1, source_target_pairs={{0,4},{1,3},{2,6},{3,1},{4,0},{5,7},{6,2},{7,5},{8,12},{9,11},{10,... | collective-permute-start | bytes 466952 | tf_op jit(solution)/shard_map/ppermute | solution.py:59
  88.2 8.2 %collective-permute-start.23 = (bf16[64,2432]{1,0:T(8,128)(2,1)S(1)}, bf16[64,2432]{1,0:T(8,128)(2,1)S(1)}, u32[]{:S(2)}, u32[]{:S(2)}) collective-permute-start(bf16[64,2432]{1,0:T(8,128)(2,1)S(1)} %pad_maximum_fusion.6), channel_id=1, source_target_pairs={{0,2},{1,5},{2,0},{3,7},{4,6},{5,1},{6,4},{7,3},{8,10},{9,13},{10,... | collective-permute-start | bytes 933896 | tf_op jit(solution)/shard_map/ppermute | solution.py:59
  91.4 7.1 %collective-permute-start.15 = (bf16[64,2432]{1,0:T(8,128)(2,1)S(1)}, bf16[64,2432]{1,0:T(8,128)(2,1)S(1)}, u32[]{:S(2)}, u32[]{:S(2)}) collective-permute-start(bf16[64,2432]{1,0:T(8,128)(2,1)S(1)} %pad_maximum_fusion.5), channel_id=1, source_target_pairs={{0,2},{1,5},{2,0},{3,7},{4,6},{5,1},{6,4},{7,3},{8,10},{9,13},{10,... | collective-permute-start | bytes 933896 | tf_op jit(solution)/shard_map/ppermute | solution.py:59
  94.7 7.1 %collective-permute-start.7 = (bf16[64,2432]{1,0:T(8,128)(2,1)S(1)}, bf16[64,2432]{1,0:T(8,128)(2,1)S(1)}, u32[]{:S(2)}, u32[]{:S(2)}) collective-permute-start(bf16[64,2432]{1,0:T(8,128)(2,1)S(1)} %pad_maximum_fusion.4), channel_id=1, source_target_pairs={{0,2},{1,5},{2,0},{3,7},{4,6},{5,1},{6,4},{7,3},{8,10},{9,13},{10,... | collective-permute-start | bytes 933896 | tf_op jit(solution)/shard_map/ppermute | solution.py:59
  96.4 6.4 %collective-permute-start.26 = (bf16[128,2432]{1,0:T(8,128)(2,1)S(1)}, bf16[128,2432]{1,0:T(8,128)(2,1)S(1)}, u32[]{:S(2)}, u32[]{:S(2)}) collective-permute-start(bf16[128,2432]{1,0:T(8,128)(2,1)S(1)} %pad_maximum_fusion.3), channel_id=1, source_target_pairs={{0,1},{1,0},{2,3},{3,2},{4,5},{5,4},{6,7},{7,6},{8,9},{9,8},{10,11... | collective-permute-start | bytes 1867784 | tf_op jit(solution)/shard_map/ppermute | solution.py:59
  98.7 5.7 %collective-permute-start.25 = (bf16[128,2432]{1,0:T(8,128)(2,1)S(1)}, bf16[128,2432]{1,0:T(8,128)(2,1)S(1)}, u32[]{:S(2)}, u32[]{:S(2)}) collective-permute-start(bf16[128,2432]{1,0:T(8,128)(2,1)S(1)} %get-tuple-element.56), channel_id=1, source_target_pairs={{0,1},{1,0},{2,3},{3,2},{4,5},{5,4},{6,7},{7,6},{8,9},{9,8},{10,11... | collective-permute-start | bytes 1867784 | tf_op jit(solution)/shard_map/ppermute | solution.py:59
  108.7 6.8 %collective-permute-start.38 = (bf16[64,2304]{1,0:T(8,128)(2,1)S(1)}, bf16[64,2304]{1,0:T(8,128)(2,1)S(1)}, u32[]{:S(2)}, u32[]{:S(2)}) collective-permute-start(bf16[64,2304]{1,0:T(8,128)(2,1)S(1)} %get-tuple-element.72), channel_id=1, source_target_pairs={{0,2},{1,5},{2,0},{3,7},{4,6},{5,1},{6,4},{7,3},{8,10},{9,13},{10,... | collective-permute-start | bytes 884744 | tf_op jit(solution)/shard_map/ppermute | solution.py:59
  110.3 9.7 %collective-permute-start.33 = (bf16[64,2432]{1,0:T(8,128)(2,1)S(1)}, bf16[64,2432]{1,0:T(8,128)(2,1)S(1)}, u32[]{:S(2)}, u32[]{:S(2)}) collective-permute-start(bf16[64,2432]{1,0:T(8,128)(2,1)S(1)} %get-tuple-element.66), channel_id=1, source_target_pairs={{0,2},{1,5},{2,0},{3,7},{4,6},{5,1},{6,4},{7,3},{8,10},{9,13},{10,... | collective-permute-start | bytes 933896 | tf_op jit(solution)/shard_map/ppermute | solution.py:59
  111.2 9.7 %collective-permute-start.28 = (bf16[64,2432]{1,0:T(8,128)(2,1)S(1)}, bf16[64,2432]{1,0:T(8,128)(2,1)S(1)}, u32[]{:S(2)}, u32[]{:S(2)}) collective-permute-start(bf16[64,2432]{1,0:T(8,128)(2,1)S(1)} %get-tuple-element.64), channel_id=1, source_target_pairs={{0,8},{1,9},{2,10},{3,11},{4,12},{5,13},{6,14},{7,15},{8,0},{9,1},... | collective-permute-start | bytes 933896 | tf_op jit(solution)/shard_map/ppermute | solution.py:59
  115.5 7.8 %collective-permute-start.39 = (bf16[32,2304]{1,0:T(8,128)(2,1)S(1)}, bf16[32,2304]{1,0:T(8,128)(2,1)S(1)}, u32[]{:S(2)}, u32[]{:S(2)}) collective-permute-start(bf16[32,2304]{1,0:T(8,128)(2,1)S(1)} %get-tuple-element.84), channel_id=1, source_target_pairs={{0,4},{1,3},{2,6},{3,1},{4,0},{5,7},{6,2},{7,5},{8,12},{9,11},{10,... | collective-permute-start | bytes 442376 | tf_op jit(solution)/shard_map/ppermute | solution.py:59
  120.1 5.4 %collective-permute-start.34 = (bf16[32,2432]{1,0:T(8,128)(2,1)S(1)}, bf16[32,2432]{1,0:T(8,128)(2,1)S(1)}, u32[]{:S(2)}, u32[]{:S(2)}) collective-permute-start(bf16[32,2432]{1,0:T(8,128)(2,1)S(1)} %get-tuple-element.78), channel_id=1, source_target_pairs={{0,4},{1,3},{2,6},{3,1},{4,0},{5,7},{6,2},{7,5},{8,12},{9,11},{10,... | collective-permute-start | bytes 466952 | tf_op jit(solution)/shard_map/ppermute | solution.py:59
  121.0 7.4 %collective-permute-start.29 = (bf16[32,2432]{1,0:T(8,128)(2,1)S(1)}, bf16[32,2432]{1,0:T(8,128)(2,1)S(1)}, u32[]{:S(2)}, u32[]{:S(2)}) collective-permute-start(bf16[32,2432]{1,0:T(8,128)(2,1)S(1)} %get-tuple-element.76), channel_id=1, source_target_pairs={{0,2},{1,5},{2,0},{3,7},{4,6},{5,1},{6,4},{7,3},{8,10},{9,13},{10,... | collective-permute-start | bytes 466952 | tf_op jit(solution)/shard_map/ppermute | solution.py:59
  125.6 7.8 %collective-permute-start.35 = (bf16[16,2432]{1,0:T(8,128)(2,1)S(1)}, bf16[16,2432]{1,0:T(8,128)(2,1)S(1)}, u32[]{:S(2)}, u32[]{:S(2)}) collective-permute-start(bf16[16,2432]{1,0:T(8,128)(2,1)S(1)} %get-tuple-element.90), channel_id=1, source_target_pairs={{0,8},{1,9},{2,10},{3,11},{4,12},{5,13},{6,14},{7,15},{8,0},{9,1},... | collective-permute-start | bytes 233480 | tf_op jit(solution)/shard_map/ppermute | solution.py:59
  127.8 5.5 %collective-permute-start.41 = (bf16[8,2304]{1,0:T(8,128)(2,1)S(1)}, bf16[8,2304]{1,0:T(8,128)(2,1)S(1)}, u32[]{:S(2)}, u32[]{:S(2)}) collective-permute-start(bf16[8,2304]{1,0:T(8,128)(2,1)S(1)} %add_convert_fusion.48), channel_id=1, source_target_pairs={{0,16},{1,17},{2,18},{3,19},{4,20},{5,21},{6,22},{7,23},{8,24},{9,... | collective-permute-start | bytes 110600 | tf_op jit(solution)/shard_map/ppermute | solution.py:59
  128.4 5.2 %collective-permute-start.30 = (bf16[16,2432]{1,0:T(8,128)(2,1)S(1)}, bf16[16,2432]{1,0:T(8,128)(2,1)S(1)}, u32[]{:S(2)}, u32[]{:S(2)}) collective-permute-start(bf16[16,2432]{1,0:T(8,128)(2,1)S(1)} %get-tuple-element.88), channel_id=1, source_target_pairs={{0,4},{1,3},{2,6},{3,1},{4,0},{5,7},{6,2},{7,5},{8,12},{9,11},{10,... | collective-permute-start | bytes 233480 | tf_op jit(solution)/shard_map/ppermute | solution.py:59
  133.4 4.9 %collective-permute-start.36 = (bf16[8,2432]{1,0:T(8,128)(2,1)S(1)}, bf16[8,2432]{1,0:T(8,128)(2,1)S(1)}, u32[]{:S(2)}, u32[]{:S(2)}) collective-permute-start(bf16[8,2432]{1,0:T(8,128)(2,1)S(1)} %add_convert_fusion.40), channel_id=1, source_target_pairs={{0,16},{1,17},{2,18},{3,19},{4,20},{5,21},{6,22},{7,23},{8,24},{9,... | collective-permute-start | bytes 116744 | tf_op jit(solution)/shard_map/ppermute | solution.py:59
  133.6 5.2 %collective-permute-start.31 = (bf16[8,2432]{1,0:T(8,128)(2,1)S(1)}, bf16[8,2432]{1,0:T(8,128)(2,1)S(1)}, u32[]{:S(2)}, u32[]{:S(2)}) collective-permute-start(bf16[8,2432]{1,0:T(8,128)(2,1)S(1)} %add_convert_fusion.42), channel_id=1, source_target_pairs={{0,16},{1,17},{2,18},{3,19},{4,20},{5,21},{6,22},{7,23},{8,24},{9,... | collective-permute-start | bytes 116744 | tf_op jit(solution)/shard_map/ppermute | solution.py:59
  (24 other events, 128.3 us)
